TPU v7x, 512 devices: a whole 4x4x16 slice. The times are simulated.
512 devices in a mesh: dp: 16 (over x_lo, y, core), expert: 32 (over x_hi, z).
Axes of the slice: x: 4 (x_hi: 2, x_lo: 2; x = x_hi * 2 + x_lo), y: 4, z: 16, core: 2. Of those that a mesh axis runs over, the one named last changes fastest.
Arguments:
- grad_out: bfloat16 [1024, 7168], P('expert', 'dp'), may hold values from -6 to 6
- routes: int32 [1024, 8], P('expert'), may hold values from 0 to 31, all different within a row; in each aligned block of 32 rows (0 to 31, 32 to 63, ...) at most 12 rows name the same one
- gates: float32 [1024, 8], P('expert'), may hold values from 0.05 to 1
- hidden: bfloat16 [32, 384, 2048], P('expert', None, 'dp'), may hold values from -0.1796875 to 0.1796875
- w_down: bfloat16 [32, 2048, 7168], P('expert', 'dp'), may hold values from -0.125 to 0.125
Outputs:
- d_hidden: bfloat16 [32, 384, 2048], P('expert', None, 'dp')
- d_down: bfloat16 [32, 2048, 7168], P('expert', 'dp')
- d_gate: float32 [1024, 8], P('expert')
Inputs may be any that keep to these rules, and one draw needn't show every extreme that they name: `routes`: each row names 8 different experts; within each aligned block of 32 rows (the tokens on one index of the expert axis) no expert is named by more than 12 rows.
All inputs are finite; a program needn't handle non-finite values.
Results may differ from a plain program's by a relative error of at most 0.0049.
Values may be sent and summed in bfloat16 or wider, within the bound.
No kernel may reach another device: no remote copies, remote signals or barrier semaphores. Data moves between devices by JAX's collectives and lax.ppermute only.
A program may use at most 128 MiB of HBM per device.

v0:
```python
import jax
import jax.numpy as jnp
from jax import lax
from jax.sharding import PartitionSpec as P


def route_tables(routes, gates, experts, capacity):
    tokens_here = routes.shape[0]
    expert_ids = lax.broadcasted_iota(jnp.int32, (1, 1, experts), 2)
    chosen = (routes[:, :, None] == expert_ids).astype(jnp.int32)
    present = jnp.sum(chosen, axis=1)
    before = jnp.cumsum(present, axis=0) - present
    route_rank = jnp.sum(chosen * before[:, None, :], axis=2)
    slot_ids = lax.broadcasted_iota(jnp.int32, (1, 1, 1, capacity), 3)
    placed = chosen[:, :, :, None] * (route_rank[:, :, None, None] == slot_ids).astype(jnp.int32)
    tok_index = lax.broadcasted_iota(jnp.int32, (tokens_here, 1, 1, 1), 0)
    slot_token = jnp.sum(placed * tok_index, axis=(0, 1))
    slot_gate = jnp.sum(placed.astype(jnp.float32) * gates[:, :, None, None], axis=(0, 1))
    counts = jnp.sum(present, axis=0)
    return (placed, slot_token, slot_gate, counts)


def on_device(grad_out, routes, gates, hidden, w_down):
    experts = lax.axis_size("expert")
    capacity = hidden.shape[1] // experts
    placed, slot_token, slot_gate, counts = route_tables(routes, gates, experts, capacity)
    picked = grad_out[slot_token]
    scaled = (slot_gate[:, :, None] * picked.astype(jnp.float32)).astype(jnp.bfloat16)
    arrived = lax.all_to_all(scaled, "expert", split_axis=0, concat_axis=0, tiled=True)
    arrived = lax.all_gather(arrived, "dp", axis=2, tiled=True)
    dispatched = arrived.reshape(-1, arrived.shape[2])
    activations = hidden[0]
    weight = w_down[0]
    values = lax.dot_general(
        dispatched, weight, (((1,), (1,)), ((), ())), preferred_element_type=jnp.float32
    )
    gate_terms = jnp.sum(activations.astype(jnp.float32) * values, axis=1)
    gradient = lax.dot_general(
        activations, dispatched, (((0,), (0,)), ((), ())), preferred_element_type=jnp.float32
    )
    d_hidden = values.astype(jnp.bfloat16)[None]
    d_down = gradient.astype(jnp.bfloat16)[None]
    summed = lax.psum(gate_terms, "dp")
    returned = lax.all_to_all(
        summed.reshape(experts, capacity), "expert", split_axis=0, concat_axis=0, tiled=True
    )
    matched = jnp.sum(placed.astype(jnp.float32) * returned[None, None, :, :], axis=(2, 3))
    d_gate = matched / gates
    return (d_hidden, d_down, d_gate)


def solution(mesh):
    in_specs = (
        P("expert", "dp"),
        P("expert", None),
        P("expert", None),
        P("expert", None, "dp"),
        P("expert", "dp", None),
    )
    out_specs = (P("expert", None, "dp"), P("expert", "dp", None), P("expert", None))
    return jax.shard_map(
        on_device, mesh=mesh, in_specs=in_specs, out_specs=out_specs, check_vma=False
    )
```

profile of v0, /device:TPU:1, one launch (start us, length us, event | category | flops | bytes accessed | tf_op | source)
XLA Modules:
  0.0 353.5 jit_solution(11881050243654104437)
XLA Ops:
  7.2 0.9 copy.26
  8.1 0.1 fusion.11
  8.4 0.7 select_reduce_fusion
  9.1 0.8 copy.27
  9.9 0.6 fusion.7
  10.5 0.6 fusion.5
  11.1 0.7 copy.28
  12.0 2.1 gather_fusion
  14.2 0.9 multiply_convert_fusion.1
  15.0 50.5 %all_to_all.14 = bf16[32,12,448]{2,1,0:T(8,128)(2,1)S(1)} all-to-all(bf16[32,12,448]{2,1,0:T(8,128)(2,1)S(1)} %multiply_convert_fusion.1), channel_id=1, replica_groups=mesh['dp'=16,'expert'=32] {'expert'}, dimensions={0} | all-to-all | bytes 688128 | tf_op jit(solution)/shard_map/all_to_all | solution.py:29
  65.5 2.2 copy.30
  67.7 0.1 copy.32
  67.8 151.6 %all-gather.2.cloned.1.call-done = bf16[32,12,7168]{0,1,2:T(8,128)(2,1)} async-done(((bf16[32,12,448]{0,1,2:T(8,128)(2,1)}), bf16[32,12,7168]{0,1,2:T(8,128)(2,1)}) %all-gather.2.cloned.1.call-update) | async-done | bytes 5505040 | tf_op jit(solution)/shard_map/all_gather | solution.py:30
  219.4 33.5 %copy.31 = bf16[32,12,7168]{2,1,0:T(8,128)(2,1)} copy(bf16[32,12,7168]{0,1,2:T(8,128)(2,1)} %all-gather.2.cloned.1.call-done) | data formatting | bytes 11010048 | tf_op jit(solution)/shard_map/all_gather | solution.py:30
  252.9 8.2 %reshape.54 = bf16[384,7168]{1,0:T(8,128)(2,1)} reshape(bf16[32,12,7168]{2,1,0:T(8,128)(2,1)} %copy.31) | data formatting | bytes 11010048 | tf_op jit(solution)/shard_map/reshape | solution.py:31
  261.1 4.3 %multiply_reduce_fusion = (f32[384]{0:T(512)S(1)}, bf16[1,384,128]{1,2,0:T(8,128)(2,1)S(1)}) fusion(bf16[1,384,128]{1,2,0:T(8,128)(2,1)S(1)} %copy.32, bf16[384,7168]{1,0:T(8,128)(2,1)} %reshape.54, bf16[1,128,7168]{2,1,0:T(8,128)(2,1)S(1)} %copy-done), kind=kOutput, calls=%fused_computation.15 | convolution fusion | flops 704839296 | bytes 7538176 | tf_op jit(solution)/shard_map/dot_general | solution.py:34
  265.5 51.4 %psum.7 = f32[32,1,12]{2,0,1:T(8,128)} all-reduce(f32[32,1,12]{2,0,1:T(8,128)S(1)} %all_to_all.10), channel_id=1, replica_groups=mesh['dp'=16,'expert'=32] {'dp'}, use_global_device_ids=true, to_apply=%region_6.7 | all-reduce | flops 384 | bytes 3072 | tf_op jit(solution)/shard_map/psum | solution.py:43
  317.0 14.4 %all-to-all-start.1 = ((f32[32,1,12]{2,1,0:T(1,128)}), f32[32,1,12]{2,1,0:T(1,128)S(1)}, u32[]{:S(2)}, u32[]{:S(2)}) async-start(f32[32,1,12]{2,1,0:T(1,128)} %bitcast.6), calls=%async_computation.1 | async-start | bytes 32768 | tf_op jit(solution)/shard_map/all_to_all | solution.py:44
  331.4 5.5 %fusion = bf16[1,128,7168]{1,2,0:T(8,128)(2,1)} fusion(bf16[384,7168]{1,0:T(8,128)(2,1)} %reshape.54, bf16[1,384,128]{2,1,0:T(8,128)(2,1)S(1)} %copy-done.4), kind=kOutput, calls=%fused_computation.2 | convolution fusion | flops 705560576 | bytes 7438336 | tf_op jit(solution)/shard_map/dot_general | solution.py:38
  336.9 0.8 copy.36
  337.6 3.9 %copy.37 = bf16[1,128,7168]{2,1,0:T(8,128)(2,1)} copy(bf16[1,128,7168]{1,2,0:T(8,128)(2,1)} %fusion) | data formatting | bytes 3670016
  341.5 3.5 all-to-all-done.1
  345.1 0.9 fusion.6
  346.0 0.7 copy.38
  (24 shorter events, 0.7 us)
Async XLA Ops:
  7.2 254.0 %copy-start = (bf16[1,128,7168]{2,1,0:T(8,128)(2,1)S(1)}, bf16[1,128,7168]{2,1,0:T(8,128)(2,1)}, u32[]{:S(2)}) copy-start(bf16[1,128,7168]{2,1,0:T(8,128)(2,1)} %param.9) | copy-start | bytes 5505028
  7.2 4.8 %copy-start.1 = (bf16[32,448]{1,0:T(8,128)(2,1)S(1)}, bf16[32,448]{1,0:T(8,128)(2,1)}, u32[]{:S(2)}) copy-start(bf16[32,448]{1,0:T(8,128)(2,1)} %param.5) | copy-start | bytes 86020
  7.2 212.2 %all-gather.2.cloned.1.call-start = ((), (), s32[]{:S(2)}) async-start(), calls=%async_computation.2 | async-start | bytes 31195136 | tf_op jit(solution)/shard_map/all_gather | solution.py:30
  8.3 3.7 %copy-start.2 = (s32[32,8,32]{2,1,0:T(8,128)}, s32[32,8,32]{2,1,0:T(8,128)S(1)}, u32[]{:S(2)}) copy-start(s32[32,8,32]{2,1,0:T(8,128)S(1)} %fusion.9) | copy-start | bytes 98308
  65.5 2.2 copy-start.4
  317.0 28.1 %all-to-all-start.1 = ((f32[32,1,12]{2,1,0:T(1,128)}), f32[32,1,12]{2,1,0:T(1,128)S(1)}, u32[]{:S(2)}, u32[]{:S(2)}) async-start(f32[32,1,12]{2,1,0:T(1,128)} %bitcast.6), calls=%async_computation.1 | async-start | bytes 32768 | tf_op jit(solution)/shard_map/all_to_all | solution.py:44
  337.6 7.5 %copy-start.3 = (s32[32,8,32]{2,1,0:T(8,128)S(1)}, s32[32,8,32]{2,1,0:T(8,128)}, u32[]{:S(2)}) copy-start(s32[32,8,32]{2,1,0:T(8,128)} %copy-done.2) | copy-start | bytes 98308
Sparse Core Ops, SparseCore 0:
  67.8 151.5 all-gather.1
where the time goes:
time: 359 us; the launch traced here: 354 us
  waiting for transfers between devices  155 us (43%)
  blocking collectives  102 us (28%)
  local copies, waits for them, and re-layouts  54.2 us (15%)
  starting transfers between devices  14.5 us (4%)
  between operations  14.2 us (4%)
  matrix products  9.79 us (3%)
  other arithmetic  3.91 us (1%)
    all_gather x1, waiting for transfers between devices, on_device(): arrived = lax.all_gather(arrived, 'dp', axis=2, tiled=True)  152 us
    psum x1, blocking collectives, on_device(): summed = lax.psum(gate_terms, 'dp')  51.4 us
    all_to_all x1, blocking collectives, on_device(): lax.all_to_all(scaled, 'expert', split_axis=0, concat_axis=0, tiled=True)  50.5 us
    all_gather x1, local copies, waits for them, and re-layouts, on_device(): arrived = lax.all_gather(arrived, 'dp', axis=2, tiled=True)  33.5 us
    all_to_all x1, starting transfers between devices, on_device(): lax.all_to_all(summed.reshape(experts, capacity), 'expert', split_axis=0,...  14.4 us
    reshape x1, local copies, waits for them, and re-layouts, on_device(): dispatched = arrived.reshape(-1, arrived.shape[2])  8.24 us
  transfers between devices with their start and end apart: 2, of which 2 were waited for; matrix products, arithmetic and copies ran while one was open for 3% of the time, Pallas kernels for 0%

commit v1 on v0

v1 whole, which is shorter than its diff:
```python
import functools

import jax
import jax.numpy as jnp
from jax import lax
from jax.experimental import pallas as pl
from jax.experimental.pallas import tpu as pltpu
from jax.sharding import PartitionSpec as P

F32 = jnp.float32
BF16 = jnp.bfloat16


def ranks(routes, experts):
    tokens, top = routes.shape
    ids = lax.broadcasted_iota(jnp.int32, (tokens, experts), 1)
    named = [routes[:, k : k + 1] == ids for k in range(top)]
    present = functools.reduce(jnp.logical_or, named)
    rows = lax.broadcasted_iota(jnp.int32, (tokens, tokens), 0)
    columns = lax.broadcasted_iota(jnp.int32, (tokens, tokens), 1)
    earlier = (columns < rows).astype(F32)
    before = jnp.dot(earlier, present.astype(F32), preferred_element_type=F32)
    return named, present, before


def pack_kernel(grad_ref, routes_ref, gates_ref, out_ref):
    experts, capacity, _ = out_ref.shape
    named, present, before = ranks(routes_ref[...], experts)
    gates = gates_ref[...]
    gate = jnp.zeros(present.shape, F32)
    for k, here in enumerate(named):
        gate = jnp.where(here, gates[:, k : k + 1], gate)
    grad = grad_ref[...]
    for c in range(capacity):
        placed = jnp.logical_and(present, before == c).astype(F32)
        chosen = placed.T.astype(BF16)
        row_gate = jnp.sum(placed * gate, axis=0, keepdims=True)
        rows = jnp.dot(chosen, grad, preferred_element_type=F32)
        out_ref[:, c, :] = (row_gate.T * rows).astype(BF16)


def values_kernel(steps, disp_ref, weight_ref, hidden_ref, dhid_ref, gate_ref, total):
    step = pl.program_id(0)

    @pl.when(step == 0)
    def _():
        total[...] = jnp.zeros_like(total)

    total[...] += jnp.dot(weight_ref[...], disp_ref[...], preferred_element_type=F32)

    @pl.when(step == steps - 1)
    def _():
        values = total[...].T
        dhid_ref[...] = values.astype(BF16)
        terms = jnp.sum(hidden_ref[...].astype(F32) * values, axis=1, keepdims=True)
        sources, capacity = gate_ref.shape
        slots = values.shape[0]
        slot = lax.broadcasted_iota(jnp.int32, (slots, capacity), 0)
        rank = lax.broadcasted_iota(jnp.int32, (slots, capacity), 1)
        spread = jnp.where(slot % capacity == rank, terms, 0.0)
        owner = lax.broadcasted_iota(jnp.int32, (sources, slots), 0)
        member = lax.broadcasted_iota(jnp.int32, (sources, slots), 1)
        fold = (member // capacity == owner).astype(F32)
        gate_ref[...] = jnp.dot(
            fold, spread, preferred_element_type=F32, precision=lax.Precision.HIGHEST
        )


def down_kernel(disp_ref, hidden_ref, out_ref, flipped):
    @pl.when(pl.program_id(0) == 0)
    def _():
        flipped[...] = hidden_ref[...].astype(F32).T.astype(BF16)

    out_ref[...] = lax.dot_general(
        flipped[...],
        disp_ref[...],
        (((1,), (1,)), ((), ())),
        preferred_element_type=F32,
    ).astype(BF16)


def gate_kernel(parts_ref, routes_ref, gates_ref, out_ref):
    _, experts, capacity = parts_ref.shape
    named, present, before = ranks(routes_ref[...], experts)
    terms = jnp.sum(parts_ref[...], axis=0).T
    matched = jnp.zeros(present.shape, F32)
    for c in range(capacity):
        here = jnp.logical_and(present, before == c)
        matched = jnp.where(here, terms[c : c + 1, :], matched)
    rows = [
        jnp.sum(jnp.where(here, matched, 0.0), axis=1, keepdims=True) for here in named
    ]
    column = lax.broadcasted_iota(jnp.int32, out_ref.shape, 1)
    total = jnp.zeros(out_ref.shape, F32)
    for k, row in enumerate(rows):
        total = jnp.where(column == k, row, total)
    out_ref[...] = total / gates_ref[...]


def whole():
    return pl.BlockSpec(memory_space=pltpu.VMEM)


def on_device(grad_out, routes, gates, hidden, w_down):
    experts, parts = lax.axis_size("expert"), lax.axis_size("dp")
    _, slots, units = hidden.shape
    width = w_down.shape[2]
    capacity = slots // experts
    share = grad_out.shape[1]

    scaled = pl.pallas_call(
        pack_kernel,
        out_shape=jax.ShapeDtypeStruct((experts, capacity, share), BF16),
        in_specs=[whole()] * 3,
        out_specs=whole(),
        name="pack",
    )(grad_out, routes, gates)
    arrived = lax.all_to_all(scaled, "expert", split_axis=0, concat_axis=0, tiled=True)
    flipped = arrived.reshape(slots, share).T
    dispatched = lax.all_gather(flipped, "dp", axis=0, tiled=True)

    depth = 1024
    steps = width // depth
    activations, weight = hidden[0], w_down[0]
    d_hidden, terms = pl.pallas_call(
        functools.partial(values_kernel, steps),
        grid=(steps,),
        out_shape=(
            jax.ShapeDtypeStruct((slots, units), BF16),
            jax.ShapeDtypeStruct((experts, capacity), F32),
        ),
        in_specs=[
            pl.BlockSpec((depth, slots), lambda i: (i, 0)),
            pl.BlockSpec((units, depth), lambda i: (0, i)),
            pl.BlockSpec((slots, units), lambda i: (0, 0)),
        ],
        out_specs=(
            pl.BlockSpec((slots, units), lambda i: (0, 0)),
            pl.BlockSpec((experts, capacity), lambda i: (0, 0)),
        ),
        scratch_shapes=[pltpu.VMEM((units, slots), F32)],
        cost_estimate=pl.CostEstimate(
            flops=2 * slots * units * width, bytes_accessed=7500000, transcendentals=0
        ),
        name="values",
    )(dispatched, weight, activations)
    d_down = pl.pallas_call(
        down_kernel,
        grid=(steps,),
        out_shape=jax.ShapeDtypeStruct((units, width), BF16),
        in_specs=[
            pl.BlockSpec((depth, slots), lambda i: (i, 0)),
            pl.BlockSpec((slots, units), lambda i: (0, 0)),
        ],
        out_specs=pl.BlockSpec((units, depth), lambda i: (0, i)),
        scratch_shapes=[pltpu.VMEM((units, slots), BF16)],
        cost_estimate=pl.CostEstimate(
            flops=2 * slots * units * width, bytes_accessed=7500000, transcendentals=0
        ),
        name="down",
    )(dispatched, activations)

    returned = lax.all_to_all(terms, "expert", split_axis=0, concat_axis=0, tiled=True)
    copies = jnp.broadcast_to(returned[None], (parts, experts, capacity))
    everyone = lax.all_to_all(copies, "dp", split_axis=0, concat_axis=0, tiled=True)
    d_gate = pl.pallas_call(
        gate_kernel,
        out_shape=jax.ShapeDtypeStruct(gates.shape, F32),
        in_specs=[whole()] * 3,
        out_specs=whole(),
        name="match",
    )(everyone, routes, gates)
    return (d_hidden[None], d_down[None], d_gate)


def solution(mesh):
    in_specs = (
        P("expert", "dp"),
        P("expert", None),
        P("expert", None),
        P("expert", None, "dp"),
        P("expert", "dp", None),
    )
    out_specs = (P("expert", None, "dp"), P("expert", "dp", None), P("expert", None))
    return jax.shard_map(
        on_device, mesh=mesh, in_specs=in_specs, out_specs=out_specs, check_vma=False
    )
```

time: 359 us -> 167 us (0.47); the launches traced: 354 us -> 166 us
  waiting for transfers between devices: 155 us -> 40.9 us
  local copies, waits for them, and re-layouts: 54.2 us -> 7.45 us
  blocking collectives: 102 us -> 78.7 us
  Pallas kernels: 0 us -> 18.9 us
  matrix products: 9.79 us -> 0 us
  starting transfers between devices: 14.5 us -> 5.14 us
    all_gather x1, waiting for transfers between devices: 152 us -> 40.9 us  [on_device(): dispatched = lax.all_gather(flipped, 'dp', axis=0, tiled=True)]
    psum x1 -> x0, blocking collectives: 51.4 us -> none  [on_device(): summed = lax.psum(gate_terms, 'dp')]
    all_gather x1 -> x0, local copies, waits for them, and re-layouts: 33.5 us -> none  [on_device(): arrived = lax.all_gather(arrived, 'dp', axis=2, tiled=True)]
    all_to_all x0 -> x1, blocking collectives: none -> 28 us  [on_device(): lax.all_to_all(terms, 'expert', split_axis=0, concat_axis=0, tiled=True)]
    pallas_call x0 -> x4, Pallas kernels: none -> 18.9 us  [the longest x1 7.33 us: on_device(): pl.pallas_call(down_kernel, grid=(steps,), out_shape=jax.ShapeDtypeStruct...]
    dot_general x2 -> x0, matrix products: 9.79 us -> none  [the longest x1 5.48 us: on_device(): lax.dot_general(activations, dispatched, (((0,), (0,)), ((), ())), prefer...]
    all_to_all x1, starting transfers between devices: 14.4 us -> 5.1 us  [on_device(): lax.all_to_all(copies, 'dp', split_axis=0, concat_axis=0, tiled=True)]
    reshape x1 -> x2, local copies, waits for them, and re-layouts: 8.24 us -> 1.1 us  [on_device(): flipped = arrived.reshape(slots, share).T]
  transfers between devices with their start and end apart: 2 -> 2, of which waited for: 2 -> 1; matrix products, arithmetic and copies ran while one was open for 3% -> 0% of each run, Pallas kernels for 0% -> 4%
where the time goes in v1:
time: 167 us; the launch traced here: 166 us
  blocking collectives  78.7 us (47%)
  waiting for transfers between devices  40.9 us (24%)
  Pallas kernels  18.9 us (11%)
  between operations  14.1 us (8%)
  local copies, waits for them, and re-layouts  7.45 us (4%)
  starting transfers between devices  5.14 us (3%)
    all_to_all x1, blocking collectives, on_device(): lax.all_to_all(scaled, 'expert', split_axis=0, concat_axis=0, tiled=True)  50.7 us
    all_gather x1, waiting for transfers between devices, on_device(): dispatched = lax.all_gather(flipped, 'dp', axis=0, tiled=True)  40.9 us
    all_to_all x1, blocking collectives, on_device(): lax.all_to_all(terms, 'expert', split_axis=0, concat_axis=0, tiled=True)  28 us
    pallas_call x1, Pallas kernels, on_device(): pl.pallas_call(down_kernel, grid=(steps,), out_shape=jax.ShapeDtypeStruct...  7.33 us
    pallas_call x1, Pallas kernels, on_device(): pl.pallas_call(functools.partial(values_kernel, steps), grid=(steps,), ou...  7.16 us
    all_to_all x1, starting transfers between devices, on_device(): lax.all_to_all(copies, 'dp', split_axis=0, concat_axis=0, tiled=True)  5.1 us
    unnamed x6, local copies, waits for them, and re-layouts  4.9 us
  transfers between devices with their start and end apart: 2, of which 1 were waited for; matrix products, arithmetic and copies ran while one was open for 0% of the time, Pallas kernels for 4%

profile of v1, /device:TPU:1, one launch (start us, length us, event | category | flops | bytes accessed | tf_op | source)
XLA Modules:
  0.0 165.8 jit_solution(4909062360436293563)
XLA Ops:
  7.2 0.0 all-gather.2.cloned.1.call-start
  7.2 1.4 copy.20.routes_ref
  8.6 1.4 copy.21.gates_ref
  9.9 2.5 %pack.1 = bf16[32,12,448]{2,1,0:T(8,128)(2,1)} custom-call(bf16[32,448]{1,0:T(8,128)(2,1)} %grad_ref.1, s32[32,8]{1,0:T(8,128)} %copy.20.routes_ref, f32[32,8]{1,0:T(8,128)} %copy.21.gates_ref), custom_call_target="tpu_custom_call" | custom-call | tf_op jit(solution)/shard_map/pack/pallas_call | solution.py:111
  12.4 50.7 %all_to_all.19 = bf16[32,12,448]{2,1,0:T(8,128)(2,1)S(1)} all-to-all(bf16[32,12,448]{2,1,0:T(8,128)(2,1)} %pack.1), channel_id=1, replica_groups=mesh['dp'=16,'expert'=32] {'expert'}, dimensions={0} | all-to-all | bytes 688128 | tf_op jit(solution)/shard_map/all_to_all | solution.py:118
  63.0 0.2 reshape.13
  63.2 0.9 copy.22
  64.1 0.0 all-gather.2.cloned.1.call-update
  64.2 40.9 %all-gather.2.cloned.1.call-done.disp_ref = bf16[7168,384]{1,0:T(8,128)(2,1)} async-done(((bf16[448,384]{1,0:T(8,128)(2,1)}), bf16[7168,384]{1,0:T(8,128)(2,1)}) %all-gather.2.cloned.1.call-update) | async-done | bytes 5505040 | tf_op jit(solution)/shard_map/all_gather | solution.py:120
  105.1 7.2 %values.1 = (bf16[384,128]{1,0:T(8,128)(2,1)}, f32[32,12]{1,0:T(8,128)}) custom-call(bf16[7168,384]{1,0:T(8,128)(2,1)} %all-gather.2.cloned.1.call-done.disp_ref, bf16[128,7168]{1,0:T(8,128)(2,1)} %bitcast.12, bf16[384,128]{1,0:T(8,128)(2,1)} %bitcast.16), custom_call_target="tpu_custom_call" | custom-call | flops 704643072 | bytes 7500000 | tf_op jit(solution)/shard_map/values/pallas_call | solution.py:125
  112.2 28.0 %all_to_all.20 = f32[32,1,12]{2,1,0:T(1,128)S(1)} all-to-all(f32[32,1,12]{2,1,0:T(1,128)} %bitcast.19), channel_id=1, replica_groups=mesh['dp'=16,'expert'=32] {'expert'}, dimensions={0} | all-to-all | bytes 3072 | tf_op jit(solution)/shard_map/all_to_all | solution.py:163
  140.2 0.1 copy.24
  140.3 0.7 reshape.14
  141.0 5.1 %all-to-all-start.2 = ((f32[16,1,384]{2,1,0:T(1,128)}), f32[16,1,384]{2,1,0:T(1,128)S(1)}, u32[]{:S(2)}, u32[]{:S(2)}) async-start(f32[16,1,384]{2,1,0:T(1,128)} %reshape.14), calls=%async_computation.2 | async-start | bytes 49152 | tf_op jit(solution)/shard_map/all_to_all | solution.py:165
  146.1 7.3 %down.1 = bf16[128,7168]{1,0:T(8,128)(2,1)} custom-call(bf16[7168,384]{1,0:T(8,128)(2,1)} %all-gather.2.cloned.1.call-done.disp_ref, bf16[384,128]{1,0:T(8,128)(2,1)} %bitcast.17), custom_call_target="tpu_custom_call" | custom-call | flops 704643072 | bytes 7500000 | tf_op jit(solution)/shard_map/down/pallas_call | solution.py:147
  153.5 0.0 all-to-all-done.2
  153.5 0.5 broadcast
  154.0 0.7 reduce
  154.7 0.1 reshape.15
  154.8 0.9 copy.25.parts_ref
  155.7 1.9 %match.1 = f32[32,8]{1,0:T(8,128)} custom-call(f32[16,32,12]{2,1,0:T(8,128)} %copy.25.parts_ref, s32[32,8]{1,0:T(8,128)} %copy.20.routes_ref, f32[32,8]{1,0:T(8,128)} %copy.21.gates_ref), custom_call_target="tpu_custom_call" | custom-call | tf_op jit(solution)/shard_map/match/pallas_call | solution.py:166
  157.6 1.4 copy.28
  (1 shorter events, 0.0 us)
Async XLA Ops:
  7.2 97.9 %all-gather.2.cloned.1.call-start = ((), (), s32[]{:S(2)}) async-start(), calls=%async_computation.3 | async-start | bytes 5849088 | tf_op jit(solution)/shard_map/all_gather | solution.py:120
  141.0 12.4 %all-to-all-start.2 = ((f32[16,1,384]{2,1,0:T(1,128)}), f32[16,1,384]{2,1,0:T(1,128)S(1)}, u32[]{:S(2)}, u32[]{:S(2)}) async-start(f32[16,1,384]{2,1,0:T(1,128)} %reshape.14), calls=%async_computation.2 | async-start | bytes 49152 | tf_op jit(solution)/shard_map/all_to_all | solution.py:165
Sparse Core Ops, SparseCore 0:
  64.3 40.7 all-gather.1

commit v2 on v1

v2 whole, which is shorter than its diff:
```python
import functools

import jax
import jax.numpy as jnp
from jax import lax
from jax.experimental import pallas as pl
from jax.experimental.pallas import tpu as pltpu
from jax.sharding import Mesh, PartitionSpec as P

F32 = jnp.float32
BF16 = jnp.bfloat16
LANES = 128


def ranks(routes, experts):
    top, tokens = routes.shape
    ids = lax.broadcasted_iota(jnp.int32, (experts, tokens), 0)
    named = [routes[k : k + 1, :] == ids for k in range(top)]
    present = functools.reduce(jnp.logical_or, named)
    rows = lax.broadcasted_iota(jnp.int32, (tokens, tokens), 0)
    columns = lax.broadcasted_iota(jnp.int32, (tokens, tokens), 1)
    earlier = (rows < columns).astype(F32)
    before = jnp.dot(present.astype(F32), earlier, preferred_element_type=F32)
    return named, present, before


def pack_kernel(grad_ref, routes_ref, gates_ref, out_ref):
    experts, rows, _ = out_ref.shape
    share = grad_ref.shape[1]
    pair = 2 * share // LANES
    named, present, before = ranks(routes_ref[...], experts)
    gates = gates_ref[...]
    gate = jnp.zeros(present.shape, F32)
    for k, here in enumerate(named):
        gate = jnp.where(here, gates[k : k + 1, :], gate)
    grad = grad_ref[...]

    def slot(c):
        placed = jnp.logical_and(present, before == c).astype(F32)
        row_gate = jnp.sum(placed * gate, axis=1, keepdims=True)
        return row_gate * jnp.dot(
            placed.astype(BF16), grad, preferred_element_type=F32
        )

    for p in range(rows // pair):
        both = jnp.concatenate([slot(2 * p), slot(2 * p + 1)], axis=1).astype(BF16)
        for i in range(pair):
            out_ref[:, pair * p + i, :] = both[:, LANES * i : LANES * (i + 1)]


def unpack_kernel(in_ref, out_ref):
    sources, rows, _ = in_ref.shape
    share, slots = out_ref.shape
    pair = 2 * share // LANES
    group = LANES // sources
    for g in range(slots // LANES):
        parts = []
        for p in range(g * group // 2, (g + 1) * group // 2):
            both = jnp.concatenate(
                [in_ref[:, pair * p + i, :].astype(F32) for i in range(pair)], axis=1
            )
            parts += [both[:, :share], both[:, share:]]
        block = jnp.concatenate(parts, axis=0)
        out_ref[:, LANES * g : LANES * (g + 1)] = block.T.astype(BF16)


def reorder(slots, sources, rank_slowest_rows):
    capacity = slots // sources
    rows = lax.broadcasted_iota(jnp.int32, (slots, slots), 0)
    columns = lax.broadcasted_iota(jnp.int32, (slots, slots), 1)
    if rank_slowest_rows:
        rows, columns = columns, rows
    matches = (rows % capacity) * sources + rows // capacity == columns
    return matches.astype(F32).astype(BF16)


def split_kernel(sources, core_ref, weight_ref, hidden_ref, keep_ref, send_ref):
    blocks = keep_ref.shape[0] - 1
    share = weight_ref.shape[1] // (2 * blocks)
    slots = hidden_ref.shape[0]
    order = reorder(slots, sources, False)
    flipped = lax.dot_general(
        hidden_ref[...], order, (((0,), (0,)), ((), ())), preferred_element_type=F32
    ).astype(BF16)
    for ref in (keep_ref, send_ref):
        ref[:, :, ref.shape[2] - LANES :] = jnp.zeros((*ref.shape[:2], LANES), BF16)
        ref[blocks, :, :slots] = flipped

    def store(first, second):
        for j in range(blocks):
            both = weight_ref[:, 2 * share * j : 2 * share * (j + 1)]
            first[j, :, :share] = both[:, :share]
            second[j, :, :share] = both[:, share:]

    pl.when(core_ref[0] == 0)(lambda: store(keep_ref, send_ref))
    pl.when(core_ref[0] != 0)(lambda: store(send_ref, keep_ref))


def values_kernel(
    steps,
    disp_ref,
    keep_ref,
    other_ref,
    keep_hidden_ref,
    other_hidden_ref,
    mine_ref,
    theirs_ref,
    gate_ref,
    total,
):
    step = pl.program_id(0)

    @pl.when(step == 0)
    def _():
        total[...] = jnp.zeros_like(total)

    weight = jnp.concatenate([keep_ref[0], other_ref[0]], axis=0)
    share = disp_ref.shape[1]
    total[...] += jnp.dot(weight[:, :share], disp_ref[0], preferred_element_type=F32)

    @pl.when(step == steps - 1)
    def _():
        values = total[...]
        units = values.shape[0] // 2
        slots = values.shape[1]
        mine_ref[...] = values[:units]
        theirs_ref[...] = values[units:]
        hidden = jnp.concatenate([keep_hidden_ref[0], other_hidden_ref[0]], axis=0)
        terms = jnp.sum(
            hidden[:, :slots].astype(F32) * values, axis=0, keepdims=True
        )
        sources, capacity = gate_ref.shape
        owner = lax.broadcasted_iota(jnp.int32, (sources, slots), 0)
        member = lax.broadcasted_iota(jnp.int32, (sources, slots), 1)
        spread = jnp.where(member % sources == owner, terms, 0.0)
        slot = lax.broadcasted_iota(jnp.int32, (slots, capacity), 0)
        rank = lax.broadcasted_iota(jnp.int32, (slots, capacity), 1)
        fold = (slot // sources == rank).astype(F32)
        gate_ref[...] = jnp.dot(
            spread, fold, preferred_element_type=F32, precision=lax.Precision.HIGHEST
        )


def down_kernel(disp_ref, keep_hidden_ref, other_hidden_ref, mine_ref, theirs_ref):
    slots = disp_ref.shape[2]
    hidden = jnp.concatenate([keep_hidden_ref[0], other_hidden_ref[0]], axis=0)
    product = lax.dot_general(
        hidden[:, :slots],
        disp_ref[0],
        (((1,), (1,)), ((), ())),
        preferred_element_type=F32,
    ).astype(BF16)
    units, share = mine_ref.shape[1], product.shape[1]
    for ref, rows in ((mine_ref, product[:units]), (theirs_ref, product[units:])):
        ref[0, :, ref.shape[2] - LANES :] = jnp.zeros((units, LANES), BF16)
        ref[0, :, :share] = rows


def finish_kernel(
    sources, core_ref, mine_ref, got_ref, values_ref, got_values_ref, down_ref, dhid_ref
):
    share = down_ref.shape[1] // 2

    def store(first, second):
        down_ref[:, :share] = first[0, :, :share]
        down_ref[:, share:] = second[0, :, :share]

    pl.when(core_ref[0] == 0)(lambda: store(mine_ref, got_ref))
    pl.when(core_ref[0] != 0)(lambda: store(got_ref, mine_ref))

    @pl.when(pl.program_id(0) == 0)
    def _():
        values = (values_ref[...] + got_values_ref[...]).T.astype(BF16)
        order = reorder(values.shape[0], sources, False)
        dhid_ref[...] = jnp.dot(order, values, preferred_element_type=F32).astype(BF16)


def gate_kernel(capacity, parts_ref, routes_ref, gates_ref, out_ref):
    top, tokens = out_ref.shape
    experts = parts_ref.shape[1] * LANES // capacity
    named, present, before = ranks(routes_ref[...], experts)
    terms = jnp.sum(parts_ref[...], axis=0)
    group = LANES // experts
    matched = jnp.zeros(present.shape, F32)
    for c in range(capacity):
        start = (c % group) * experts
        row = terms[c // group : c // group + 1, start : start + experts]
        spread = jnp.broadcast_to(row, (8, experts)).T[:, :1]
        here = jnp.logical_and(present, before == c)
        matched = jnp.where(here, spread, matched)
    total = [jnp.sum(jnp.where(n, matched, 0.0), axis=0, keepdims=True) for n in named]
    out_ref[...] = jnp.concatenate(total, axis=0) / gates_ref[...]


def whole():
    return pl.BlockSpec(memory_space=pltpu.VMEM)


def scalar():
    return pl.BlockSpec(memory_space=pltpu.SMEM)


def limit(mib):
    return pltpu.CompilerParams(vmem_limit_bytes=mib * 2**20)


def cost(flops, moved):
    return pl.CostEstimate(flops=flops, bytes_accessed=moved, transcendentals=0)


def swap_all(x, axis):
    return lax.all_to_all(x, axis, split_axis=0, concat_axis=0, tiled=True)


def on_device(grad_out, routes, gates, hidden, w_down):
    experts, chips = lax.axis_size("expert"), lax.axis_size("chip")
    _, slots, units = hidden.shape
    width = w_down.shape[2]
    capacity = slots // experts
    share = grad_out.shape[1]
    rows = capacity * share // LANES
    core = lax.axis_index("core").astype(jnp.int32).reshape(1)
    routes, gates = routes.T, gates.T

    def to_other_core(x):
        return lax.ppermute(x, "core", [(0, 1), (1, 0)])

    packed = pl.pallas_call(
        pack_kernel,
        out_shape=jax.ShapeDtypeStruct((experts, rows, LANES), BF16),
        in_specs=[whole()] * 3,
        out_specs=whole(),
        compiler_params=limit(8),
        name="pack",
    )(grad_out, routes, gates)
    arrived = swap_all(packed, "expert")

    padded = -(-share // LANES) * LANES
    half = jax.ShapeDtypeStruct((chips + 1, units, padded), BF16)
    keep, send = pl.pallas_call(
        functools.partial(split_kernel, experts),
        out_shape=(half, half),
        in_specs=[scalar(), whole(), whole()],
        out_specs=(whole(), whole()),
        cost_estimate=cost(2 * units * slots * slots, 2 * 2 * units * width),
        compiler_params=limit(16),
        name="split",
    )(core, w_down[0], hidden[0])
    other = to_other_core(send)

    own = pl.pallas_call(
        unpack_kernel,
        out_shape=jax.ShapeDtypeStruct((share, slots), BF16),
        in_specs=[whole()],
        out_specs=whole(),
        compiler_params=limit(8),
        name="unpack",
    )(arrived)
    dispatched = swap_all(jnp.broadcast_to(own[None], (chips, share, slots)), "chip")

    block = pl.BlockSpec((1, share, slots), lambda i: (i, 0, 0))
    columns = pl.BlockSpec((1, units, padded), lambda i: (i, 0, 0))
    last = pl.BlockSpec((1, units, padded), lambda i: (chips, 0, 0))
    table = pl.BlockSpec((units, slots), lambda i: (0, 0))
    flops = 2 * slots * units * width
    mine, theirs, terms = pl.pallas_call(
        functools.partial(values_kernel, chips),
        grid=(chips,),
        out_shape=(
            jax.ShapeDtypeStruct((units, slots), F32),
            jax.ShapeDtypeStruct((units, slots), F32),
            jax.ShapeDtypeStruct((experts, capacity), F32),
        ),
        in_specs=[block, columns, columns, last, last],
        out_specs=(table, table, pl.BlockSpec((experts, capacity), lambda i: (0, 0))),
        scratch_shapes=[pltpu.VMEM((2 * units, slots), F32)],
        cost_estimate=cost(flops, slots * width + 2 * units * width),
        compiler_params=limit(12),
        name="values",
    )(dispatched, keep, other, keep, other)
    returned = swap_all(terms, "expert")

    part = jax.ShapeDtypeStruct((chips, units, padded), BF16)
    down, down_theirs = pl.pallas_call(
        down_kernel,
        grid=(chips,),
        out_shape=(part, part),
        in_specs=[block, last, last],
        out_specs=(columns, columns),
        cost_estimate=cost(flops, slots * width + 2 * units * width),
        compiler_params=limit(12),
        name="down",
    )(dispatched, keep, other)
    returned, theirs, down_theirs = lax.optimization_barrier(
        (returned, theirs, down_theirs)
    )
    got_down = to_other_core(down_theirs)
    got = to_other_core(theirs)
    d_down, d_hidden = pl.pallas_call(
        functools.partial(finish_kernel, experts),
        grid=(chips,),
        out_shape=(
            jax.ShapeDtypeStruct((units, width), BF16),
            jax.ShapeDtypeStruct((slots, units), BF16),
        ),
        in_specs=[scalar(), columns, columns, table, table],
        out_specs=(
            pl.BlockSpec((units, 2 * share), lambda i: (0, i)),
            pl.BlockSpec((slots, units), lambda i: (0, 0)),
        ),
        cost_estimate=cost(2 * units * slots * slots, 4 * units * width),
        compiler_params=limit(12),
        name="finish",
    )(core, down, got_down, mine, got)

    flat = returned.T.reshape(1, slots // LANES, LANES)
    copies = jnp.broadcast_to(flat, (2 * chips, *flat.shape[1:]))
    everyone = swap_all(copies, ("chip", "core"))
    everyone, _ = lax.optimization_barrier((everyone, d_hidden))
    d_gate = pl.pallas_call(
        functools.partial(gate_kernel, capacity),
        out_shape=jax.ShapeDtypeStruct(gates.shape, F32),
        in_specs=[whole()] * 3,
        out_specs=whole(),
        compiler_params=limit(4),
        name="match",
    )(everyone, routes, gates)
    return (d_hidden[None], d_down[None], d_gate.T)


def solution(mesh):
    parts, experts = mesh.devices.shape
    devices = mesh.devices.reshape(parts // 2, 2, experts)
    finer = Mesh(devices, ("chip", "core", "expert"))
    dp = ("chip", "core")
    in_specs = (
        P("expert", dp),
        P("expert", None),
        P("expert", None),
        P("expert", None, dp),
        P("expert", dp, None),
    )
    out_specs = (P("expert", None, dp), P("expert", dp, None), P("expert", None))
    return jax.shard_map(
        on_device, mesh=finer, in_specs=in_specs, out_specs=out_specs, check_vma=False
    )
```

time: 167 us -> 133 us (0.80)
  blocking collectives: 78.7 us -> 44.8 us
  starting transfers between devices: 5.14 us -> 25.9 us
  between operations: 14.1 us -> 0.76 us
  waiting for transfers between devices: 40.9 us -> 30.8 us
  local copies, waits for them, and re-layouts: 7.45 us -> 16.5 us
  Pallas kernels: 18.9 us -> 13.4 us
    all_gather x1 -> x0, waiting for transfers between devices: 40.9 us -> none  [on_device(): dispatched = lax.all_gather(flipped, 'dp', axis=0, tiled=True)]
    all_to_all x2 -> x1, blocking collectives: 78.7 us -> 44.8 us  [swap_all(): return lax.all_to_all(x, axis, split_axis=0, concat_axis=0, tiled=True)]
    all_to_all x1 -> x3, waiting for transfers between devices: 0.01 us -> 28.3 us  [swap_all(): return lax.all_to_all(x, axis, split_axis=0, concat_axis=0, tiled=True)]
    ppermute x0 -> x3, starting transfers between devices: none -> 11.4 us  [to_other_core(): return lax.ppermute(x, 'core', [(0, 1), (1, 0)])]
    all_to_all x1 -> x3, starting transfers between devices: 5.1 us -> 14.5 us  [swap_all(): return lax.all_to_all(x, axis, split_axis=0, concat_axis=0, tiled=True)]
    unnamed x6 -> x32, local copies, waits for them, and re-layouts: 4.9 us -> 13.9 us
    pallas_call x4 -> x7, Pallas kernels: 18.9 us -> 13.4 us  [the longest x1 3.68 us: on_device(): pl.pallas_call(functools.partial(finish_kernel, experts), grid=(chips,),...]
    ppermute x0 -> x3, waiting for transfers between devices: none -> 2.46 us  [to_other_core(): return lax.ppermute(x, 'core', [(0, 1), (1, 0)])]
  transfers between devices with their start and end apart: 2 -> 6, of which waited for: 1 -> 4; matrix products, arithmetic and copies ran while one was open for 0% -> 1% of each run, Pallas kernels for 4% -> 5%
where the time goes in v2:
time: 133 us; the launch traced here: 132 us
  blocking collectives  44.8 us (34%)
  waiting for transfers between devices  30.8 us (23%)
  starting transfers between devices  25.9 us (19%)
  local copies, waits for them, and re-layouts  16.5 us (12%)
  Pallas kernels  13.4 us (10%)
    all_to_all x1, blocking collectives, swap_all(): return lax.all_to_all(x, axis, split_axis=0, concat_axis=0, tiled=True)  44.8 us
    all_to_all x3, waiting for transfers between devices, swap_all(): return lax.all_to_all(x, axis, split_axis=0, concat_axis=0, tiled=True)  28.3 us
    all_to_all x3, starting transfers between devices, swap_all(): return lax.all_to_all(x, axis, split_axis=0, concat_axis=0, tiled=True)  14.5 us
    unnamed x32, local copies, waits for them, and re-layouts  13.9 us
    ppermute x3, starting transfers between devices, to_other_core(): return lax.ppermute(x, 'core', [(0, 1), (1, 0)])  11.4 us
    pallas_call x1, Pallas kernels, on_device(): pl.pallas_call(functools.partial(finish_kernel, experts), grid=(chips,),...  3.68 us
    pallas_call x1, Pallas kernels, on_device(): pl.pallas_call(functools.partial(values_kernel, chips), grid=(chips,), ou...  3.42 us
  transfers between devices with their start and end apart: 6, of which 4 were waited for; matrix products, arithmetic and copies ran while one was open for 1% of the time, Pallas kernels for 5%

profile of v2, /device:TPU:1, one launch (start us, length us, event | category | flops | bytes accessed | tf_op | source)
XLA Modules:
  0.0 132.2 jit_solution(8333123893814337130)
XLA Ops:
  2.8 1.2 pack.1
  4.0 44.8 %all_to_all.27.in_ref = bf16[32,42,128]{2,1,0:T(8,128)(2,1)S(1)} all-to-all(bf16[32,42,128]{2,1,0:T(8,128)(2,1)S(1)} %pack.1), channel_id=1, replica_groups=mesh['chip'=8,'core'=2,'expert'=32] {'expert'}, dimensions={0} | all-to-all | bytes 688128 | tf_op jit(solution)/shard_map/all_to_all | solution.py:212
  49.5 1.8 %broadcast_in_dim.19 = bf16[8,448,384]{2,1,0:T(8,128)(2,1)} broadcast(bf16[448,384]{1,0:T(8,128)(2,1)S(1)} %unpack.1), dimensions={1,2} | broadcast | bytes 3096576 | tf_op jit(solution)/shard_map/broadcast_in_dim | solution.py:259
  51.2 4.3 %all-to-all-start.1 = ((bf16[8,448,384]{2,1,0:T(8,128)(2,1)}), bf16[8,448,384]{2,1,0:T(8,128)(2,1)S(1)}, u32[]{:S(2)}, u32[]{:S(2)}) async-start(bf16[8,448,384]{2,1,0:T(8,128)(2,1)} %broadcast_in_dim.19), calls=%async_computation.1 | async-start | bytes 5505024 | tf_op jit(solution)/shard_map/all_to_all | solution.py:212
  55.6 1.5 %copy-done.6 = bf16[1,128,7168]{2,1,0:T(8,128)(2,1)S(1)} copy-done((bf16[1,128,7168]{2,1,0:T(8,128)(2,1)S(1)}, bf16[1,128,7168]{2,1,0:T(8,128)(2,1)}, u32[]{:S(2)}) %copy-start.6) | copy-done | bytes 1835032
  57.9 1.0 copy-done
  58.9 5.3 %collective-permute-start = (bf16[9,128,512]{2,1,0:T(8,128)(2,1)S(1)}, bf16[9,128,512]{2,1,0:T(8,128)(2,1)S(1)}, u32[]{:S(2)}, u32[]{:S(2)}) collective-permute-start(bf16[9,128,512]{2,1,0:T(8,128)(2,1)S(1)} %get-tuple-element.17), channel_id=1, source_target_pairs={{0,32},{32,0},{1,33},{33,1},{2,34},{34,2},{3,35},{35,3},{4,36},{36... | collective-permute-start | bytes 3538952 | tf_op jit(solution)/shard_map/ppermute | solution.py:226
  64.3 2.5 %collective-permute-done.other_hidden_ref.other_ref = bf16[9,128,512]{2,1,0:T(8,128)(2,1)S(1)} collective-permute-done((bf16[9,128,512]{2,1,0:T(8,128)(2,1)S(1)}, bf16[9,128,512]{2,1,0:T(8,128)(2,1)S(1)}, u32[]{:S(2)}, u32[]{:S(2)}) %collective-permute-start) | collective-permute-done | bytes 1179680 | tf_op jit(solution)/shard_map/ppermute | solution.py:226
  66.7 1.0 copy-done.3
  67.7 21.0 %all-to-all-done.1.disp_ref = bf16[8,448,384]{2,1,0:T(8,128)(2,1)S(1)} async-done(((bf16[8,448,384]{2,1,0:T(8,128)(2,1)}), bf16[8,448,384]{2,1,0:T(8,128)(2,1)S(1)}, u32[]{:S(2)}, u32[]{:S(2)}) %all-to-all-start.1) | async-done | bytes 2752544 | tf_op jit(solution)/shard_map/all_to_all | solution.py:212
  88.7 1.3 copy-done.1
  90.0 1.3 copy-done.4
  91.3 3.4 %values.1 = (f32[128,384]{1,0:T(8,128)S(1)}, f32[128,384]{1,0:T(8,128)S(1)}, f32[32,12]{1,0:T(8,128)}) custom-call(bf16[8,448,384]{2,1,0:T(8,128)(2,1)S(1)} %all-to-all-done.1.disp_ref, bf16[9,128,512]{2,1,0:T(8,128)(2,1)S(1)} %copy-done.1, bf16[9,128,512]{2,1,0:T(8,128)(2,1)S(1)} %copy-done.4, bf16[9,128,512]{2,1,0:T(8,128)(2,1)S(1)} %copy-done.1, ...), custom_call_target="tpu_custom_call" | custom-call | flops 704643072 | bytes 4587520 | tf_op jit(solution)/shard_map/values/pallas_call | solution.py:266
  94.7 6.4 %all-to-all-start.2 = ((f32[32,1,12]{2,1,0:T(1,128)}), f32[32,1,12]{2,1,0:T(1,128)S(1)}, u32[]{:S(2)}, u32[]{:S(2)}) async-start(f32[32,1,12]{2,1,0:T(1,128)} %bitcast.6), calls=%async_computation.2 | async-start | bytes 32768 | tf_op jit(solution)/shard_map/all_to_all | solution.py:212
  101.1 1.3 copy-done.2
  102.4 1.3 copy-done.5
  103.7 2.6 %down.1 = (bf16[8,128,512]{2,1,0:T(8,128)(2,1)S(1)}, bf16[8,128,512]{2,1,0:T(8,128)(2,1)S(1)}) custom-call(bf16[8,448,384]{2,1,0:T(8,128)(2,1)S(1)} %all-to-all-done.1.disp_ref, bf16[9,128,512]{2,1,0:T(8,128)(2,1)S(1)} %copy-done.2, bf16[9,128,512]{2,1,0:T(8,128)(2,1)S(1)} %copy-done.5), custom_call_target="tpu_custom_call" | custom-call | flops 704643072 | bytes 4587520 | tf_op jit(solution)/shard_map/down/pallas_call | solution.py:284
  107.3 1.0 copy-done.15
  108.3 6.4 %all-to-all-done.2 = f32[32,1,12]{2,1,0:T(1,128)S(1)} async-done(((f32[32,1,12]{2,1,0:T(1,128)}), f32[32,1,12]{2,1,0:T(1,128)S(1)}, u32[]{:S(2)}, u32[]{:S(2)}) %all-to-all-start.2) | async-done | bytes 1568 | tf_op jit(solution)/shard_map/all_to_all | solution.py:212
  114.7 4.2 %collective-permute-start.1 = (bf16[8,128,512]{2,1,0:T(8,128)(2,1)}, bf16[8,128,512]{2,1,0:T(8,128)(2,1)S(1)}, u32[]{:S(2)}, u32[]{:S(2)}) collective-permute-start(bf16[8,128,512]{2,1,0:T(8,128)(2,1)} %copy-done.15), channel_id=1, source_target_pairs={{0,32},{32,0},{1,33},{33,1},{2,34},{34,2},{3,35},{35,3},{4,36},{36... | collective-permute-start | bytes 3145736 | tf_op jit(solution)/shard_map/ppermute | solution.py:226
  118.9 1.9 %collective-permute-start.2 = (f32[128,384]{1,0:T(8,128)S(1)}, f32[128,384]{1,0:T(8,128)S(1)}, u32[]{:S(2)}, u32[]{:S(2)}) collective-permute-start(f32[128,384]{1,0:T(8,128)S(1)} %get-tuple-element.24), channel_id=1, source_target_pairs={{0,32},{32,0},{1,33},{33,1},{2,34},{34,2},{3,35},{35,3},{4,36},{36... | collective-permute-start | bytes 589832 | tf_op jit(solution)/shard_map/ppermute | solution.py:226
  121.6 3.8 %all-to-all-start.3 = ((f32[16,3,128]{2,1,0:T(4,128)}), f32[16,3,128]{2,1,0:T(4,128)S(1)}, u32[]{:S(2)}, u32[]{:S(2)}) async-start(f32[16,3,128]{2,1,0:T(4,128)} %broadcast_in_dim.23), calls=%async_computation.3 | async-start | bytes 65536 | tf_op jit(solution)/shard_map/all_to_all | solution.py:212
  125.4 1.2 copy-done.8
  126.6 3.7 %finish.1 = (bf16[128,7168]{1,0:T(8,128)(2,1)}, bf16[384,128]{1,0:T(8,128)(2,1)}) custom-call(s32[1]{0:T(128)} %bitcast.core_ref, bf16[8,128,512]{2,1,0:T(8,128)(2,1)S(1)} %copy-done.8, bf16[8,128,512]{2,1,0:T(8,128)(2,1)S(1)} %collective-permute-done.1.got_ref, f32[128,384]{1,0:T(8,128)S(1)} %get-tuple-element.23.values_ref, ...), custom_call_target="tpu_custom_call" | custom-call | flops 37748736 | bytes 3670016 | tf_op jit(solution)/shard_map/finish/pallas_call | solution.py:299
  (32 shorter events, 7.3 us)
Async XLA Ops:
  0.6 0.8 copy-start.10
  1.4 0.7 copy-start.11
  2.1 0.7 copy-start.13
  51.2 4.3 %copy-start.9 = (bf16[1,384,128]{2,1,0:T(8,128)(2,1)S(1)}, bf16[1,384,128]{2,1,0:T(8,128)(2,1)}, u32[]{:S(2)}) copy-start(bf16[1,384,128]{2,1,0:T(8,128)(2,1)} %param.8) | copy-start | bytes 294916
  51.2 37.5 %all-to-all-start.1 = ((bf16[8,448,384]{2,1,0:T(8,128)(2,1)}), bf16[8,448,384]{2,1,0:T(8,128)(2,1)S(1)}, u32[]{:S(2)}, u32[]{:S(2)}) async-start(bf16[8,448,384]{2,1,0:T(8,128)(2,1)} %broadcast_in_dim.19), calls=%async_computation.1 | async-start | bytes 5505024 | tf_op jit(solution)/shard_map/all_to_all | solution.py:212
  55.6 1.5 %copy-start.6 = (bf16[1,128,7168]{2,1,0:T(8,128)(2,1)S(1)}, bf16[1,128,7168]{2,1,0:T(8,128)(2,1)}, u32[]{:S(2)}) copy-start(bf16[1,128,7168]{2,1,0:T(8,128)(2,1)} %param.9) | copy-start | bytes 5505028
  57.9 1.0 copy-start
  58.9 7.8 %collective-permute-start = (bf16[9,128,512]{2,1,0:T(8,128)(2,1)S(1)}, bf16[9,128,512]{2,1,0:T(8,128)(2,1)S(1)}, u32[]{:S(2)}, u32[]{:S(2)}) collective-permute-start(bf16[9,128,512]{2,1,0:T(8,128)(2,1)S(1)} %get-tuple-element.17), channel_id=1, source_target_pairs={{0,32},{32,0},{1,33},{33,1},{2,34},{34,2},{3,35},{35,3},{4,36},{36... | collective-permute-start | bytes 3538952 | tf_op jit(solution)/shard_map/ppermute | solution.py:226
  66.7 1.0 copy-start.3
  88.7 1.3 copy-start.1
  90.0 1.3 copy-start.4
  94.7 20.0 %all-to-all-start.2 = ((f32[32,1,12]{2,1,0:T(1,128)}), f32[32,1,12]{2,1,0:T(1,128)S(1)}, u32[]{:S(2)}, u32[]{:S(2)}) async-start(f32[32,1,12]{2,1,0:T(1,128)} %bitcast.6), calls=%async_computation.2 | async-start | bytes 32768 | tf_op jit(solution)/shard_map/all_to_all | solution.py:212
  101.1 1.3 copy-start.2
  102.4 1.3 copy-start.5
  106.3 1.0 copy-start.7
  107.3 1.0 copy-start.15
  108.3 22.9 %copy-start.12 = (s32[32,8]{0,1:T(8,128)S(1)}, s32[32,8]{0,1:T(8,128)}, u32[]{:S(2)}) copy-start(s32[32,8]{0,1:T(8,128)} %param.6) | copy-start | bytes 3076
  108.3 22.9 %copy-start.14 = (f32[32,8]{0,1:T(8,128)S(1)}, f32[32,8]{0,1:T(8,128)}, u32[]{:S(2)}) copy-start(f32[32,8]{0,1:T(8,128)} %param.7) | copy-start | bytes 3076
  114.7 10.6 %collective-permute-start.1 = (bf16[8,128,512]{2,1,0:T(8,128)(2,1)}, bf16[8,128,512]{2,1,0:T(8,128)(2,1)S(1)}, u32[]{:S(2)}, u32[]{:S(2)}) collective-permute-start(bf16[8,128,512]{2,1,0:T(8,128)(2,1)} %copy-done.15), channel_id=1, source_target_pairs={{0,32},{32,0},{1,33},{33,1},{2,34},{34,2},{3,35},{35,3},{4,36},{36... | collective-permute-start | bytes 3145736 | tf_op jit(solution)/shard_map/ppermute | solution.py:226
  118.9 6.5 %collective-permute-start.2 = (f32[128,384]{1,0:T(8,128)S(1)}, f32[128,384]{1,0:T(8,128)S(1)}, u32[]{:S(2)}, u32[]{:S(2)}) collective-permute-start(f32[128,384]{1,0:T(8,128)S(1)} %get-tuple-element.24), channel_id=1, source_target_pairs={{0,32},{32,0},{1,33},{33,1},{2,34},{34,2},{3,35},{35,3},{4,36},{36... | collective-permute-start | bytes 589832 | tf_op jit(solution)/shard_map/ppermute | solution.py:226
  121.6 9.6 %all-to-all-start.3 = ((f32[16,3,128]{2,1,0:T(4,128)}), f32[16,3,128]{2,1,0:T(4,128)S(1)}, u32[]{:S(2)}, u32[]{:S(2)}) async-start(f32[16,3,128]{2,1,0:T(4,128)} %broadcast_in_dim.23), calls=%async_computation.3 | async-start | bytes 65536 | tf_op jit(solution)/shard_map/all_to_all | solution.py:212
  125.4 1.2 copy-start.8

commit v3 on v2

v3 whole, which is shorter than its diff:
```python
import functools

import jax
import jax.numpy as jnp
from jax import lax
from jax.experimental import pallas as pl
from jax.experimental.pallas import tpu as pltpu
from jax.sharding import Mesh, PartitionSpec as P

F32 = jnp.float32
BF16 = jnp.bfloat16
LANES = 128


def ranks(routes, experts):
    top, tokens = routes.shape
    ids = lax.broadcasted_iota(jnp.int32, (experts, tokens), 0)
    named = [routes[k : k + 1, :] == ids for k in range(top)]
    present = functools.reduce(jnp.logical_or, named)
    rows = lax.broadcasted_iota(jnp.int32, (tokens, tokens), 0)
    columns = lax.broadcasted_iota(jnp.int32, (tokens, tokens), 1)
    earlier = (rows < columns).astype(F32)
    before = jnp.dot(present.astype(F32), earlier, preferred_element_type=F32)
    return named, present, before


def pack_kernel(grad_ref, routes_ref, gates_ref, out_ref):
    experts, lines, length = out_ref.shape
    grad = grad_ref[...]
    fitting = length // grad.shape[1]
    named, present, before = ranks(routes_ref[...], experts)
    gates = gates_ref[...]
    gate = jnp.zeros(present.shape, F32)
    for k, here in enumerate(named):
        gate = jnp.where(here, gates[k : k + 1, :], gate)

    def slot(c):
        placed = jnp.logical_and(present, before == c).astype(F32)
        row_gate = jnp.sum(placed * gate, axis=1, keepdims=True)
        return row_gate * jnp.dot(
            placed.astype(BF16), grad, preferred_element_type=F32
        )

    for line in range(lines):
        rows = [slot(fitting * line + i) for i in range(fitting)]
        out_ref[:, line, :] = jnp.concatenate(rows, axis=1).astype(BF16)


def unpack_kernel(in_ref, out_ref, flipped, done):
    sources, lines, length = in_ref.shape
    share, slots = flipped.shape
    fitting = length // share
    rows = [in_ref[:, line, :].astype(F32) for line in range(lines)]
    group = LANES // sources
    for g in range(slots // LANES):
        parts = []
        for c in range(g * group, (g + 1) * group):
            start = share * (c % fitting)
            parts.append(rows[c // fitting][:, start : start + share])
        block = jnp.concatenate(parts, axis=0)
        flipped[:, LANES * g : LANES * (g + 1)] = block.T.astype(BF16)
    copies = [
        pltpu.make_async_copy(flipped, out_ref.at[i], done.at[i])
        for i in range(out_ref.shape[0])
    ]
    for copy in copies:
        copy.start()
    for copy in copies:
        copy.wait()


def split_kernel(
    sources, core_ref, weight_ref, hidden_ref, keep_ref, send_ref, order_ref
):
    blocks = keep_ref.shape[0] - 1
    share = weight_ref.shape[1] // (2 * blocks)
    slots = hidden_ref.shape[0]
    capacity = slots // sources
    rows = lax.broadcasted_iota(jnp.int32, (slots, slots), 0)
    columns = lax.broadcasted_iota(jnp.int32, (slots, slots), 1)
    matches = (rows % capacity) * sources + rows // capacity == columns
    order = matches.astype(F32).astype(BF16)
    order_ref[...] = order
    flipped = lax.dot_general(
        hidden_ref[...], order, (((0,), (0,)), ((), ())), preferred_element_type=F32
    ).astype(BF16)
    for ref in (keep_ref, send_ref):
        ref[:, :, ref.shape[2] - LANES :] = jnp.zeros((*ref.shape[:2], LANES), BF16)
        ref[blocks, :, :slots] = flipped

    def store(first, second):
        for j in range(blocks):
            both = weight_ref[:, 2 * share * j : 2 * share * (j + 1)]
            first[j, :, :share] = both[:, :share]
            second[j, :, :share] = both[:, share:]

    pl.when(core_ref[0] == 0)(lambda: store(keep_ref, send_ref))
    pl.when(core_ref[0] != 0)(lambda: store(send_ref, keep_ref))


def values_kernel(
    far, disp_ref, keep_ref, other_ref, mine_ref, theirs_ref, gate_ref, weight, done
):
    blocks, share, slots = disp_ref.shape
    units = mine_ref.shape[0]
    copies = [
        [
            pltpu.make_async_copy(ref.at[j], weight.at[j, half], done.at[j, half])
            for half, ref in enumerate((keep_ref, other_ref))
        ]
        for j in range(blocks + 1)
    ]
    for pair in copies:
        for copy in pair:
            copy.start()
    values = jnp.zeros((2 * units, slots), F32)
    for j in range(blocks):
        for copy in copies[j]:
            copy.wait()
        both = weight[j].reshape(2 * units, weight.shape[3])[:, :share]
        values += jnp.dot(both, disp_ref[j], preferred_element_type=F32)
    for copy in copies[blocks]:
        copy.wait()
    hidden = weight[blocks].reshape(2 * units, weight.shape[3])[:, :slots]
    terms = jnp.sum(hidden.astype(F32) * values, axis=0, keepdims=True)
    mine_ref[...] = values[:units]
    theirs_ref[...] = values[units:]

    near, width = gate_ref.shape
    member = lax.broadcasted_iota(jnp.int32, (near, slots), 1)
    owner = lax.broadcasted_iota(jnp.int32, (near, slots), 0)
    spread = jnp.where(member % near == owner, terms, 0.0)
    slot = lax.broadcasted_iota(jnp.int32, (slots, width), 0) // near
    column = lax.broadcasted_iota(jnp.int32, (slots, width), 1)
    fold = (slot % far) * (width // far) + slot // far == column
    gate_ref[...] = jnp.dot(
        spread,
        fold.astype(F32),
        preferred_element_type=F32,
        precision=lax.Precision.HIGHEST,
    )


def down_kernel(
    disp_ref, keep_hidden_ref, other_hidden_ref, values_ref, mine_ref, theirs_ref
):
    blocks, share, slots = disp_ref.shape
    units = values_ref.shape[0]
    hidden = jnp.concatenate([keep_hidden_ref[0], other_hidden_ref[0]], axis=0)
    hidden = hidden[:, :slots]
    for ref in (mine_ref, theirs_ref):
        ref[:, :, ref.shape[2] - LANES :] = jnp.zeros((*ref.shape[:2], LANES), BF16)
    for j in range(blocks):
        product = lax.dot_general(
            hidden, disp_ref[j], (((1,), (1,)), ((), ())), preferred_element_type=F32
        ).astype(BF16)
        mine_ref[j, :, :share] = product[:units]
        theirs_ref[j, :, :share] = product[units:]
    values = values_ref[...]
    high = values.astype(BF16)
    theirs_ref[blocks, :, :slots] = high
    theirs_ref[blocks + 1, :, :slots] = (values - high.astype(F32)).astype(BF16)


def finish_kernel(
    core_ref,
    mine_ref,
    got_ref,
    values_ref,
    order_ref,
    down_ref,
    dhid_ref,
):
    step, blocks = pl.program_id(0), mine_ref.shape[0]
    last = got_ref.shape[0] - 2
    share = down_ref.shape[1] // (2 * blocks)
    slots = values_ref.shape[1]

    def store(mine_first):
        for j in range(blocks):
            start = 2 * share * j
            both = [mine_ref[j, :, :share], got_ref[step * blocks + j, :, :share]]
            both = both if mine_first else both[::-1]
            down_ref[:, start : start + 2 * share] = jnp.concatenate(both, axis=1)

    pl.when(core_ref[0] == 0)(lambda: store(True))
    pl.when(core_ref[0] != 0)(lambda: store(False))

    @pl.when(step == 0)
    def _():
        high = got_ref[last, :, :slots].astype(F32)
        low = got_ref[last + 1, :, :slots].astype(F32)
        values = (values_ref[...] + (high + low)).T.astype(BF16)
        dhid_ref[...] = jnp.dot(
            order_ref[...], values, preferred_element_type=F32
        ).astype(BF16)


def gate_kernel(near, capacity, parts_ref, routes_ref, gates_ref, out_ref):
    experts = parts_ref.shape[1] * LANES // capacity
    named, present, before = ranks(routes_ref[...], experts)
    terms = jnp.sum(parts_ref[...], axis=0)
    matched = jnp.zeros(present.shape, F32)
    for c in range(capacity):
        pieces = []
        for far in range(experts // near):
            line, lane = divmod((far * capacity + c) * near, LANES)
            pieces.append(terms[line : line + 1, lane : lane + near])
        row = jnp.concatenate(pieces, axis=1)
        spread = jnp.broadcast_to(row, (8, experts)).T[:, :1]
        here = jnp.logical_and(present, before == c)
        matched = jnp.where(here, spread, matched)
    total = [jnp.sum(jnp.where(n, matched, 0.0), axis=0, keepdims=True) for n in named]
    out_ref[...] = jnp.concatenate(total, axis=0) / gates_ref[...]


def whole():
    return pl.BlockSpec(memory_space=pltpu.VMEM)


def scalar():
    return pl.BlockSpec(memory_space=pltpu.SMEM)


def stays():
    return pl.BlockSpec(memory_space=pltpu.HBM)


def in_hbm(x):
    return pltpu.with_memory_space_constraint(x, pltpu.HBM)


def in_vmem(x):
    return pltpu.with_memory_space_constraint(x, pltpu.VMEM)


def limit(mib):
    return pltpu.CompilerParams(vmem_limit_bytes=mib * 2**20)


def cost(flops, moved):
    return pl.CostEstimate(flops=flops, bytes_accessed=moved, transcendentals=0)


def swap_all(x, axis):
    return lax.all_to_all(x, axis, split_axis=0, concat_axis=0, tiled=True)


def on_device(grad_out, routes, gates, hidden, w_down):
    near, far = lax.axis_size("near"), lax.axis_size("far")
    experts, chips = near * far, lax.axis_size("chip")
    _, slots, units = hidden.shape
    width = w_down.shape[2]
    capacity = slots // experts
    share = grad_out.shape[1]
    padded = -(-share // LANES) * LANES
    core = lax.axis_index("core").astype(jnp.int32).reshape(1)
    routes, gates = routes.T, gates.T
    bf16 = functools.partial(pltpu.HBM, dtype=BF16)
    f32 = functools.partial(pltpu.HBM, dtype=F32)

    def to_other_core(x):
        return lax.ppermute(x, "core", [(0, 1), (1, 0)])

    packed = pl.pallas_call(
        pack_kernel,
        out_shape=jax.ShapeDtypeStruct((experts, 2, capacity * share // 2), BF16),
        in_specs=[whole()] * 3,
        out_specs=whole(),
        name="pack",
    )(grad_out, routes, gates)
    arrived = swap_all(packed, ("far", "near"))

    half = bf16((chips + 1, units, padded))
    keep, send, order = pl.pallas_call(
        functools.partial(split_kernel, experts),
        out_shape=(half, half, bf16((slots, slots))),
        in_specs=[scalar(), whole(), whole()],
        out_specs=(whole(),) * 3,
        cost_estimate=cost(2 * units * slots * slots, 2 * 2 * units * width),
        name="split",
    )(core, w_down[0], hidden[0])
    other = in_hbm(to_other_core(send))
    keep, order = in_hbm(keep), in_hbm(order)

    copies = pl.pallas_call(
        unpack_kernel,
        out_shape=bf16((chips, share, slots)),
        in_specs=[whole()],
        out_specs=pl.BlockSpec(memory_space=pl.ANY),
        scratch_shapes=[
            pltpu.VMEM((share, slots), BF16),
            pltpu.SemaphoreType.DMA((chips,)),
        ],
        compiler_params=limit(8),
        name="unpack",
    )(arrived)
    dispatched = in_vmem(swap_all(copies, "chip"))

    flops = 2 * slots * units * width
    mine, theirs, terms = pl.pallas_call(
        functools.partial(values_kernel, far),
        out_shape=(
            f32((units, slots)),
            f32((units, slots)),
            jax.ShapeDtypeStruct((near, far * capacity), F32),
        ),
        in_specs=[whole(), stays(), stays()],
        out_specs=(whole(),) * 3,
        scratch_shapes=[
            pltpu.VMEM((chips + 1, 2, units, padded), BF16),
            pltpu.SemaphoreType.DMA((chips + 1, 2)),
        ],
        compiler_params=limit(16),
        cost_estimate=cost(flops, slots * width + 2 * units * width),
        name="values",
    )(dispatched, keep, other)
    returned = swap_all(terms, "near")
    theirs = in_hbm(theirs)

    last = pl.BlockSpec((1, units, padded), lambda i: (chips, 0, 0))
    table = pl.BlockSpec((units, slots), lambda i: (0, 0))
    down, beside = pl.pallas_call(
        down_kernel,
        grid=(1,),
        out_shape=(
            bf16((chips, units, padded)),
            bf16((chips + 2, units, padded)),
        ),
        in_specs=[whole(), last, last, table],
        out_specs=(whole(), whole()),
        compiler_params=limit(16),
        cost_estimate=cost(flops, slots * width + 2 * units * width),
        name="down",
    )(dispatched, keep, other, theirs)
    returned, beside = lax.optimization_barrier((returned, beside))
    got = in_vmem(to_other_core(beside))
    down, mine = in_hbm(down), in_hbm(mine)

    steps = 4
    some = pl.BlockSpec((chips // steps, units, padded), lambda i: (i, 0, 0))

    d_down, d_hidden = pl.pallas_call(
        finish_kernel,
        grid=(steps,),
        out_shape=(
            jax.ShapeDtypeStruct((units, width), BF16),
            jax.ShapeDtypeStruct((slots, units), BF16),
        ),
        in_specs=[
            scalar(),
            some,
            whole(),
            table,
            pl.BlockSpec((slots, slots), lambda i: (0, 0)),
        ],
        out_specs=(
            pl.BlockSpec((units, width // steps), lambda i: (0, i)),
            pl.BlockSpec((slots, units), lambda i: (0, 0)),
        ),
        compiler_params=limit(16),
        cost_estimate=cost(2 * units * slots * slots, 4 * units * width),
        name="finish",
    )(core, down, got, mine, order)

    returned = returned.reshape(near, far, capacity).transpose(1, 2, 0)
    returned = swap_all(returned.reshape(far, near * capacity), "far")
    flat = returned.reshape(1, slots // LANES, LANES)
    flat = jnp.broadcast_to(flat, (2 * chips, *flat.shape[1:]))
    everyone = swap_all(flat, ("chip", "core"))
    everyone, _ = lax.optimization_barrier((everyone, d_hidden))
    d_gate = pl.pallas_call(
        functools.partial(gate_kernel, near, capacity),
        out_shape=jax.ShapeDtypeStruct(gates.shape, F32),
        in_specs=[whole()] * 3,
        out_specs=whole(),
        compiler_params=limit(4),
        name="match",
    )(everyone, routes, gates)
    return (d_hidden[None], d_down[None], d_gate.T)


def solution(mesh):
    parts, experts = mesh.devices.shape
    devices = mesh.devices.reshape(parts // 2, 2, 2, experts // 2)
    finer = Mesh(devices, ("chip", "core", "far", "near"))
    dp, expert = ("chip", "core"), ("far", "near")
    in_specs = (
        P(expert, dp),
        P(expert, None),
        P(expert, None),
        P(expert, None, dp),
        P(expert, dp, None),
    )
    out_specs = (P(expert, None, dp), P(expert, dp, None), P(expert, None))
    return jax.shard_map(
        on_device, mesh=finer, in_specs=in_specs, out_specs=out_specs, check_vma=False
    )
```

time: 133 us -> 129 us (0.970)
  local copies, waits for them, and re-layouts: 16.5 us -> 0.96 us
  Pallas kernels: 13.4 us -> 20.8 us
  blocking collectives: 44.8 us -> 49.6 us
  starting transfers between devices: 25.9 us -> 23.5 us
  waiting for transfers between devices: 30.8 us -> 33 us
    unnamed x32 -> x4, local copies, waits for them, and re-layouts: 13.9 us -> 0.01 us
    all_to_all x1 -> x2, blocking collectives: 44.8 us -> 49.6 us  [swap_all(): return lax.all_to_all(x, axis, split_axis=0, concat_axis=0, tiled=True)]
    pallas_call x6, Pallas kernels: 12.5 us -> 16.9 us  [the longest x1 4.29 us: on_device(): pl.pallas_call(finish_kernel, grid=(steps,), out_shape=(jax.ShapeDtypeStr...]
    pallas_call x1, Pallas kernels: 0.84 us -> 3.87 us  [on_device(): pl.pallas_call(functools.partial(split_kernel, experts), out_shape=(half,...]
    ppermute x3 -> x2, starting transfers between devices: 11.4 us -> 9.46 us  [to_other_core(): return lax.ppermute(x, 'core', [(0, 1), (1, 0)])]
    all_to_all x3, waiting for transfers between devices: 28.3 us -> 30.2 us  [swap_all(): return lax.all_to_all(x, axis, split_axis=0, concat_axis=0, tiled=True)]
    broadcast_in_dim x3 -> x2, local copies, waits for them, and re-layouts: 2.48 us -> 0.69 us  [on_device(): flat = jnp.broadcast_to(flat, (2 * chips, *flat.shape[1:]))]
    ppermute x3 -> x2, waiting for transfers between devices: 2.46 us -> 2.8 us  [to_other_core(): return lax.ppermute(x, 'core', [(0, 1), (1, 0)])]
  transfers between devices with their start and end apart: 6 -> 5, of which waited for: 4 -> 4; matrix products, arithmetic and copies ran while one was open for 1% -> 1% of each run, Pallas kernels for 5% -> 9%
where the time goes in v3:
time: 129 us
  blocking collectives  49.6 us (38%)
  waiting for transfers between devices  33 us (26%)
  starting transfers between devices  23.5 us (18%)
  Pallas kernels  20.8 us (16%)
    all_to_all x2, blocking collectives, swap_all(): return lax.all_to_all(x, axis, split_axis=0, concat_axis=0, tiled=True)  49.6 us
    all_to_all x3, waiting for transfers between devices, swap_all(): return lax.all_to_all(x, axis, split_axis=0, concat_axis=0, tiled=True)  30.2 us
    all_to_all x3, starting transfers between devices, swap_all(): return lax.all_to_all(x, axis, split_axis=0, concat_axis=0, tiled=True)  14.1 us
    ppermute x2, starting transfers between devices, to_other_core(): return lax.ppermute(x, 'core', [(0, 1), (1, 0)])  9.46 us
    pallas_call x1, Pallas kernels, on_device(): pl.pallas_call(finish_kernel, grid=(steps,), out_shape=(jax.ShapeDtypeStr...  4.29 us
    pallas_call x1, Pallas kernels, on_device(): pl.pallas_call(functools.partial(values_kernel, far), out_shape=(f32((uni...  3.93 us
    pallas_call x1, Pallas kernels, on_device(): pl.pallas_call(functools.partial(split_kernel, experts), out_shape=(half,...  3.87 us
    pallas_call x1, Pallas kernels, on_device(): pl.pallas_call(down_kernel, grid=(1,), out_shape=(bf16((chips, units, pad...  3.7 us
  transfers between devices with their start and end apart: 5, of which 4 were waited for; matrix products, arithmetic and copies ran while one was open for 1% of the time, Pallas kernels for 9%

profile of v3, /device:TPU:1, one launch (start us, length us, event | category | flops | bytes accessed | tf_op | source)
XLA Modules:
  0.0 128.6 jit_solution(10013459769507005003)
XLA Ops:
  0.6 2.0 %pack.1 = bf16[32,2,2688]{2,1,0:T(2,128)(2,1)} custom-call(bf16[32,448]{1,0:T(8,128)(2,1)} %grad_ref.1, s32[8,32]{1,0:T(8,128)} %bitcast.13, f32[8,32]{1,0:T(8,128)} %bitcast.15), custom_call_target="tpu_custom_call" | custom-call | tf_op jit(solution)/shard_map/pack/pallas_call | solution.py:265
  2.6 43.2 %all_to_all.37.in_ref = bf16[32,2,2688]{2,1,0:T(2,128)(2,1)S(1)} all-to-all(bf16[32,2,2688]{2,1,0:T(2,128)(2,1)} %pack.1), channel_id=1, replica_groups=mesh['chip'=8,'core'=2,'far'=2,'near'=16] {'far','near'}, dimensions={0} | all-to-all | bytes 688128 | tf_op jit(solution)/shard_map/all_to_all | solution.py:246
  45.8 2.1 %unpack.1 = bf16[8,448,384]{2,1,0:T(8,128)(2,1)} custom-call(bf16[32,2,2688]{2,1,0:T(2,128)(2,1)S(1)} %all_to_all.37.in_ref), custom_call_target="tpu_custom_call" | custom-call | tf_op jit(solution)/shard_map/unpack/pallas_call | solution.py:286
  47.9 4.2 %all-to-all-start.1 = ((bf16[8,448,384]{2,1,0:T(8,128)(2,1)}), bf16[8,448,384]{2,1,0:T(8,128)(2,1)S(1)}, u32[]{:S(2)}, u32[]{:S(2)}) async-start(bf16[8,448,384]{2,1,0:T(8,128)(2,1)} %unpack.1), calls=%async_computation.1 | async-start | bytes 5505024 | tf_op jit(solution)/shard_map/all_to_all | solution.py:246
  52.1 3.9 %split.1 = (bf16[9,128,512]{2,1,0:T(8,128)(2,1)}, bf16[9,128,512]{2,1,0:T(8,128)(2,1)}, bf16[384,384]{1,0:T(8,128)(2,1)}) custom-call(s32[1]{0:T(128)} %bitcast.core_ref, bf16[128,7168]{1,0:T(8,128)(2,1)} %bitcast.17, bf16[384,128]{1,0:T(8,128)(2,1)} %bitcast.18), custom_call_target="tpu_custom_call" | custom-call | flops 37748736 | bytes 3670016 | tf_op jit(solution)/shard_map/split/pallas_call | solution.py:275
  56.0 5.3 %collective-permute-start = (bf16[9,128,512]{2,1,0:T(8,128)(2,1)}, bf16[9,128,512]{2,1,0:T(8,128)(2,1)}, u32[]{:S(2)}, u32[]{:S(2)}) collective-permute-start(bf16[9,128,512]{2,1,0:T(8,128)(2,1)} %get-tuple-element.17), channel_id=1, source_target_pairs={{0,32},{32,0},{1,33},{33,1},{2,34},{34,2},{3,35},{35,3},{4,36},{36... | collective-permute-start | bytes 3538952 | tf_op jit(solution)/shard_map/ppermute | solution.py:263
  61.3 2.8 %collective-permute-done.other_ref.other_hidden_ref = bf16[9,128,512]{2,1,0:T(8,128)(2,1)} collective-permute-done((bf16[9,128,512]{2,1,0:T(8,128)(2,1)}, bf16[9,128,512]{2,1,0:T(8,128)(2,1)}, u32[]{:S(2)}, u32[]{:S(2)}) %collective-permute-start) | collective-permute-done | bytes 1179680 | tf_op jit(solution)/shard_map/ppermute | solution.py:263
  64.1 21.2 %all-to-all-done.1.disp_ref = bf16[8,448,384]{2,1,0:T(8,128)(2,1)S(1)} async-done(((bf16[8,448,384]{2,1,0:T(8,128)(2,1)}), bf16[8,448,384]{2,1,0:T(8,128)(2,1)S(1)}, u32[]{:S(2)}, u32[]{:S(2)}) %all-to-all-start.1) | async-done | bytes 2752544 | tf_op jit(solution)/shard_map/all_to_all | solution.py:246
  85.3 3.9 %values.1 = (f32[128,384]{1,0:T(8,128)}, f32[128,384]{1,0:T(8,128)}, f32[16,24]{1,0:T(8,128)}) custom-call(bf16[8,448,384]{2,1,0:T(8,128)(2,1)S(1)} %all-to-all-done.1.disp_ref, bf16[9,128,512]{2,1,0:T(8,128)(2,1)} %get-tuple-element.16.keep_ref.keep_hidden_ref, bf16[9,128,512]{2,1,0:T(8,128)(2,1)} %collective-permute-done.other_ref.other_hidden_ref), custom_call_target="tpu_custom_call" | custom-call | flops 704643072 | bytes 4587520 | tf_op jit(solution)/shard_map/values/pallas_call | solution.py:301
  89.2 5.1 %all-to-all-start.2 = ((f32[16,1,24]{2,1,0:T(1,128)}), f32[16,1,24]{2,1,0:T(1,128)S(1)}, u32[]{:S(2)}, u32[]{:S(2)}) async-start(f32[16,1,24]{2,1,0:T(1,128)} %bitcast.6), calls=%async_computation.2 | async-start | bytes 16384 | tf_op jit(solution)/shard_map/all_to_all | solution.py:246
  94.3 3.7 %down.1 = (bf16[8,128,512]{2,1,0:T(8,128)(2,1)}, bf16[10,128,512]{2,1,0:T(8,128)(2,1)}) custom-call(bf16[8,448,384]{2,1,0:T(8,128)(2,1)S(1)} %all-to-all-done.1.disp_ref, bf16[9,128,512]{2,1,0:T(8,128)(2,1)} %get-tuple-element.16.keep_ref.keep_hidden_ref, bf16[9,128,512]{2,1,0:T(8,128)(2,1)} %collective-permute-done.other_ref.other_hidden_ref, ...), custom_call_target="tpu_custom_call" | custom-call | flops 704643072 | bytes 4587520 | tf_op jit(solution)/shard_map/down/pallas_call | solution.py:323
  98.0 7.5 %all-to-all-done.2 = f32[16,1,24]{2,1,0:T(1,128)S(1)} async-done(((f32[16,1,24]{2,1,0:T(1,128)}), f32[16,1,24]{2,1,0:T(1,128)S(1)}, u32[]{:S(2)}, u32[]{:S(2)}) %all-to-all-start.2) | async-done | bytes 1568 | tf_op jit(solution)/shard_map/all_to_all | solution.py:246
  105.5 4.2 %collective-permute-start.1 = (bf16[10,128,512]{2,1,0:T(8,128)(2,1)}, bf16[10,128,512]{2,1,0:T(8,128)(2,1)S(1)}, u32[]{:S(2)}, u32[]{:S(2)}) collective-permute-start(bf16[10,128,512]{2,1,0:T(8,128)(2,1)} %get-tuple-element.22), channel_id=1, source_target_pairs={{0,32},{32,0},{1,33},{33,1},{2,34},{34,2},{3,35},{35,3},{4,36},{36... | collective-permute-start | bytes 3932168 | tf_op jit(solution)/shard_map/ppermute | solution.py:263
  109.7 0.1 reshape.22
  109.8 0.1 copy.10
  109.9 0.1 all_to_all.31
  109.9 6.5 %all_to_all.38 = f32[2,1,192]{2,1,0:T(1,128)S(1)} all-to-all(f32[2,1,192]{2,1,0:T(1,128)S(1)} %all_to_all.31), channel_id=1, replica_groups=mesh['chip'=8,'core'=2,'far'=2,'near'=16] {'far'}, dimensions={0} | all-to-all | bytes 3072 | tf_op jit(solution)/shard_map/all_to_all | solution.py:246
  116.4 0.1 broadcast_in_dim.15
  116.5 0.6 broadcast_in_dim.16
  117.1 4.8 %all-to-all-start.4 = ((f32[16,3,128]{2,1,0:T(4,128)}), f32[16,3,128]{2,1,0:T(4,128)S(1)}, u32[]{:S(2)}, u32[]{:S(2)}) async-start(f32[16,3,128]{2,1,0:T(4,128)} %broadcast_in_dim.16), calls=%async_computation.4 | async-start | bytes 65536 | tf_op jit(solution)/shard_map/all_to_all | solution.py:246
  121.9 0.0 copy-start.1
  121.9 4.3 %finish.1 = (bf16[128,7168]{1,0:T(8,128)(2,1)}, bf16[384,128]{1,0:T(8,128)(2,1)}) custom-call(s32[1]{0:T(128)} %bitcast.core_ref, bf16[8,128,512]{2,1,0:T(8,128)(2,1)} %get-tuple-element.19.mine_ref, bf16[10,128,512]{2,1,0:T(8,128)(2,1)S(1)} %collective-permute-done.1.got_ref, f32[128,384]{1,0:T(8,128)} %get-tuple-element.23.values_ref, ...), custom_call_target="tpu_custom_call" | custom-call | flops 37748736 | bytes 3670016 | tf_op jit(solution)/shard_map/finish/pallas_call | solution.py:343
  126.2 1.5 %all-to-all-done.4.parts_ref = f32[16,3,128]{2,1,0:T(4,128)S(1)} async-done(((f32[16,3,128]{2,1,0:T(4,128)}), f32[16,3,128]{2,1,0:T(4,128)S(1)}, u32[]{:S(2)}, u32[]{:S(2)}) %all-to-all-start.4) | async-done | bytes 24608 | tf_op jit(solution)/shard_map/all_to_all | solution.py:246
  127.7 0.9 match.1
  (5 shorter events, 0.0 us)
Async XLA Ops:
  47.9 37.4 %all-to-all-start.1 = ((bf16[8,448,384]{2,1,0:T(8,128)(2,1)}), bf16[8,448,384]{2,1,0:T(8,128)(2,1)S(1)}, u32[]{:S(2)}, u32[]{:S(2)}) async-start(bf16[8,448,384]{2,1,0:T(8,128)(2,1)} %unpack.1), calls=%async_computation.1 | async-start | bytes 5505024 | tf_op jit(solution)/shard_map/all_to_all | solution.py:246
  56.0 8.1 %collective-permute-start = (bf16[9,128,512]{2,1,0:T(8,128)(2,1)}, bf16[9,128,512]{2,1,0:T(8,128)(2,1)}, u32[]{:S(2)}, u32[]{:S(2)}) collective-permute-start(bf16[9,128,512]{2,1,0:T(8,128)(2,1)} %get-tuple-element.17), channel_id=1, source_target_pairs={{0,32},{32,0},{1,33},{33,1},{2,34},{34,2},{3,35},{35,3},{4,36},{36... | collective-permute-start | bytes 3538952 | tf_op jit(solution)/shard_map/ppermute | solution.py:263
  89.2 16.3 %all-to-all-start.2 = ((f32[16,1,24]{2,1,0:T(1,128)}), f32[16,1,24]{2,1,0:T(1,128)S(1)}, u32[]{:S(2)}, u32[]{:S(2)}) async-start(f32[16,1,24]{2,1,0:T(1,128)} %bitcast.6), calls=%async_computation.2 | async-start | bytes 16384 | tf_op jit(solution)/shard_map/all_to_all | solution.py:246
  105.5 16.4 %collective-permute-start.1 = (bf16[10,128,512]{2,1,0:T(8,128)(2,1)}, bf16[10,128,512]{2,1,0:T(8,128)(2,1)S(1)}, u32[]{:S(2)}, u32[]{:S(2)}) collective-permute-start(bf16[10,128,512]{2,1,0:T(8,128)(2,1)} %get-tuple-element.22), channel_id=1, source_target_pairs={{0,32},{32,0},{1,33},{33,1},{2,34},{34,2},{3,35},{35,3},{4,36},{36... | collective-permute-start | bytes 3932168 | tf_op jit(solution)/shard_map/ppermute | solution.py:263
  117.1 10.6 %all-to-all-start.4 = ((f32[16,3,128]{2,1,0:T(4,128)}), f32[16,3,128]{2,1,0:T(4,128)S(1)}, u32[]{:S(2)}, u32[]{:S(2)}) async-start(f32[16,3,128]{2,1,0:T(4,128)} %broadcast_in_dim.16), calls=%async_computation.4 | async-start | bytes 65536 | tf_op jit(solution)/shard_map/all_to_all | solution.py:246
  121.9 5.8 %copy-start = (s32[32,8]{0,1:T(8,128)S(1)}, s32[32,8]{0,1:T(8,128)}, u32[]{:S(2)}) copy-start(s32[32,8]{0,1:T(8,128)} %param.6) | copy-start | bytes 3076
  121.9 5.8 %copy-start.1 = (f32[32,8]{0,1:T(8,128)S(1)}, f32[32,8]{0,1:T(8,128)}, u32[]{:S(2)}) copy-start(f32[32,8]{0,1:T(8,128)} %param.7) | copy-start | bytes 3076

commit v4 on v3

--- a/solution.py
+++ b/solution.py
@@ -99,7 +99,7 @@
 
 
 def values_kernel(
-    far, disp_ref, keep_ref, other_ref, mine_ref, theirs_ref, gate_ref, weight, done
+    disp_ref, keep_ref, other_ref, mine_ref, theirs_ref, gate_ref, weight, done
 ):
     blocks, share, slots = disp_ref.shape
     units = mine_ref.shape[0]
@@ -126,19 +126,18 @@
     mine_ref[...] = values[:units]
     theirs_ref[...] = values[units:]
 
-    near, width = gate_ref.shape
-    member = lax.broadcasted_iota(jnp.int32, (near, slots), 1)
-    owner = lax.broadcasted_iota(jnp.int32, (near, slots), 0)
-    spread = jnp.where(member % near == owner, terms, 0.0)
-    slot = lax.broadcasted_iota(jnp.int32, (slots, width), 0) // near
-    column = lax.broadcasted_iota(jnp.int32, (slots, width), 1)
-    fold = (slot % far) * (width // far) + slot // far == column
-    gate_ref[...] = jnp.dot(
-        spread,
-        fold.astype(F32),
-        preferred_element_type=F32,
-        precision=lax.Precision.HIGHEST,
-    )
+    lines = [terms[:, i : i + LANES] for i in range(0, slots, LANES)]
+    gate_ref[...] = jnp.broadcast_to(jnp.concatenate(lines, axis=0), gate_ref.shape)
+
+
+def sum_kernel(parts_ref, out_ref):
+    sources, capacity = out_ref.shape
+    terms = jnp.sum(parts_ref[...], axis=0)
+    rows = []
+    for c in range(capacity):
+        line, lane = divmod(c * sources, LANES)
+        rows.append(terms[line : line + 1, lane : lane + sources])
+    out_ref[...] = jnp.concatenate(rows, axis=0).T
 
 
 def down_kernel(
@@ -196,20 +195,13 @@
         ).astype(BF16)
 
 
-def gate_kernel(near, capacity, parts_ref, routes_ref, gates_ref, out_ref):
-    experts = parts_ref.shape[1] * LANES // capacity
+def gate_kernel(terms_ref, routes_ref, gates_ref, out_ref):
+    experts, capacity = terms_ref.shape
     named, present, before = ranks(routes_ref[...], experts)
-    terms = jnp.sum(parts_ref[...], axis=0)
     matched = jnp.zeros(present.shape, F32)
     for c in range(capacity):
-        pieces = []
-        for far in range(experts // near):
-            line, lane = divmod((far * capacity + c) * near, LANES)
-            pieces.append(terms[line : line + 1, lane : lane + near])
-        row = jnp.concatenate(pieces, axis=1)
-        spread = jnp.broadcast_to(row, (8, experts)).T[:, :1]
         here = jnp.logical_and(present, before == c)
-        matched = jnp.where(here, spread, matched)
+        matched = jnp.where(here, terms_ref[:, c : c + 1], matched)
     total = [jnp.sum(jnp.where(n, matched, 0.0), axis=0, keepdims=True) for n in named]
     out_ref[...] = jnp.concatenate(total, axis=0) / gates_ref[...]
 
@@ -247,8 +239,7 @@
 
 
 def on_device(grad_out, routes, gates, hidden, w_down):
-    near, far = lax.axis_size("near"), lax.axis_size("far")
-    experts, chips = near * far, lax.axis_size("chip")
+    experts, chips = lax.axis_size("expert"), lax.axis_size("chip")
     _, slots, units = hidden.shape
     width = w_down.shape[2]
     capacity = slots // experts
@@ -269,7 +260,7 @@
         out_specs=whole(),
         name="pack",
     )(grad_out, routes, gates)
-    arrived = swap_all(packed, ("far", "near"))
+    arrived = swap_all(packed, "expert")
 
     half = bf16((chips + 1, units, padded))
     keep, send, order = pl.pallas_call(
@@ -299,11 +290,11 @@
 
     flops = 2 * slots * units * width
     mine, theirs, terms = pl.pallas_call(
-        functools.partial(values_kernel, far),
+        values_kernel,
         out_shape=(
             f32((units, slots)),
             f32((units, slots)),
-            jax.ShapeDtypeStruct((near, far * capacity), F32),
+            jax.ShapeDtypeStruct((2 * chips, slots // LANES, LANES), F32),
         ),
         in_specs=[whole(), stays(), stays()],
         out_specs=(whole(),) * 3,
@@ -315,7 +306,7 @@
         cost_estimate=cost(flops, slots * width + 2 * units * width),
         name="values",
     )(dispatched, keep, other)
-    returned = swap_all(terms, "near")
+    parts = swap_all(terms, ("chip", "core"))
     theirs = in_hbm(theirs)
 
     last = pl.BlockSpec((1, units, padded), lambda i: (chips, 0, 0))
@@ -333,7 +324,7 @@
         cost_estimate=cost(flops, slots * width + 2 * units * width),
         name="down",
     )(dispatched, keep, other, theirs)
-    returned, beside = lax.optimization_barrier((returned, beside))
+    parts, beside = lax.optimization_barrier((parts, beside))
     got = in_vmem(to_other_core(beside))
     down, mine = in_hbm(down), in_hbm(mine)
 
@@ -363,36 +354,40 @@
         name="finish",
     )(core, down, got, mine, order)
 
-    returned = returned.reshape(near, far, capacity).transpose(1, 2, 0)
-    returned = swap_all(returned.reshape(far, near * capacity), "far")
-    flat = returned.reshape(1, slots // LANES, LANES)
-    flat = jnp.broadcast_to(flat, (2 * chips, *flat.shape[1:]))
-    everyone = swap_all(flat, ("chip", "core"))
-    everyone, _ = lax.optimization_barrier((everyone, d_hidden))
+    sums = pl.pallas_call(
+        sum_kernel,
+        out_shape=jax.ShapeDtypeStruct((experts, capacity), F32),
+        in_specs=[whole()],
+        out_specs=whole(),
+        compiler_params=limit(4),
+        name="sum",
+    )(parts)
+    returned = swap_all(sums, "expert")
+    returned, _ = lax.optimization_barrier((returned, d_hidden))
     d_gate = pl.pallas_call(
-        functools.partial(gate_kernel, near, capacity),
+        gate_kernel,
         out_shape=jax.ShapeDtypeStruct(gates.shape, F32),
         in_specs=[whole()] * 3,
         out_specs=whole(),
         compiler_params=limit(4),
         name="match",
-    )(everyone, routes, gates)
+    )(returned, routes, gates)
     return (d_hidden[None], d_down[None], d_gate.T)
 
 
 def solution(mesh):
     parts, experts = mesh.devices.shape
-    devices = mesh.devices.reshape(parts // 2, 2, 2, experts // 2)
-    finer = Mesh(devices, ("chip", "core", "far", "near"))
-    dp, expert = ("chip", "core"), ("far", "near")
+    devices = mesh.devices.reshape(parts // 2, 2, experts)
+    finer = Mesh(devices, ("chip", "core", "expert"))
+    dp = ("chip", "core")
     in_specs = (
-        P(expert, dp),
-        P(expert, None),
-        P(expert, None),
-        P(expert, None, dp),
-        P(expert, dp, None),
+        P("expert", dp),
+        P("expert", None),
+        P("expert", None),
+        P("expert", None, dp),
+        P("expert", dp, None),
     )
-    out_specs = (P(expert, None, dp), P(expert, dp, None), P(expert, None))
+    out_specs = (P("expert", None, dp), P("expert", dp, None), P("expert", None))
     return jax.shard_map(
         on_device, mesh=finer, in_specs=in_specs, out_specs=out_specs, check_vma=False
     )

time: 129 us -> 124 us (0.961)
  blocking collectives: 49.6 us -> 43.2 us
  waiting for transfers between devices: 33 us -> 35.5 us
    all_to_all x2 -> x1, blocking collectives: 49.6 us -> 43.2 us  [swap_all(): return lax.all_to_all(x, axis, split_axis=0, concat_axis=0, tiled=True)]
    all_to_all x3, waiting for transfers between devices: 30.2 us -> 32.7 us  [swap_all(): return lax.all_to_all(x, axis, split_axis=0, concat_axis=0, tiled=True)]
    ppermute x2, starting transfers between devices: 9.46 us -> 7.58 us  [to_other_core(): return lax.ppermute(x, 'core', [(0, 1), (1, 0)])]
    pallas_call x2 -> x3, Pallas kernels: 4.84 us -> 5.24 us  [the longest x1 3.71 us: on_device(): pl.pallas_call(values_kernel, out_shape=(f32((units, slots)), f32((units,...]
  transfers between devices with their start and end apart: 5 -> 5, of which waited for: 4 -> 4; matrix products, arithmetic and copies ran while one was open for 1% -> 0% of each run, Pallas kernels for 9% -> 10%
where the time goes in v4:
time: 124 us; the launch traced here: 123 us
  blocking collectives  43.2 us (35%)
  waiting for transfers between devices  35.5 us (29%)
  starting transfers between devices  22.5 us (18%)
  Pallas kernels  21.2 us (17%)
    all_to_all x1, blocking collectives, swap_all(): return lax.all_to_all(x, axis, split_axis=0, concat_axis=0, tiled=True)  43.2 us
    all_to_all x3, waiting for transfers between devices, swap_all(): return lax.all_to_all(x, axis, split_axis=0, concat_axis=0, tiled=True)  32.7 us
    all_to_all x3, starting transfers between devices, swap_all(): return lax.all_to_all(x, axis, split_axis=0, concat_axis=0, tiled=True)  14.9 us
    ppermute x2, starting transfers between devices, to_other_core(): return lax.ppermute(x, 'core', [(0, 1), (1, 0)])  7.58 us
    pallas_call x1, Pallas kernels, on_device(): pl.pallas_call(finish_kernel, grid=(steps,), out_shape=(jax.ShapeDtypeStr...  4.29 us
    pallas_call x1, Pallas kernels, on_device(): pl.pallas_call(functools.partial(split_kernel, experts), out_shape=(half,...  3.87 us
    pallas_call x1, Pallas kernels, on_device(): pl.pallas_call(values_kernel, out_shape=(f32((units, slots)), f32((units,...  3.71 us
    pallas_call x1, Pallas kernels, on_device(): pl.pallas_call(down_kernel, grid=(1,), out_shape=(bf16((chips, units, pad...  3.7 us
  transfers between devices with their start and end apart: 5, of which 4 were waited for; matrix products, arithmetic and copies ran while one was open for 0% of the time, Pallas kernels for 10%

profile of v4, /device:TPU:1, one launch (start us, length us, event | category | flops | bytes accessed | tf_op | source)
XLA Modules:
  0.0 123.0 jit_solution(5866898639743772730)
XLA Ops:
  0.6 2.0 %pack.1 = bf16[32,2,2688]{2,1,0:T(2,128)(2,1)} custom-call(bf16[32,448]{1,0:T(8,128)(2,1)} %grad_ref.1, s32[8,32]{1,0:T(8,128)} %bitcast.13, f32[8,32]{1,0:T(8,128)} %bitcast.15), custom_call_target="tpu_custom_call" | custom-call | tf_op jit(solution)/shard_map/pack/pallas_call | solution.py:256
  2.6 43.2 %all_to_all.27.in_ref = bf16[32,2,2688]{2,1,0:T(2,128)(2,1)S(1)} all-to-all(bf16[32,2,2688]{2,1,0:T(2,128)(2,1)} %pack.1), channel_id=1, replica_groups=mesh['chip'=8,'core'=2,'expert'=32] {'expert'}, dimensions={0} | all-to-all | bytes 688128 | tf_op jit(solution)/shard_map/all_to_all | solution.py:238
  45.8 2.1 %unpack.1 = bf16[8,448,384]{2,1,0:T(8,128)(2,1)} custom-call(bf16[32,2,2688]{2,1,0:T(2,128)(2,1)S(1)} %all_to_all.27.in_ref), custom_call_target="tpu_custom_call" | custom-call | tf_op jit(solution)/shard_map/unpack/pallas_call | solution.py:277
  47.9 4.2 %all-to-all-start.1 = ((bf16[8,448,384]{2,1,0:T(8,128)(2,1)}), bf16[8,448,384]{2,1,0:T(8,128)(2,1)S(1)}, u32[]{:S(2)}, u32[]{:S(2)}) async-start(bf16[8,448,384]{2,1,0:T(8,128)(2,1)} %unpack.1), calls=%async_computation.1 | async-start | bytes 5505024 | tf_op jit(solution)/shard_map/all_to_all | solution.py:238
  52.1 3.9 %split.1 = (bf16[9,128,512]{2,1,0:T(8,128)(2,1)}, bf16[9,128,512]{2,1,0:T(8,128)(2,1)}, bf16[384,384]{1,0:T(8,128)(2,1)}) custom-call(s32[1]{0:T(128)} %bitcast.core_ref, bf16[128,7168]{1,0:T(8,128)(2,1)} %bitcast.17, bf16[384,128]{1,0:T(8,128)(2,1)} %bitcast.18), custom_call_target="tpu_custom_call" | custom-call | flops 37748736 | bytes 3670016 | tf_op jit(solution)/shard_map/split/pallas_call | solution.py:266
  56.0 5.3 %collective-permute-start = (bf16[9,128,512]{2,1,0:T(8,128)(2,1)}, bf16[9,128,512]{2,1,0:T(8,128)(2,1)}, u32[]{:S(2)}, u32[]{:S(2)}) collective-permute-start(bf16[9,128,512]{2,1,0:T(8,128)(2,1)} %get-tuple-element.17), channel_id=1, source_target_pairs={{0,32},{32,0},{1,33},{33,1},{2,34},{34,2},{3,35},{35,3},{4,36},{36... | collective-permute-start | bytes 3538952 | tf_op jit(solution)/shard_map/ppermute | solution.py:254
  61.3 2.8 %collective-permute-done.other_ref.other_hidden_ref = bf16[9,128,512]{2,1,0:T(8,128)(2,1)} collective-permute-done((bf16[9,128,512]{2,1,0:T(8,128)(2,1)}, bf16[9,128,512]{2,1,0:T(8,128)(2,1)}, u32[]{:S(2)}, u32[]{:S(2)}) %collective-permute-start) | collective-permute-done | bytes 1179680 | tf_op jit(solution)/shard_map/ppermute | solution.py:254
  64.1 21.2 %all-to-all-done.1.disp_ref = bf16[8,448,384]{2,1,0:T(8,128)(2,1)S(1)} async-done(((bf16[8,448,384]{2,1,0:T(8,128)(2,1)}), bf16[8,448,384]{2,1,0:T(8,128)(2,1)S(1)}, u32[]{:S(2)}, u32[]{:S(2)}) %all-to-all-start.1) | async-done | bytes 2752544 | tf_op jit(solution)/shard_map/all_to_all | solution.py:238
  85.3 3.7 %values.1 = (f32[128,384]{1,0:T(8,128)}, f32[128,384]{1,0:T(8,128)}, f32[16,3,128]{2,1,0:T(4,128)}) custom-call(bf16[8,448,384]{2,1,0:T(8,128)(2,1)S(1)} %all-to-all-done.1.disp_ref, bf16[9,128,512]{2,1,0:T(8,128)(2,1)} %get-tuple-element.16.keep_ref.keep_hidden_ref, bf16[9,128,512]{2,1,0:T(8,128)(2,1)} %collective-permute-done.other_ref.other_hidden_ref), custom_call_target="tpu_custom_call" | custom-call | flops 704643072 | bytes 4587520 | tf_op jit(solution)/shard_map/values/pallas_call | solution.py:292
  89.0 4.5 %all-to-all-start.2 = ((f32[16,3,128]{2,1,0:T(4,128)}), f32[16,3,128]{2,1,0:T(4,128)S(1)}, u32[]{:S(2)}, u32[]{:S(2)}) async-start(f32[16,3,128]{2,1,0:T(4,128)} %get-tuple-element.20), calls=%async_computation.2 | async-start | bytes 65536 | tf_op jit(solution)/shard_map/all_to_all | solution.py:238
  93.5 3.7 %down.1 = (bf16[8,128,512]{2,1,0:T(8,128)(2,1)}, bf16[10,128,512]{2,1,0:T(8,128)(2,1)}) custom-call(bf16[8,448,384]{2,1,0:T(8,128)(2,1)S(1)} %all-to-all-done.1.disp_ref, bf16[9,128,512]{2,1,0:T(8,128)(2,1)} %get-tuple-element.16.keep_ref.keep_hidden_ref, bf16[9,128,512]{2,1,0:T(8,128)(2,1)} %collective-permute-done.other_ref.other_hidden_ref, ...), custom_call_target="tpu_custom_call" | custom-call | flops 704643072 | bytes 4587520 | tf_op jit(solution)/shard_map/down/pallas_call | solution.py:314
  97.2 2.1 %all-to-all-done.2.parts_ref = f32[16,3,128]{2,1,0:T(4,128)S(1)} async-done(((f32[16,3,128]{2,1,0:T(4,128)}), f32[16,3,128]{2,1,0:T(4,128)S(1)}, u32[]{:S(2)}, u32[]{:S(2)}) %all-to-all-start.2) | async-done | bytes 24608 | tf_op jit(solution)/shard_map/all_to_all | solution.py:238
  99.3 2.3 %collective-permute-start.1 = (bf16[10,128,512]{2,1,0:T(8,128)(2,1)}, bf16[10,128,512]{2,1,0:T(8,128)(2,1)S(1)}, u32[]{:S(2)}, u32[]{:S(2)}) collective-permute-start(bf16[10,128,512]{2,1,0:T(8,128)(2,1)} %get-tuple-element.22), channel_id=1, source_target_pairs={{0,32},{32,0},{1,33},{33,1},{2,34},{34,2},{3,35},{35,3},{4,36},{36... | collective-permute-start | bytes 3932168 | tf_op jit(solution)/shard_map/ppermute | solution.py:254
  101.6 0.8 sum.1
  102.4 6.1 %all-to-all-start.3 = ((f32[32,1,12]{2,1,0:T(1,128)}), f32[32,1,12]{2,1,0:T(1,128)S(1)}, u32[]{:S(2)}, u32[]{:S(2)}) async-start(f32[32,1,12]{2,1,0:T(1,128)} %bitcast.8), calls=%async_computation.3 | async-start | bytes 32768 | tf_op jit(solution)/shard_map/all_to_all | solution.py:238
  108.5 0.0 collective-permute-done.1.got_ref
  108.5 0.0 copy-start
  108.5 0.0 copy-start.1
  108.5 4.3 %finish.1 = (bf16[128,7168]{1,0:T(8,128)(2,1)}, bf16[384,128]{1,0:T(8,128)(2,1)}) custom-call(s32[1]{0:T(128)} %bitcast.core_ref, bf16[8,128,512]{2,1,0:T(8,128)(2,1)} %get-tuple-element.19.mine_ref, bf16[10,128,512]{2,1,0:T(8,128)(2,1)S(1)} %collective-permute-done.1.got_ref, f32[128,384]{1,0:T(8,128)} %get-tuple-element.23.values_ref, ...), custom_call_target="tpu_custom_call" | custom-call | flops 37748736 | bytes 3670016 | tf_op jit(solution)/shard_map/finish/pallas_call | solution.py:334
  112.8 9.4 %all-to-all-done.3 = f32[32,1,12]{2,1,0:T(1,128)S(1)} async-done(((f32[32,1,12]{2,1,0:T(1,128)}), f32[32,1,12]{2,1,0:T(1,128)S(1)}, u32[]{:S(2)}, u32[]{:S(2)}) %all-to-all-start.3) | async-done | bytes 1568 | tf_op jit(solution)/shard_map/all_to_all | solution.py:238
  122.2 0.0 copy-done
  122.2 0.0 copy-done.1
  122.2 0.8 match.1
Async XLA Ops:
  47.9 37.4 %all-to-all-start.1 = ((bf16[8,448,384]{2,1,0:T(8,128)(2,1)}), bf16[8,448,384]{2,1,0:T(8,128)(2,1)S(1)}, u32[]{:S(2)}, u32[]{:S(2)}) async-start(bf16[8,448,384]{2,1,0:T(8,128)(2,1)} %unpack.1), calls=%async_computation.1 | async-start | bytes 5505024 | tf_op jit(solution)/shard_map/all_to_all | solution.py:238
  56.0 8.1 %collective-permute-start = (bf16[9,128,512]{2,1,0:T(8,128)(2,1)}, bf16[9,128,512]{2,1,0:T(8,128)(2,1)}, u32[]{:S(2)}, u32[]{:S(2)}) collective-permute-start(bf16[9,128,512]{2,1,0:T(8,128)(2,1)} %get-tuple-element.17), channel_id=1, source_target_pairs={{0,32},{32,0},{1,33},{33,1},{2,34},{34,2},{3,35},{35,3},{4,36},{36... | collective-permute-start | bytes 3538952 | tf_op jit(solution)/shard_map/ppermute | solution.py:254
  89.0 10.3 %all-to-all-start.2 = ((f32[16,3,128]{2,1,0:T(4,128)}), f32[16,3,128]{2,1,0:T(4,128)S(1)}, u32[]{:S(2)}, u32[]{:S(2)}) async-start(f32[16,3,128]{2,1,0:T(4,128)} %get-tuple-element.20), calls=%async_computation.2 | async-start | bytes 65536 | tf_op jit(solution)/shard_map/all_to_all | solution.py:238
  99.3 9.2 %collective-permute-start.1 = (bf16[10,128,512]{2,1,0:T(8,128)(2,1)}, bf16[10,128,512]{2,1,0:T(8,128)(2,1)S(1)}, u32[]{:S(2)}, u32[]{:S(2)}) collective-permute-start(bf16[10,128,512]{2,1,0:T(8,128)(2,1)} %get-tuple-element.22), channel_id=1, source_target_pairs={{0,32},{32,0},{1,33},{33,1},{2,34},{34,2},{3,35},{35,3},{4,36},{36... | collective-permute-start | bytes 3932168 | tf_op jit(solution)/shard_map/ppermute | solution.py:254
  102.4 19.8 %all-to-all-start.3 = ((f32[32,1,12]{2,1,0:T(1,128)}), f32[32,1,12]{2,1,0:T(1,128)S(1)}, u32[]{:S(2)}, u32[]{:S(2)}) async-start(f32[32,1,12]{2,1,0:T(1,128)} %bitcast.8), calls=%async_computation.3 | async-start | bytes 32768 | tf_op jit(solution)/shard_map/all_to_all | solution.py:238
  108.5 13.7 %copy-start = (s32[32,8]{0,1:T(8,128)S(1)}, s32[32,8]{0,1:T(8,128)}, u32[]{:S(2)}) copy-start(s32[32,8]{0,1:T(8,128)} %param.6) | copy-start | bytes 3076
  108.5 13.7 %copy-start.1 = (f32[32,8]{0,1:T(8,128)S(1)}, f32[32,8]{0,1:T(8,128)}, u32[]{:S(2)}) copy-start(f32[32,8]{0,1:T(8,128)} %param.7) | copy-start | bytes 3076

commit v5 on v4

v5 whole, which is shorter than its diff:
```python
import functools

import jax
import jax.numpy as jnp
from jax import lax
from jax.experimental import pallas as pl
from jax.experimental.pallas import tpu as pltpu
from jax.sharding import Mesh, PartitionSpec as P

F32 = jnp.float32
BF16 = jnp.bfloat16
LANES = 128


def ranks(routes, experts):
    top, tokens = routes.shape
    ids = lax.broadcasted_iota(jnp.int32, (experts, tokens), 0)
    named = [routes[k : k + 1, :] == ids for k in range(top)]
    present = functools.reduce(jnp.logical_or, named)
    rows = lax.broadcasted_iota(jnp.int32, (tokens, tokens), 0)
    columns = lax.broadcasted_iota(jnp.int32, (tokens, tokens), 1)
    earlier = (rows < columns).astype(F32)
    before = jnp.dot(present.astype(F32), earlier, preferred_element_type=F32)
    return named, present, before


def pack_kernel(grad_ref, routes_ref, gates_ref, out_ref):
    experts, lines, length = out_ref.shape
    grad = grad_ref[...]
    fitting = length // grad.shape[1]
    named, present, before = ranks(routes_ref[...], experts)
    gates = gates_ref[...]
    gate = jnp.zeros(present.shape, F32)
    for k, here in enumerate(named):
        gate = jnp.where(here, gates[k : k + 1, :], gate)

    def slot(c):
        placed = jnp.logical_and(present, before == c).astype(F32)
        row_gate = jnp.sum(placed * gate, axis=1, keepdims=True)
        return row_gate * jnp.dot(
            placed.astype(BF16), grad, preferred_element_type=F32
        )

    for line in range(lines):
        rows = [slot(fitting * line + i) for i in range(fitting)]
        out_ref[:, line, :] = jnp.concatenate(rows, axis=1).astype(BF16)


def unpack_kernel(in_ref, out_ref, flipped, done):
    sources, lines, length = in_ref.shape
    share, slots = flipped.shape
    fitting = length // share
    rows = [in_ref[:, line, :].astype(F32) for line in range(lines)]
    group = LANES // sources
    for g in range(slots // LANES):
        parts = []
        for c in range(g * group, (g + 1) * group):
            start = share * (c % fitting)
            parts.append(rows[c // fitting][:, start : start + share])
        block = jnp.concatenate(parts, axis=0)
        flipped[:, LANES * g : LANES * (g + 1)] = block.T.astype(BF16)
    copies = [
        pltpu.make_async_copy(flipped, out_ref.at[i], done.at[i])
        for i in range(out_ref.shape[0])
    ]
    for copy in copies:
        copy.start()
    for copy in copies:
        copy.wait()


def cases(place_ref, body):
    for far in range(2):
        for core in range(2):
            here = jnp.logical_and(place_ref[0] == far, place_ref[1] == core)
            pl.when(here)(functools.partial(body, far, core))


def columns(far, core, y, blocks, share):
    start = ((far * blocks + y) * 2 + core) * share
    return slice(start, start + share)


def split_kernel(sources, place_ref, weight_ref, hidden_ref, keep_ref, far_ref, order_ref):
    slots = hidden_ref.shape[0]
    all_mine = keep_ref.shape[1] - slots
    blocks = 4
    share = all_mine // (2 * blocks)
    capacity = slots // sources
    rows = lax.broadcasted_iota(jnp.int32, (slots, slots), 0)
    cols = lax.broadcasted_iota(jnp.int32, (slots, slots), 1)
    matches = (rows % capacity) * sources + rows // capacity == cols
    order = matches.astype(F32).astype(BF16)
    order_ref[...] = order
    flipped = lax.dot_general(
        hidden_ref[...], order, (((0,), (0,)), ((), ())), preferred_element_type=F32
    ).astype(BF16)

    def store(far, core):
        for ref, f in ((keep_ref, far), (far_ref, 1 - far)):
            for half, c in enumerate((core, 1 - core)):
                pieces = [
                    weight_ref[:, columns(f, c, y, blocks, share)]
                    for y in range(blocks)
                ]
                start = half * blocks * share
                ref[:, start : start + blocks * share] = jnp.concatenate(
                    pieces, axis=1
                )
            ref[:, all_mine:] = flipped

    cases(place_ref, store)


def product(half, disp_ref, keep_ref, far_ref, weight, done):
    blocks, share, slots = disp_ref.shape
    units, wide = keep_ref.shape[0], 2 * share
    copies = []
    for step in range(blocks // 2):
        here = pl.ds((half * blocks // 2 + step) * wide, wide)
        copies.append(
            [
                pltpu.make_async_copy(
                    ref.at[:, here], weight.at[step, k], done.at[step, k]
                )
                for k, ref in enumerate((keep_ref, far_ref))
            ]
        )
    for now in copies:
        for copy in now:
            copy.start()
    values = jnp.zeros((2 * units, slots), F32)
    for step, now in enumerate(copies):
        for copy in now:
            copy.wait()
        rows = weight[step].reshape(2 * units, wide)
        block = disp_ref[2 * step : 2 * step + 2].reshape(wide, slots)
        values += jnp.dot(rows, block, preferred_element_type=F32)
    return values


def first_kernel(disp_ref, keep_ref, far_ref, values_ref, weight, done):
    values_ref[...] = product(0, disp_ref, keep_ref, far_ref, weight, done)


def values_kernel(
    disp_ref,
    keep_ref,
    far_ref,
    first_ref,
    mine_ref,
    theirs_ref,
    gate_ref,
    weight,
    done,
    hidden,
    ready,
):
    units, slots = mine_ref.shape
    after = pl.ds(keep_ref.shape[1] - slots, slots)
    copies = [
        pltpu.make_async_copy(ref.at[:, after], hidden.at[k], ready.at[k])
        for k, ref in enumerate((keep_ref, far_ref))
    ]
    for copy in copies:
        copy.start()
    values = first_ref[...] + product(1, disp_ref, keep_ref, far_ref, weight, done)
    for copy in copies:
        copy.wait()
    left = hidden[...].reshape(2 * units, slots).astype(F32)
    terms = jnp.sum(left * values, axis=0, keepdims=True)
    mine_ref[...] = values[:units]
    theirs_ref[...] = values[units:]
    lines = [terms[:, i : i + LANES] for i in range(0, slots, LANES)]
    gate_ref[...] = jnp.broadcast_to(jnp.concatenate(lines, axis=0), gate_ref.shape)


def down_kernel(
    own_ref, other_ref, keep_ref, far_ref, values_ref, mine_ref, send_ref, hidden, ready
):
    blocks, share, slots = own_ref.shape
    units, wide = hidden.shape[1], 2 * share
    all_mine = mine_ref.shape[1]
    after = pl.ds(all_mine, slots)
    copies = [
        pltpu.make_async_copy(ref.at[:, after], hidden.at[k], ready.at[k])
        for k, ref in enumerate((keep_ref, far_ref))
    ]
    for copy in copies:
        copy.start()
    for copy in copies:
        copy.wait()
    left = hidden[...].reshape(2 * units, slots)
    for half, ref in enumerate((own_ref, other_ref)):
        for step in range(blocks // 2):
            block = ref[2 * step : 2 * step + 2].reshape(wide, slots)
            down = lax.dot_general(
                left, block, (((1,), (1,)), ((), ())), preferred_element_type=F32
            ).astype(BF16)
            start = (half * blocks // 2 + step) * wide
            mine_ref[:, start : start + wide] = down[:units]
            send_ref[:, start : start + wide] = down[units:]
    values = values_ref[...]
    high = values.astype(BF16)
    send_ref[:, all_mine : all_mine + slots] = high
    send_ref[:, all_mine + slots :] = (values - high.astype(F32)).astype(BF16)


def finish_kernel(
    place_ref, mine_ref, got_ref, values_ref, order_ref, down_ref, dhid_ref
):
    slots = values_ref.shape[1]
    all_mine = mine_ref.shape[1]
    blocks = 4
    share = all_mine // (2 * blocks)

    def store(far, core):
        for f in range(2):
            ref = mine_ref if f == far else got_ref
            for y in range(blocks):
                pair = []
                for c in range(2):
                    start = share * ((0 if c == core else blocks) + y)
                    pair.append(ref[:, start : start + share])
                start = 2 * share * (f * blocks + y)
                down_ref[:, start : start + 2 * share] = jnp.concatenate(pair, axis=1)

    cases(place_ref, store)
    high = got_ref[:, all_mine : all_mine + slots].astype(F32)
    low = got_ref[:, all_mine + slots :].astype(F32)
    flipped = (values_ref[...] + (high + low)).T.astype(BF16)
    dhid_ref[...] = jnp.dot(
        order_ref[...], flipped, preferred_element_type=F32
    ).astype(BF16)


def sum_kernel(parts_ref, out_ref):
    sources, capacity = out_ref.shape
    terms = jnp.sum(parts_ref[...], axis=0)
    rows = []
    for c in range(capacity):
        line, lane = divmod(c * sources, LANES)
        rows.append(terms[line : line + 1, lane : lane + sources])
    out_ref[...] = jnp.concatenate(rows, axis=0).T


def gate_kernel(terms_ref, routes_ref, gates_ref, out_ref):
    experts, capacity = terms_ref.shape
    named, present, before = ranks(routes_ref[...], experts)
    matched = jnp.zeros(present.shape, F32)
    for c in range(capacity):
        here = jnp.logical_and(present, before == c)
        matched = jnp.where(here, terms_ref[:, c : c + 1], matched)
    total = [jnp.sum(jnp.where(n, matched, 0.0), axis=0, keepdims=True) for n in named]
    out_ref[...] = jnp.concatenate(total, axis=0) / gates_ref[...]


def whole():
    return pl.BlockSpec(memory_space=pltpu.VMEM)


def scalar():
    return pl.BlockSpec(memory_space=pltpu.SMEM)


def stays():
    return pl.BlockSpec(memory_space=pltpu.HBM)


def in_hbm(x):
    return pltpu.with_memory_space_constraint(x, pltpu.HBM)


def in_vmem(x):
    return pltpu.with_memory_space_constraint(x, pltpu.VMEM)


def limit(mib):
    return pltpu.CompilerParams(vmem_limit_bytes=mib * 2**20)


def cost(flops, moved):
    return pl.CostEstimate(flops=flops, bytes_accessed=moved, transcendentals=0)


def swap_all(x, axis):
    return lax.all_to_all(x, axis, split_axis=0, concat_axis=0, tiled=True)


def on_device(grad_out, routes, gates, hidden, w_down):
    experts, rows_y = lax.axis_size("expert"), lax.axis_size("y")
    _, slots, units = hidden.shape
    width = w_down.shape[2]
    capacity = slots // experts
    share = grad_out.shape[1]
    mine = rows_y * share
    place = jnp.stack([lax.axis_index("x"), lax.axis_index("core")]).astype(jnp.int32)
    routes, gates = routes.T, gates.T
    bf16 = functools.partial(pltpu.HBM, dtype=BF16)
    f32 = functools.partial(pltpu.HBM, dtype=F32)

    def other(x, axis):
        return lax.ppermute(x, axis, [(0, 1), (1, 0)])

    packed = pl.pallas_call(
        pack_kernel,
        out_shape=jax.ShapeDtypeStruct((experts, 2, capacity * share // 2), BF16),
        in_specs=[whole()] * 3,
        out_specs=whole(),
        name="pack",
    )(grad_out, routes, gates)
    arrived = swap_all(packed, "expert")

    all_mine = 2 * mine
    longer = bf16((units, all_mine + slots))
    keep, to_far, order = pl.pallas_call(
        functools.partial(split_kernel, experts),
        out_shape=(longer, longer, bf16((slots, slots))),
        in_specs=[scalar(), whole(), whole()],
        out_specs=(whole(),) * 3,
        cost_estimate=cost(2 * units * slots * slots, 2 * 2 * units * width),
        name="split",
    )(place, w_down[0], hidden[0])
    from_far = other(to_far, "x")
    arrived, from_far = lax.optimization_barrier((arrived, from_far))

    copies = pl.pallas_call(
        unpack_kernel,
        out_shape=bf16((rows_y, share, slots)),
        in_specs=[whole()],
        out_specs=pl.BlockSpec(memory_space=pl.ANY),
        scratch_shapes=[
            pltpu.VMEM((share, slots), BF16),
            pltpu.SemaphoreType.DMA((rows_y,)),
        ],
        compiler_params=limit(8),
        name="unpack",
    )(arrived)
    dispatched = swap_all(copies, "y")
    from_core = in_vmem(other(dispatched, "core"))
    dispatched = in_vmem(dispatched)

    keep, from_far = in_hbm(keep), in_hbm(from_far)
    flops = 2 * slots * units * width
    scratch = [
        pltpu.VMEM((rows_y // 2, 2, units, 2 * share), BF16),
        pltpu.SemaphoreType.DMA((rows_y // 2, 2)),
    ]
    activations = [
        pltpu.VMEM((2, units, slots), BF16),
        pltpu.SemaphoreType.DMA((2,)),
    ]
    first = pl.pallas_call(
        first_kernel,
        out_shape=f32((2 * units, slots)),
        in_specs=[whole(), stays(), stays()],
        out_specs=whole(),
        scratch_shapes=scratch,
        compiler_params=limit(16),
        cost_estimate=cost(flops // 2, slots * width + units * width),
        name="first",
    )(dispatched, keep, from_far)
    mine_values, theirs, terms = pl.pallas_call(
        values_kernel,
        out_shape=(
            f32((units, slots)),
            f32((units, slots)),
            jax.ShapeDtypeStruct((4 * rows_y, slots // LANES, LANES), F32),
        ),
        in_specs=[whole(), stays(), stays(), whole()],
        out_specs=(whole(),) * 3,
        scratch_shapes=scratch + activations,
        compiler_params=limit(16),
        cost_estimate=cost(flops // 2, slots * width + units * width),
        name="values",
    )(from_core, keep, from_far, in_hbm(first))
    parts = swap_all(terms, ("x", "y", "core"))

    down, back = pl.pallas_call(
        down_kernel,
        out_shape=(bf16((units, all_mine)), bf16((units, all_mine + 2 * slots))),
        in_specs=[whole()] * 2 + [stays()] * 2 + [whole()],
        out_specs=(whole(),) * 2,
        scratch_shapes=activations,
        compiler_params=limit(16),
        cost_estimate=cost(flops, slots * width + 2 * units * width),
        name="down",
    )(dispatched, from_core, keep, from_far, in_hbm(theirs))
    parts, back = lax.optimization_barrier((parts, back))
    got = other(back, "x")

    d_down, d_hidden = pl.pallas_call(
        finish_kernel,
        out_shape=(
            jax.ShapeDtypeStruct((units, width), BF16),
            jax.ShapeDtypeStruct((slots, units), BF16),
        ),
        in_specs=[scalar()] + [whole()] * 4,
        out_specs=(whole(),) * 2,
        compiler_params=limit(16),
        cost_estimate=cost(2 * units * slots * slots, 4 * units * width),
        name="finish",
    )(place, in_hbm(down), in_vmem(got), in_hbm(mine_values), in_hbm(order))

    sums = pl.pallas_call(
        sum_kernel,
        out_shape=jax.ShapeDtypeStruct((experts, capacity), F32),
        in_specs=[whole()],
        out_specs=whole(),
        compiler_params=limit(4),
        name="sum",
    )(parts)
    returned = swap_all(sums, "expert")
    returned, _ = lax.optimization_barrier((returned, d_hidden))
    d_gate = pl.pallas_call(
        gate_kernel,
        out_shape=jax.ShapeDtypeStruct(gates.shape, F32),
        in_specs=[whole()] * 3,
        out_specs=whole(),
        compiler_params=limit(4),
        name="match",
    )(returned, routes, gates)
    return (d_hidden[None], d_down[None], d_gate.T)


def solution(mesh):
    parts, experts = mesh.devices.shape
    devices = mesh.devices.reshape(2, parts // 4, 2, experts)
    finer = Mesh(devices, ("x", "y", "core", "expert"))
    dp = ("x", "y", "core")
    in_specs = (
        P("expert", dp),
        P("expert", None),
        P("expert", None),
        P("expert", None, dp),
        P("expert", dp, None),
    )
    out_specs = (P("expert", None, dp), P("expert", dp, None), P("expert", None))
    return jax.shard_map(
        on_device, mesh=finer, in_specs=in_specs, out_specs=out_specs, check_vma=False
    )
```

time: 124 us -> 129 us (1.040)
  blocking collectives: 43.2 us -> 20.8 us
  starting transfers between devices: 22.5 us -> 44.4 us
  waiting for transfers between devices: 35.5 us -> 39.3 us
  Pallas kernels: 21.2 us -> 22.8 us
    ppermute x2 -> x3, waiting for transfers between devices: 2.8 us -> 37.9 us  [other(): return lax.ppermute(x, axis, [(0, 1), (1, 0)])]
    all_to_all x3, waiting for transfers between devices: 32.7 us -> 1.37 us  [swap_all(): return lax.all_to_all(x, axis, split_axis=0, concat_axis=0, tiled=True)]
    all_to_all x1, blocking collectives: 43.2 us -> 20.8 us  [swap_all(): return lax.all_to_all(x, axis, split_axis=0, concat_axis=0, tiled=True)]
    all_to_all x3, starting transfers between devices: 14.9 us -> 35.1 us  [swap_all(): return lax.all_to_all(x, axis, split_axis=0, concat_axis=0, tiled=True)]
    ppermute x2 -> x3, starting transfers between devices: 7.58 us -> 9.26 us  [other(): return lax.ppermute(x, axis, [(0, 1), (1, 0)])]
    pallas_call x4 -> x5, Pallas kernels: 13.9 us -> 15.4 us  [the longest x1 4.47 us: on_device(): pl.pallas_call(down_kernel, out_shape=(bf16((units, all_mine)), bf16((uni...]
  transfers between devices with their start and end apart: 5 -> 6, of which waited for: 4 -> 3; matrix products, arithmetic and copies ran while one was open for 0% -> 1% of each run, Pallas kernels for 10% -> 11%
where the time goes in v5:
time: 129 us
  starting transfers between devices  44.4 us (34%)
  waiting for transfers between devices  39.3 us (30%)
  Pallas kernels  22.8 us (18%)
  blocking collectives  20.8 us (16%)
    ppermute x3, waiting for transfers between devices, other(): return lax.ppermute(x, axis, [(0, 1), (1, 0)])  37.9 us
    all_to_all x3, starting transfers between devices, swap_all(): return lax.all_to_all(x, axis, split_axis=0, concat_axis=0, tiled=True)  35.1 us
    all_to_all x1, blocking collectives, swap_all(): return lax.all_to_all(x, axis, split_axis=0, concat_axis=0, tiled=True)  20.8 us
    ppermute x3, starting transfers between devices, other(): return lax.ppermute(x, axis, [(0, 1), (1, 0)])  9.26 us
    pallas_call x1, Pallas kernels, on_device(): pl.pallas_call(down_kernel, out_shape=(bf16((units, all_mine)), bf16((uni...  4.47 us
    pallas_call x1, Pallas kernels, on_device(): pl.pallas_call(values_kernel, out_shape=(f32((units, slots)), f32((units,...  3.82 us
    pallas_call x1, Pallas kernels, on_device(): pl.pallas_call(functools.partial(split_kernel, experts), out_shape=(longe...  3.61 us
    pallas_call x1, Pallas kernels, on_device(): pl.pallas_call(finish_kernel, out_shape=(jax.ShapeDtypeStruct((units, wid...  3.03 us
  transfers between devices with their start and end apart: 6, of which 3 were waited for; matrix products, arithmetic and copies ran while one was open for 1% of the time, Pallas kernels for 11%

profile of v5, /device:TPU:1, one launch (start us, length us, event | category | flops | bytes accessed | tf_op | source)
XLA Modules:
  0.0 128.7 jit_solution(14076931160746676414)
XLA Ops:
  0.6 2.0 %pack.1 = bf16[32,2,2688]{2,1,0:T(2,128)(2,1)} custom-call(bf16[32,448]{1,0:T(8,128)(2,1)} %grad_ref.1, s32[8,32]{1,0:T(8,128)} %bitcast.14, f32[8,32]{1,0:T(8,128)} %bitcast.16), custom_call_target="tpu_custom_call" | custom-call | tf_op jit(solution)/shard_map/pack/pallas_call | solution.py:305
  2.6 18.5 %all-to-all-start = ((bf16[32,2,2688]{2,1,0:T(2,128)(2,1)}), bf16[32,2,2688]{2,1,0:T(2,128)(2,1)S(1)}, u32[]{:S(2)}, u32[]{:S(2)}) async-start(bf16[32,2,2688]{2,1,0:T(2,128)(2,1)} %pack.1), calls=%async_computation | async-start | bytes 688128 | tf_op jit(solution)/shard_map/all_to_all | solution.py:287
  21.2 0.6 pad_add_fusion.place_ref
  21.8 3.6 %split.1 = (bf16[128,3968]{1,0:T(8,128)(2,1)}, bf16[128,3968]{1,0:T(8,128)(2,1)}, bf16[384,384]{1,0:T(8,128)(2,1)}) custom-call(s32[2]{0:T(128)} %pad_add_fusion.place_ref, bf16[128,7168]{1,0:T(8,128)(2,1)} %bitcast.18, bf16[384,128]{1,0:T(8,128)(2,1)} %bitcast.19), custom_call_target="tpu_custom_call" | custom-call | flops 37748736 | bytes 3670016 | tf_op jit(solution)/shard_map/split/pallas_call | solution.py:316
  25.4 2.2 %collective-permute-start = (bf16[128,3968]{1,0:T(8,128)(2,1)}, bf16[128,3968]{1,0:T(8,128)(2,1)}, u32[]{:S(2)}, u32[]{:S(2)}) collective-permute-start(bf16[128,3968]{1,0:T(8,128)(2,1)} %get-tuple-element.18), channel_id=1, source_target_pairs={{0,256},{256,0},{1,257},{257,1},{2,258},{258,2},{3,259},{259,3},{4... | collective-permute-start | bytes 3047432 | tf_op jit(solution)/shard_map/ppermute | solution.py:303
  27.6 25.9 %collective-permute-done.far_ref = bf16[128,3968]{1,0:T(8,128)(2,1)} collective-permute-done((bf16[128,3968]{1,0:T(8,128)(2,1)}, bf16[128,3968]{1,0:T(8,128)(2,1)}, u32[]{:S(2)}, u32[]{:S(2)}) %collective-permute-start) | collective-permute-done | bytes 1015840 | tf_op jit(solution)/shard_map/ppermute | solution.py:303
  53.5 0.0 all-to-all-done.in_ref
  53.5 1.6 %unpack.1 = bf16[4,448,384]{2,1,0:T(8,128)(2,1)} custom-call(bf16[32,2,2688]{2,1,0:T(2,128)(2,1)S(1)} %all-to-all-done.in_ref), custom_call_target="tpu_custom_call" | custom-call | tf_op jit(solution)/shard_map/unpack/pallas_call | solution.py:327
  55.1 20.8 %all_to_all.27.disp_ref.own_ref = bf16[4,448,384]{2,1,0:T(8,128)(2,1)S(1)} all-to-all(bf16[4,448,384]{2,1,0:T(8,128)(2,1)} %unpack.1), channel_id=1, replica_groups=mesh['x'=2,'y'=4,'core'=2,'expert'=32] {'y'}, dimensions={0} | all-to-all | bytes 2752512 | tf_op jit(solution)/shard_map/all_to_all | solution.py:287
  75.9 4.8 %collective-permute-start.1 = (bf16[4,448,384]{2,1,0:T(8,128)(2,1)S(1)}, bf16[4,448,384]{2,1,0:T(8,128)(2,1)S(1)}, u32[]{:S(2)}, u32[]{:S(2)}) collective-permute-start(bf16[4,448,384]{2,1,0:T(8,128)(2,1)S(1)} %all_to_all.27.disp_ref.own_ref), channel_id=1, source_target_pairs={{0,32},{32,0},{1,33},{33,1},{2,34},{34,2},{3,35},{35,3},{4,36},{36... | collective-permute-start | bytes 4128776 | tf_op jit(solution)/shard_map/ppermute | solution.py:303
  80.8 2.7 %first.1.first_ref = f32[256,384]{1,0:T(8,128)} custom-call(bf16[4,448,384]{2,1,0:T(8,128)(2,1)S(1)} %all_to_all.27.disp_ref.own_ref, bf16[128,3968]{1,0:T(8,128)(2,1)} %get-tuple-element.20.keep_ref, bf16[128,3968]{1,0:T(8,128)(2,1)} %collective-permute-done.far_ref), custom_call_target="tpu_custom_call" | custom-call | flops 352321536 | bytes 3670016 | tf_op jit(solution)/shard_map/first/pallas_call | solution.py:353
  83.5 0.0 collective-permute-done.1.disp_ref.other_ref
  83.5 3.8 %values.1 = (f32[128,384]{1,0:T(8,128)}, f32[128,384]{1,0:T(8,128)}, f32[16,3,128]{2,1,0:T(4,128)}) custom-call(bf16[4,448,384]{2,1,0:T(8,128)(2,1)S(1)} %collective-permute-done.1.disp_ref.other_ref, bf16[128,3968]{1,0:T(8,128)(2,1)} %get-tuple-element.20.keep_ref, bf16[128,3968]{1,0:T(8,128)(2,1)} %collective-permute-done.far_ref, f32[256,384]{1,0:T(8,128)} %first.1.first_ref), custom_call_target="tpu_custom_call" | custom-call | flops 352321536 | bytes 3670016 | tf_op jit(solution)/shard_map/values/pallas_call | solution.py:363
  87.4 3.6 %all-to-all-start.2 = ((f32[16,3,128]{2,1,0:T(4,128)}), f32[16,3,128]{2,1,0:T(4,128)S(1)}, u32[]{:S(2)}, u32[]{:S(2)}) async-start(f32[16,3,128]{2,1,0:T(4,128)} %get-tuple-element.24), calls=%async_computation.2 | async-start | bytes 65536 | tf_op jit(solution)/shard_map/all_to_all | solution.py:287
  91.0 4.5 %down.1 = (bf16[128,3584]{1,0:T(8,128)(2,1)}, bf16[128,4352]{1,0:T(8,128)(2,1)}) custom-call(bf16[4,448,384]{2,1,0:T(8,128)(2,1)S(1)} %all_to_all.27.disp_ref.own_ref, bf16[4,448,384]{2,1,0:T(8,128)(2,1)S(1)} %collective-permute-done.1.disp_ref.other_ref, bf16[128,3968]{1,0:T(8,128)(2,1)} %get-tuple-element.20.keep_ref, ...), custom_call_target="tpu_custom_call" | custom-call | flops 704643072 | bytes 4587520 | tf_op jit(solution)/shard_map/down/pallas_call | solution.py:379
  95.5 0.0 copy-start
  95.5 0.0 copy-start.1
  95.5 1.4 %all-to-all-done.2.parts_ref = f32[16,3,128]{2,1,0:T(4,128)S(1)} async-done(((f32[16,3,128]{2,1,0:T(4,128)}), f32[16,3,128]{2,1,0:T(4,128)S(1)}, u32[]{:S(2)}, u32[]{:S(2)}) %all-to-all-start.2) | async-done | bytes 24608 | tf_op jit(solution)/shard_map/all_to_all | solution.py:287
  96.9 2.2 %collective-permute-start.2 = (bf16[128,4352]{1,0:T(8,128)(2,1)}, bf16[128,4352]{1,0:T(8,128)(2,1)S(1)}, u32[]{:S(2)}, u32[]{:S(2)}) collective-permute-start(bf16[128,4352]{1,0:T(8,128)(2,1)} %get-tuple-element.26), channel_id=1, source_target_pairs={{0,256},{256,0},{1,257},{257,1},{2,258},{258,2},{3,259},{259,3},{4... | collective-permute-start | bytes 3342344 | tf_op jit(solution)/shard_map/ppermute | solution.py:303
  99.1 0.8 sum.1
  99.9 13.0 %all-to-all-start.3 = ((f32[32,1,12]{2,1,0:T(1,128)}), f32[32,1,12]{2,1,0:T(1,128)S(1)}, u32[]{:S(2)}, u32[]{:S(2)}) async-start(f32[32,1,12]{2,1,0:T(1,128)} %bitcast.9), calls=%async_computation.3 | async-start | bytes 32768 | tf_op jit(solution)/shard_map/all_to_all | solution.py:287
  112.9 12.0 %collective-permute-done.2.got_ref = bf16[128,4352]{1,0:T(8,128)(2,1)S(1)} collective-permute-done((bf16[128,4352]{1,0:T(8,128)(2,1)}, bf16[128,4352]{1,0:T(8,128)(2,1)S(1)}, u32[]{:S(2)}, u32[]{:S(2)}) %collective-permute-start.2) | collective-permute-done | bytes 1114144 | tf_op jit(solution)/shard_map/ppermute | solution.py:303
  124.9 3.0 %finish.1 = (bf16[128,7168]{1,0:T(8,128)(2,1)}, bf16[384,128]{1,0:T(8,128)(2,1)}) custom-call(s32[2]{0:T(128)S(1)} %copy-done.2, bf16[128,3584]{1,0:T(8,128)(2,1)} %get-tuple-element.23.mine_ref, bf16[128,4352]{1,0:T(8,128)(2,1)S(1)} %collective-permute-done.2.got_ref, f32[128,384]{1,0:T(8,128)} %get-tuple-element.27.values_ref, ...), custom_call_target="tpu_custom_call" | custom-call | flops 37748736 | bytes 3670016 | tf_op jit(solution)/shard_map/finish/pallas_call | solution.py:392
  127.9 0.8 match.1
  (5 shorter events, 0.0 us)
Async XLA Ops:
  2.6 50.9 %all-to-all-start = ((bf16[32,2,2688]{2,1,0:T(2,128)(2,1)}), bf16[32,2,2688]{2,1,0:T(2,128)(2,1)S(1)}, u32[]{:S(2)}, u32[]{:S(2)}) async-start(bf16[32,2,2688]{2,1,0:T(2,128)(2,1)} %pack.1), calls=%async_computation | async-start | bytes 688128 | tf_op jit(solution)/shard_map/all_to_all | solution.py:287
  25.4 28.1 %collective-permute-start = (bf16[128,3968]{1,0:T(8,128)(2,1)}, bf16[128,3968]{1,0:T(8,128)(2,1)}, u32[]{:S(2)}, u32[]{:S(2)}) collective-permute-start(bf16[128,3968]{1,0:T(8,128)(2,1)} %get-tuple-element.18), channel_id=1, source_target_pairs={{0,256},{256,0},{1,257},{257,1},{2,258},{258,2},{3,259},{259,3},{4... | collective-permute-start | bytes 3047432 | tf_op jit(solution)/shard_map/ppermute | solution.py:303
  75.9 7.6 %collective-permute-start.1 = (bf16[4,448,384]{2,1,0:T(8,128)(2,1)S(1)}, bf16[4,448,384]{2,1,0:T(8,128)(2,1)S(1)}, u32[]{:S(2)}, u32[]{:S(2)}) collective-permute-start(bf16[4,448,384]{2,1,0:T(8,128)(2,1)S(1)} %all_to_all.27.disp_ref.own_ref), channel_id=1, source_target_pairs={{0,32},{32,0},{1,33},{33,1},{2,34},{34,2},{3,35},{35,3},{4,36},{36... | collective-permute-start | bytes 4128776 | tf_op jit(solution)/shard_map/ppermute | solution.py:303
  87.4 9.5 %all-to-all-start.2 = ((f32[16,3,128]{2,1,0:T(4,128)}), f32[16,3,128]{2,1,0:T(4,128)S(1)}, u32[]{:S(2)}, u32[]{:S(2)}) async-start(f32[16,3,128]{2,1,0:T(4,128)} %get-tuple-element.24), calls=%async_computation.2 | async-start | bytes 65536 | tf_op jit(solution)/shard_map/all_to_all | solution.py:287
  91.0 33.9 %copy-start.2 = (s32[2]{0:T(128)S(1)}, s32[2]{0:T(128)}, u32[]{:S(2)}) copy-start(s32[2]{0:T(128)} %pad_add_fusion.place_ref) | copy-start | bytes 28
  95.5 32.4 %copy-start = (s32[32,8]{0,1:T(8,128)S(1)}, s32[32,8]{0,1:T(8,128)}, u32[]{:S(2)}) copy-start(s32[32,8]{0,1:T(8,128)} %param.6) | copy-start | bytes 3076
  95.5 32.4 %copy-start.1 = (f32[32,8]{0,1:T(8,128)S(1)}, f32[32,8]{0,1:T(8,128)}, u32[]{:S(2)}) copy-start(f32[32,8]{0,1:T(8,128)} %param.7) | copy-start | bytes 3076
  96.9 28.0 %collective-permute-start.2 = (bf16[128,4352]{1,0:T(8,128)(2,1)}, bf16[128,4352]{1,0:T(8,128)(2,1)S(1)}, u32[]{:S(2)}, u32[]{:S(2)}) collective-permute-start(bf16[128,4352]{1,0:T(8,128)(2,1)} %get-tuple-element.26), channel_id=1, source_target_pairs={{0,256},{256,0},{1,257},{257,1},{2,258},{258,2},{3,259},{259,3},{4... | collective-permute-start | bytes 3342344 | tf_op jit(solution)/shard_map/ppermute | solution.py:303
  99.9 28.0 %all-to-all-start.3 = ((f32[32,1,12]{2,1,0:T(1,128)}), f32[32,1,12]{2,1,0:T(1,128)S(1)}, u32[]{:S(2)}, u32[]{:S(2)}) async-start(f32[32,1,12]{2,1,0:T(1,128)} %bitcast.9), calls=%async_computation.3 | async-start | bytes 32768 | tf_op jit(solution)/shard_map/all_to_all | solution.py:287

commit v6 on v5

--- a/solution.py
+++ b/solution.py
@@ -81,7 +81,16 @@
     return slice(start, start + share)
 
 
-def split_kernel(sources, place_ref, weight_ref, hidden_ref, keep_ref, far_ref, order_ref):
+def split_kernel(
+    sources,
+    place_ref,
+    weight_ref,
+    hidden_ref,
+    keep_ref,
+    far_ref,
+    later_ref,
+    order_ref,
+):
     slots = hidden_ref.shape[0]
     all_mine = keep_ref.shape[1] - slots
     blocks = 4
@@ -96,58 +105,31 @@
         hidden_ref[...], order, (((0,), (0,)), ((), ())), preferred_element_type=F32
     ).astype(BF16)
 
+    mine = blocks * share
+
     def store(far, core):
-        for ref, f in ((keep_ref, far), (far_ref, 1 - far)):
-            for half, c in enumerate((core, 1 - core)):
-                pieces = [
-                    weight_ref[:, columns(f, c, y, blocks, share)]
-                    for y in range(blocks)
-                ]
-                start = half * blocks * share
-                ref[:, start : start + blocks * share] = jnp.concatenate(
-                    pieces, axis=1
-                )
-            ref[:, all_mine:] = flipped
+        def part(f, c):
+            pieces = [
+                weight_ref[:, columns(f, c, y, blocks, share)] for y in range(blocks)
+            ]
+            return jnp.concatenate(pieces, axis=1)
+
+        keep_ref[:, :mine] = part(far, core)
+        keep_ref[:, mine:all_mine] = part(far, 1 - core)
+        keep_ref[:, all_mine:] = flipped
+        far_ref[:, :mine] = part(1 - far, core)
+        far_ref[:, mine:] = flipped
+        later_ref[...] = part(1 - far, 1 - core)
 
     cases(place_ref, store)
 
 
-def product(half, disp_ref, keep_ref, far_ref, weight, done):
-    blocks, share, slots = disp_ref.shape
-    units, wide = keep_ref.shape[0], 2 * share
-    copies = []
-    for step in range(blocks // 2):
-        here = pl.ds((half * blocks // 2 + step) * wide, wide)
-        copies.append(
-            [
-                pltpu.make_async_copy(
-                    ref.at[:, here], weight.at[step, k], done.at[step, k]
-                )
-                for k, ref in enumerate((keep_ref, far_ref))
-            ]
-        )
-    for now in copies:
-        for copy in now:
-            copy.start()
-    values = jnp.zeros((2 * units, slots), F32)
-    for step, now in enumerate(copies):
-        for copy in now:
-            copy.wait()
-        rows = weight[step].reshape(2 * units, wide)
-        block = disp_ref[2 * step : 2 * step + 2].reshape(wide, slots)
-        values += jnp.dot(rows, block, preferred_element_type=F32)
-    return values
-
-
-def first_kernel(disp_ref, keep_ref, far_ref, values_ref, weight, done):
-    values_ref[...] = product(0, disp_ref, keep_ref, far_ref, weight, done)
-
-
 def values_kernel(
-    disp_ref,
+    own_ref,
+    other_ref,
     keep_ref,
     far_ref,
-    first_ref,
+    later_ref,
     mine_ref,
     theirs_ref,
     gate_ref,
@@ -156,16 +138,35 @@
     hidden,
     ready,
 ):
-    units, slots = mine_ref.shape
-    after = pl.ds(keep_ref.shape[1] - slots, slots)
-    copies = [
-        pltpu.make_async_copy(ref.at[:, after], hidden.at[k], ready.at[k])
-        for k, ref in enumerate((keep_ref, far_ref))
-    ]
-    for copy in copies:
-        copy.start()
-    values = first_ref[...] + product(1, disp_ref, keep_ref, far_ref, weight, done)
-    for copy in copies:
+    blocks, share, slots = own_ref.shape
+    units, wide, mine = mine_ref.shape[0], 2 * share, blocks * share
+    steps = blocks // 2
+    copies = []
+    for step in range(2 * steps):
+        here = pl.ds(step * wide, wide)
+        if step < steps:
+            from_far = far_ref.at[:, here]
+        else:
+            from_far = later_ref.at[:, pl.ds(step * wide - mine, wide)]
+        copies.append(
+            [
+                pltpu.make_async_copy(ref, weight.at[step, k], done.at[step, k])
+                for k, ref in enumerate((keep_ref.at[:, here], from_far))
+            ]
+        )
+    last = activations(keep_ref, far_ref, 2 * mine, mine, hidden, ready)
+    for now in copies + [last]:
+        for copy in now:
+            copy.start()
+    values = jnp.zeros((2 * units, slots), F32)
+    for step, now in enumerate(copies):
+        for copy in now:
+            copy.wait()
+        rows = weight[step].reshape(2 * units, wide)
+        ref, first = (own_ref, step) if step < steps else (other_ref, step - steps)
+        block = ref[2 * first : 2 * first + 2].reshape(wide, slots)
+        values += jnp.dot(rows, block, preferred_element_type=F32)
+    for copy in last:
         copy.wait()
     left = hidden[...].reshape(2 * units, slots).astype(F32)
     terms = jnp.sum(left * values, axis=0, keepdims=True)
@@ -175,59 +176,71 @@
     gate_ref[...] = jnp.broadcast_to(jnp.concatenate(lines, axis=0), gate_ref.shape)
 
 
-def down_kernel(
-    own_ref, other_ref, keep_ref, far_ref, values_ref, mine_ref, send_ref, hidden, ready
-):
-    blocks, share, slots = own_ref.shape
-    units, wide = hidden.shape[1], 2 * share
-    all_mine = mine_ref.shape[1]
-    after = pl.ds(all_mine, slots)
-    copies = [
-        pltpu.make_async_copy(ref.at[:, after], hidden.at[k], ready.at[k])
-        for k, ref in enumerate((keep_ref, far_ref))
+def activations(keep_ref, far_ref, keep_start, far_start, hidden, ready):
+    slots = hidden.shape[2]
+    return [
+        pltpu.make_async_copy(ref.at[:, pl.ds(start, slots)], hidden.at[k], ready.at[k])
+        for k, (ref, start) in enumerate(((keep_ref, keep_start), (far_ref, far_start)))
     ]
+
+
+def down_kernel(disp_ref, keep_ref, far_ref, mine_ref, send_ref, hidden, ready):
+    blocks, share, slots = disp_ref.shape
+    units, wide, mine = hidden.shape[1], 2 * share, blocks * share
+    copies = activations(keep_ref, far_ref, 2 * mine, mine, hidden, ready)
     for copy in copies:
         copy.start()
     for copy in copies:
         copy.wait()
     left = hidden[...].reshape(2 * units, slots)
-    for half, ref in enumerate((own_ref, other_ref)):
-        for step in range(blocks // 2):
-            block = ref[2 * step : 2 * step + 2].reshape(wide, slots)
-            down = lax.dot_general(
-                left, block, (((1,), (1,)), ((), ())), preferred_element_type=F32
-            ).astype(BF16)
-            start = (half * blocks // 2 + step) * wide
-            mine_ref[:, start : start + wide] = down[:units]
-            send_ref[:, start : start + wide] = down[units:]
+    for step in range(blocks // 2):
+        block = disp_ref[2 * step : 2 * step + 2].reshape(wide, slots)
+        down = lax.dot_general(
+            left, block, (((1,), (1,)), ((), ())), preferred_element_type=F32
+        ).astype(BF16)
+        mine_ref[:, wide * step : wide * (step + 1)] = down[:units]
+        send_ref[:, wide * step : wide * (step + 1)] = down[units:]
+
+
+def rest_kernel(
+    disp_ref, keep_ref, far_ref, values_ref, mine_ref, send_ref, hidden, ready
+):
+    down_kernel(disp_ref, keep_ref, far_ref, mine_ref, send_ref, hidden, ready)
+    mine, slots = mine_ref.shape[1], values_ref.shape[1]
     values = values_ref[...]
     high = values.astype(BF16)
-    send_ref[:, all_mine : all_mine + slots] = high
-    send_ref[:, all_mine + slots :] = (values - high.astype(F32)).astype(BF16)
+    send_ref[:, mine : mine + slots] = high
+    send_ref[:, mine + slots :] = (values - high.astype(F32)).astype(BF16)
 
 
 def finish_kernel(
-    place_ref, mine_ref, got_ref, values_ref, order_ref, down_ref, dhid_ref
+    place_ref,
+    own_ref,
+    other_ref,
+    got_own_ref,
+    got_other_ref,
+    values_ref,
+    order_ref,
+    down_ref,
+    dhid_ref,
 ):
     slots = values_ref.shape[1]
-    all_mine = mine_ref.shape[1]
+    mine = own_ref.shape[1]
     blocks = 4
-    share = all_mine // (2 * blocks)
+    share = mine // blocks
 
     def store(far, core):
         for f in range(2):
-            ref = mine_ref if f == far else got_ref
+            refs = (own_ref, other_ref) if f == far else (got_own_ref, got_other_ref)
+            refs = refs if core == 0 else refs[::-1]
             for y in range(blocks):
-                pair = []
-                for c in range(2):
-                    start = share * ((0 if c == core else blocks) + y)
-                    pair.append(ref[:, start : start + share])
+                pair = [ref[:, share * y : share * (y + 1)] for ref in refs]
                 start = 2 * share * (f * blocks + y)
                 down_ref[:, start : start + 2 * share] = jnp.concatenate(pair, axis=1)
 
     cases(place_ref, store)
-    high = got_ref[:, all_mine : all_mine + slots].astype(F32)
-    low = got_ref[:, all_mine + slots :].astype(F32)
+    high = got_other_ref[:, mine : mine + slots].astype(F32)
+    low = got_other_ref[:, mine + slots :].astype(F32)
     flipped = (values_ref[...] + (high + low)).T.astype(BF16)
     dhid_ref[...] = jnp.dot(
         order_ref[...], flipped, preferred_element_type=F32
@@ -311,18 +324,24 @@
     )(grad_out, routes, gates)
     arrived = swap_all(packed, "expert")
 
-    all_mine = 2 * mine
-    longer = bf16((units, all_mine + slots))
-    keep, to_far, order = pl.pallas_call(
+    keep, to_far, to_far_later, order = pl.pallas_call(
         functools.partial(split_kernel, experts),
-        out_shape=(longer, longer, bf16((slots, slots))),
+        out_shape=(
+            bf16((units, 2 * mine + slots)),
+            bf16((units, mine + slots)),
+            bf16((units, mine)),
+            bf16((slots, slots)),
+        ),
         in_specs=[scalar(), whole(), whole()],
-        out_specs=(whole(),) * 3,
+        out_specs=(whole(),) * 4,
         cost_estimate=cost(2 * units * slots * slots, 2 * 2 * units * width),
         name="split",
     )(place, w_down[0], hidden[0])
     from_far = other(to_far, "x")
-    arrived, from_far = lax.optimization_barrier((arrived, from_far))
+    arrived, from_far, to_far_later = lax.optimization_barrier(
+        (arrived, from_far, to_far_later)
+    )
+    later = other(to_far_later, "x")
 
     copies = pl.pallas_call(
         unpack_kernel,
@@ -336,30 +355,30 @@
         compiler_params=limit(8),
         name="unpack",
     )(arrived)
-    dispatched = swap_all(copies, "y")
-    from_core = in_vmem(other(dispatched, "core"))
+    dispatched, later = lax.optimization_barrier((swap_all(copies, "y"), later))
+    from_core = other(dispatched, "core")
     dispatched = in_vmem(dispatched)
 
-    keep, from_far = in_hbm(keep), in_hbm(from_far)
+    keep, from_far, later = in_hbm(keep), in_hbm(from_far), in_vmem(later)
     flops = 2 * slots * units * width
+    moved = slots * width + 2 * units * width
     scratch = [
-        pltpu.VMEM((rows_y // 2, 2, units, 2 * share), BF16),
-        pltpu.SemaphoreType.DMA((rows_y // 2, 2)),
-    ]
-    activations = [
         pltpu.VMEM((2, units, slots), BF16),
         pltpu.SemaphoreType.DMA((2,)),
     ]
-    first = pl.pallas_call(
-        first_kernel,
-        out_shape=f32((2 * units, slots)),
+    down_own, back_own = pl.pallas_call(
+        down_kernel,
+        out_shape=(bf16((units, mine)), bf16((units, mine))),
         in_specs=[whole(), stays(), stays()],
-        out_specs=whole(),
+        out_specs=(whole(),) * 2,
         scratch_shapes=scratch,
         compiler_params=limit(16),
-        cost_estimate=cost(flops // 2, slots * width + units * width),
-        name="first",
+        cost_estimate=cost(flops // 2, moved // 2),
+        name="down",
     )(dispatched, keep, from_far)
+    from_core, back_own = lax.optimization_barrier((from_core, back_own))
+    got_own = other(back_own, "x")
+
     mine_values, theirs, terms = pl.pallas_call(
         values_kernel,
         out_shape=(
@@ -367,27 +386,31 @@
             f32((units, slots)),
             jax.ShapeDtypeStruct((4 * rows_y, slots // LANES, LANES), F32),
         ),
-        in_specs=[whole(), stays(), stays(), whole()],
+        in_specs=[whole()] * 2 + [stays()] * 2 + [whole()],
         out_specs=(whole(),) * 3,
-        scratch_shapes=scratch + activations,
+        scratch_shapes=[
+            pltpu.VMEM((rows_y, 2, units, 2 * share), BF16),
+            pltpu.SemaphoreType.DMA((rows_y, 2)),
+        ]
+        + scratch,
         compiler_params=limit(16),
-        cost_estimate=cost(flops // 2, slots * width + units * width),
+        cost_estimate=cost(flops, moved),
         name="values",
-    )(from_core, keep, from_far, in_hbm(first))
+    )(dispatched, in_vmem(from_core), keep, from_far, later)
     parts = swap_all(terms, ("x", "y", "core"))
 
-    down, back = pl.pallas_call(
-        down_kernel,
-        out_shape=(bf16((units, all_mine)), bf16((units, all_mine + 2 * slots))),
-        in_specs=[whole()] * 2 + [stays()] * 2 + [whole()],
+    down_other, back_other = pl.pallas_call(
+        rest_kernel,
+        out_shape=(bf16((units, mine)), bf16((units, mine + 2 * slots))),
+        in_specs=[whole()] + [stays()] * 2 + [whole()],
         out_specs=(whole(),) * 2,
-        scratch_shapes=activations,
+        scratch_shapes=scratch,
         compiler_params=limit(16),
-        cost_estimate=cost(flops, slots * width + 2 * units * width),
-        name="down",
-    )(dispatched, from_core, keep, from_far, in_hbm(theirs))
-    parts, back = lax.optimization_barrier((parts, back))
-    got = other(back, "x")
+        cost_estimate=cost(flops // 2, moved // 2),
+        name="rest",
+    )(in_vmem(from_core), keep, from_far, in_hbm(theirs))
+    parts, back_other, got_own = lax.optimization_barrier((parts, back_other, got_own))
+    got_other = other(back_other, "x")
 
     d_down, d_hidden = pl.pallas_call(
         finish_kernel,
@@ -395,12 +418,20 @@
             jax.ShapeDtypeStruct((units, width), BF16),
             jax.ShapeDtypeStruct((slots, units), BF16),
         ),
-        in_specs=[scalar()] + [whole()] * 4,
+        in_specs=[scalar()] + [whole()] * 6,
         out_specs=(whole(),) * 2,
         compiler_params=limit(16),
         cost_estimate=cost(2 * units * slots * slots, 4 * units * width),
         name="finish",
-    )(place, in_hbm(down), in_vmem(got), in_hbm(mine_values), in_hbm(order))
+    )(
+        place,
+        in_hbm(down_own),
+        in_hbm(down_other),
+        in_vmem(got_own),
+        in_vmem(got_other),
+        in_hbm(mine_values),
+        in_hbm(order),
+    )
 
     sums = pl.pallas_call(
         sum_kernel,

time: 129 us -> 121 us (0.938)
  blocking collectives: 20.8 us -> 0 us
  starting transfers between devices: 44.4 us -> 53.5 us
  waiting for transfers between devices: 39.3 us -> 43.8 us
    all_to_all x1 -> x0, blocking collectives: 20.8 us -> none  [swap_all(): return lax.all_to_all(x, axis, split_axis=0, concat_axis=0, tiled=True)]
    all_to_all x3 -> x4, waiting for transfers between devices: 1.37 us -> 15.8 us  [swap_all(): return lax.all_to_all(x, axis, split_axis=0, concat_axis=0, tiled=True)]
    ppermute x3 -> x5, waiting for transfers between devices: 37.9 us -> 27.9 us  [other(): return lax.ppermute(x, axis, [(0, 1), (1, 0)])]
    ppermute x3 -> x5, starting transfers between devices: 9.26 us -> 15.3 us  [other(): return lax.ppermute(x, axis, [(0, 1), (1, 0)])]
    all_to_all x3 -> x4, starting transfers between devices: 35.1 us -> 38.2 us  [swap_all(): return lax.all_to_all(x, axis, split_axis=0, concat_axis=0, tiled=True)]
  transfers between devices with their start and end apart: 6 -> 9, of which waited for: 3 -> 8; matrix products, arithmetic and copies ran while one was open for 1% -> 0% of each run, Pallas kernels for 11% -> 14%
where the time goes in v6:
time: 121 us; the launch traced here: 120 us
  starting transfers between devices  53.5 us (44%)
  waiting for transfers between devices  43.8 us (36%)
  Pallas kernels  21.7 us (18%)
    all_to_all x4, starting transfers between devices, swap_all(): return lax.all_to_all(x, axis, split_axis=0, concat_axis=0, tiled=True)  38.2 us
    ppermute x5, waiting for transfers between devices, other(): return lax.ppermute(x, axis, [(0, 1), (1, 0)])  27.9 us
    all_to_all x4, waiting for transfers between devices, swap_all(): return lax.all_to_all(x, axis, split_axis=0, concat_axis=0, tiled=True)  15.8 us
    ppermute x5, starting transfers between devices, other(): return lax.ppermute(x, axis, [(0, 1), (1, 0)])  15.3 us
    pallas_call x1, Pallas kernels, on_device(): pl.pallas_call(functools.partial(split_kernel, experts), out_shape=(bf16(...  3.61 us
    pallas_call x1, Pallas kernels, on_device(): pl.pallas_call(rest_kernel, out_shape=(bf16((units, mine)), bf16((units,...  3.6 us
    pallas_call x1, Pallas kernels, on_device(): pl.pallas_call(values_kernel, out_shape=(f32((units, slots)), f32((units,...  3.6 us
    pallas_call x1, Pallas kernels, on_device(): pl.pallas_call(finish_kernel, out_shape=(jax.ShapeDtypeStruct((units, wid...  3.17 us
  transfers between devices with their start and end apart: 9, of which 8 were waited for; matrix products, arithmetic and copies ran while one was open for 0% of the time, Pallas kernels for 14%

profile of v6, /device:TPU:1, one launch (start us, length us, event | category | flops | bytes accessed | tf_op | source)
XLA Modules:
  0.0 120.4 jit_solution(13993580731108529226)
XLA Ops:
  0.6 2.0 %pack.1 = bf16[32,2,2688]{2,1,0:T(2,128)(2,1)} custom-call(bf16[32,448]{1,0:T(8,128)(2,1)} %grad_ref.1, s32[8,32]{1,0:T(8,128)} %bitcast.14, f32[8,32]{1,0:T(8,128)} %bitcast.16), custom_call_target="tpu_custom_call" | custom-call | tf_op jit(solution)/shard_map/pack/pallas_call | solution.py:318
  2.6 18.5 %all-to-all-start = ((bf16[32,2,2688]{2,1,0:T(2,128)(2,1)}), bf16[32,2,2688]{2,1,0:T(2,128)(2,1)S(1)}, u32[]{:S(2)}, u32[]{:S(2)}) async-start(bf16[32,2,2688]{2,1,0:T(2,128)(2,1)} %pack.1), calls=%async_computation | async-start | bytes 688128 | tf_op jit(solution)/shard_map/all_to_all | solution.py:300
  21.7 3.6 %split.1 = (bf16[128,3968]{1,0:T(8,128)(2,1)}, bf16[128,2176]{1,0:T(8,128)(2,1)}, bf16[128,1792]{1,0:T(8,128)(2,1)}, bf16[384,384]{1,0:T(8,128)(2,1)}) custom-call(s32[2]{0:T(128)} %pad_add_fusion.place_ref, bf16[128,7168]{1,0:T(8,128)(2,1)} %bitcast.18, bf16[384,128]{1,0:T(8,128)(2,1)} %bitcast.19), custom_call_target="tpu_custom_call" | custom-call | flops 37748736 | bytes 3670016 | tf_op jit(solution)/shard_map/split/pallas_call | solution.py:327
  25.4 2.2 %collective-permute-start = (bf16[128,2176]{1,0:T(8,128)(2,1)}, bf16[128,2176]{1,0:T(8,128)(2,1)}, u32[]{:S(2)}, u32[]{:S(2)}) collective-permute-start(bf16[128,2176]{1,0:T(8,128)(2,1)} %get-tuple-element.27), channel_id=1, source_target_pairs={{0,256},{256,0},{1,257},{257,1},{2,258},{258,2},{3,259},{259,3},{4... | collective-permute-start | bytes 1671176 | tf_op jit(solution)/shard_map/ppermute | solution.py:316
  27.6 15.9 %collective-permute-done.far_ref = bf16[128,2176]{1,0:T(8,128)(2,1)} collective-permute-done((bf16[128,2176]{1,0:T(8,128)(2,1)}, bf16[128,2176]{1,0:T(8,128)(2,1)}, u32[]{:S(2)}, u32[]{:S(2)}) %collective-permute-start) | collective-permute-done | bytes 557088 | tf_op jit(solution)/shard_map/ppermute | solution.py:316
  43.4 2.4 %all-to-all-done.in_ref = bf16[32,2,2688]{2,1,0:T(2,128)(2,1)S(1)} async-done(((bf16[32,2,2688]{2,1,0:T(2,128)(2,1)}), bf16[32,2,2688]{2,1,0:T(2,128)(2,1)S(1)}, u32[]{:S(2)}, u32[]{:S(2)}) %all-to-all-start) | async-done | bytes 344096 | tf_op jit(solution)/shard_map/all_to_all | solution.py:300
  45.8 1.6 %unpack.1 = bf16[4,448,384]{2,1,0:T(8,128)(2,1)} custom-call(bf16[32,2,2688]{2,1,0:T(2,128)(2,1)S(1)} %all-to-all-done.in_ref), custom_call_target="tpu_custom_call" | custom-call | tf_op jit(solution)/shard_map/unpack/pallas_call | solution.py:346
  47.4 4.3 %all-to-all-start.1 = ((bf16[4,448,384]{2,1,0:T(8,128)(2,1)}), bf16[4,448,384]{2,1,0:T(8,128)(2,1)S(1)}, u32[]{:S(2)}, u32[]{:S(2)}) async-start(bf16[4,448,384]{2,1,0:T(8,128)(2,1)} %unpack.1), calls=%async_computation.1 | async-start | bytes 2752512 | tf_op jit(solution)/shard_map/all_to_all | solution.py:300
  51.8 2.2 %collective-permute-start.1 = (bf16[128,1792]{1,0:T(8,128)(2,1)S(1)}, bf16[128,1792]{1,0:T(8,128)(2,1)S(1)}, u32[]{:S(2)}, u32[]{:S(2)}) collective-permute-start(bf16[128,1792]{1,0:T(8,128)(2,1)S(1)} %copy-done.3), channel_id=1, source_target_pairs={{0,256},{256,0},{1,257},{257,1},{2,258},{258,2},{3,259},{259,3},{4... | collective-permute-start | bytes 1376264 | tf_op jit(solution)/shard_map/ppermute | solution.py:316
  54.0 8.3 %collective-permute-done.1.later_ref = bf16[128,1792]{1,0:T(8,128)(2,1)S(1)} collective-permute-done((bf16[128,1792]{1,0:T(8,128)(2,1)S(1)}, bf16[128,1792]{1,0:T(8,128)(2,1)S(1)}, u32[]{:S(2)}, u32[]{:S(2)}) %collective-permute-start.1) | collective-permute-done | bytes 458784 | tf_op jit(solution)/shard_map/ppermute | solution.py:316
  62.3 4.4 %all-to-all-done.1.disp_ref.own_ref = bf16[4,448,384]{2,1,0:T(8,128)(2,1)S(1)} async-done(((bf16[4,448,384]{2,1,0:T(8,128)(2,1)}), bf16[4,448,384]{2,1,0:T(8,128)(2,1)S(1)}, u32[]{:S(2)}, u32[]{:S(2)}) %all-to-all-start.1) | async-done | bytes 1376288 | tf_op jit(solution)/shard_map/all_to_all | solution.py:300
  66.7 6.5 %collective-permute-start.2 = (bf16[4,448,384]{2,1,0:T(8,128)(2,1)S(1)}, bf16[4,448,384]{2,1,0:T(8,128)(2,1)S(1)}, u32[]{:S(2)}, u32[]{:S(2)}) collective-permute-start(bf16[4,448,384]{2,1,0:T(8,128)(2,1)S(1)} %all-to-all-done.1.disp_ref.own_ref), channel_id=1, source_target_pairs={{0,32},{32,0},{1,33},{33,1},{2,34},{34,2},{3,35},{35,3},{4,36},{36... | collective-permute-start | bytes 4128776 | tf_op jit(solution)/shard_map/ppermute | solution.py:316
  73.2 2.6 %down.1 = (bf16[128,1792]{1,0:T(8,128)(2,1)}, bf16[128,1792]{1,0:T(8,128)(2,1)}) custom-call(bf16[4,448,384]{2,1,0:T(8,128)(2,1)S(1)} %all-to-all-done.1.disp_ref.own_ref, bf16[128,3968]{1,0:T(8,128)(2,1)} %get-tuple-element.32.keep_ref, bf16[128,2176]{1,0:T(8,128)(2,1)} %collective-permute-done.far_ref), custom_call_target="tpu_custom_call" | custom-call | flops 352321536 | bytes 2293760 | tf_op jit(solution)/shard_map/down/pallas_call | solution.py:369
  76.0 2.2 %collective-permute-start.3 = (bf16[128,1792]{1,0:T(8,128)(2,1)}, bf16[128,1792]{1,0:T(8,128)(2,1)}, u32[]{:S(2)}, u32[]{:S(2)}) collective-permute-start(bf16[128,1792]{1,0:T(8,128)(2,1)} %get-tuple-element.42), channel_id=1, source_target_pairs={{0,256},{256,0},{1,257},{257,1},{2,258},{258,2},{3,259},{259,3},{4... | collective-permute-start | bytes 1376264 | tf_op jit(solution)/shard_map/ppermute | solution.py:316
  78.2 3.6 %values.1 = (f32[128,384]{1,0:T(8,128)}, f32[128,384]{1,0:T(8,128)}, f32[16,3,128]{2,1,0:T(4,128)}) custom-call(bf16[4,448,384]{2,1,0:T(8,128)(2,1)S(1)} %all-to-all-done.1.disp_ref.own_ref, bf16[4,448,384]{2,1,0:T(8,128)(2,1)S(1)} %collective-permute-done.2.other_ref.disp_ref, bf16[128,3968]{1,0:T(8,128)(2,1)} %get-tuple-element.32.keep_ref, ...), custom_call_target="tpu_custom_call" | custom-call | flops 704643072 | bytes 4587520 | tf_op jit(solution)/shard_map/values/pallas_call | solution.py:382
  81.8 4.0 %all-to-all-start.2 = ((f32[16,3,128]{2,1,0:T(4,128)}), f32[16,3,128]{2,1,0:T(4,128)S(1)}, u32[]{:S(2)}, u32[]{:S(2)}) async-start(f32[16,3,128]{2,1,0:T(4,128)} %get-tuple-element.40), calls=%async_computation.2 | async-start | bytes 65536 | tf_op jit(solution)/shard_map/all_to_all | solution.py:300
  85.8 3.6 %rest.1 = (bf16[128,1792]{1,0:T(8,128)(2,1)}, bf16[128,2560]{1,0:T(8,128)(2,1)}) custom-call(bf16[4,448,384]{2,1,0:T(8,128)(2,1)S(1)} %collective-permute-done.2.other_ref.disp_ref, bf16[128,3968]{1,0:T(8,128)(2,1)} %get-tuple-element.32.keep_ref, bf16[128,2176]{1,0:T(8,128)(2,1)} %collective-permute-done.far_ref, f32[128,384]{1,0:T(8,128)} %get-tuple-element.38.values_ref), custom_call_target="tpu_custom_call" | custom-call | flops 352321536 | bytes 2293760 | tf_op jit(solution)/shard_map/rest/pallas_call | solution.py:402
  89.4 2.2 %all-to-all-done.2.parts_ref = f32[16,3,128]{2,1,0:T(4,128)S(1)} async-done(((f32[16,3,128]{2,1,0:T(4,128)}), f32[16,3,128]{2,1,0:T(4,128)S(1)}, u32[]{:S(2)}, u32[]{:S(2)}) %all-to-all-start.2) | async-done | bytes 24608 | tf_op jit(solution)/shard_map/all_to_all | solution.py:300
  91.6 2.2 %collective-permute-start.4 = (bf16[128,2560]{1,0:T(8,128)(2,1)}, bf16[128,2560]{1,0:T(8,128)(2,1)S(1)}, u32[]{:S(2)}, u32[]{:S(2)}) collective-permute-start(bf16[128,2560]{1,0:T(8,128)(2,1)} %get-tuple-element.44), channel_id=1, source_target_pairs={{0,256},{256,0},{1,257},{257,1},{2,258},{258,2},{3,259},{259,3},{4... | collective-permute-start | bytes 1966088 | tf_op jit(solution)/shard_map/ppermute | solution.py:316
  94.6 11.4 %all-to-all-start.3 = ((f32[32,1,12]{2,1,0:T(1,128)}), f32[32,1,12]{2,1,0:T(1,128)S(1)}, u32[]{:S(2)}, u32[]{:S(2)}) async-start(f32[32,1,12]{2,1,0:T(1,128)} %bitcast.9), calls=%async_computation.3 | async-start | bytes 32768 | tf_op jit(solution)/shard_map/all_to_all | solution.py:300
  105.9 3.7 %collective-permute-done.4.got_other_ref = bf16[128,2560]{1,0:T(8,128)(2,1)S(1)} collective-permute-done((bf16[128,2560]{1,0:T(8,128)(2,1)}, bf16[128,2560]{1,0:T(8,128)(2,1)S(1)}, u32[]{:S(2)}, u32[]{:S(2)}) %collective-permute-start.4) | collective-permute-done | bytes 655392 | tf_op jit(solution)/shard_map/ppermute | solution.py:316
  109.6 3.2 %finish.1 = (bf16[128,7168]{1,0:T(8,128)(2,1)}, bf16[384,128]{1,0:T(8,128)(2,1)}) custom-call(s32[2]{0:T(128)S(1)} %copy-done.2, bf16[128,1792]{1,0:T(8,128)(2,1)} %get-tuple-element.34.own_ref, bf16[128,1792]{1,0:T(8,128)(2,1)} %get-tuple-element.39.other_ref, bf16[128,1792]{1,0:T(8,128)(2,1)} %collective-permute-done.3.got_own_ref, ...), custom_call_target="tpu_custom_call" | custom-call | flops 37748736 | bytes 3670016 | tf_op jit(solution)/shard_map/finish/pallas_call | solution.py:415
  112.8 6.8 %all-to-all-done.3 = f32[32,1,12]{2,1,0:T(1,128)S(1)} async-done(((f32[32,1,12]{2,1,0:T(1,128)}), f32[32,1,12]{2,1,0:T(1,128)S(1)}, u32[]{:S(2)}, u32[]{:S(2)}) %all-to-all-start.3) | async-done | bytes 1568 | tf_op jit(solution)/shard_map/all_to_all | solution.py:300
  119.6 0.8 match.1
  (12 shorter events, 1.5 us)
Async XLA Ops:
  2.6 43.2 %all-to-all-start = ((bf16[32,2,2688]{2,1,0:T(2,128)(2,1)}), bf16[32,2,2688]{2,1,0:T(2,128)(2,1)S(1)}, u32[]{:S(2)}, u32[]{:S(2)}) async-start(bf16[32,2,2688]{2,1,0:T(2,128)(2,1)} %pack.1), calls=%async_computation | async-start | bytes 688128 | tf_op jit(solution)/shard_map/all_to_all | solution.py:300
  25.4 18.1 %collective-permute-start = (bf16[128,2176]{1,0:T(8,128)(2,1)}, bf16[128,2176]{1,0:T(8,128)(2,1)}, u32[]{:S(2)}, u32[]{:S(2)}) collective-permute-start(bf16[128,2176]{1,0:T(8,128)(2,1)} %get-tuple-element.27), channel_id=1, source_target_pairs={{0,256},{256,0},{1,257},{257,1},{2,258},{258,2},{3,259},{259,3},{4... | collective-permute-start | bytes 1671176 | tf_op jit(solution)/shard_map/ppermute | solution.py:316
  47.4 4.3 %copy-start.3 = (bf16[128,1792]{1,0:T(8,128)(2,1)S(1)}, bf16[128,1792]{1,0:T(8,128)(2,1)}, u32[]{:S(2)}) copy-start(bf16[128,1792]{1,0:T(8,128)(2,1)} %get-tuple-element.30) | copy-start | bytes 1376260
  47.4 19.3 %all-to-all-start.1 = ((bf16[4,448,384]{2,1,0:T(8,128)(2,1)}), bf16[4,448,384]{2,1,0:T(8,128)(2,1)S(1)}, u32[]{:S(2)}, u32[]{:S(2)}) async-start(bf16[4,448,384]{2,1,0:T(8,128)(2,1)} %unpack.1), calls=%async_computation.1 | async-start | bytes 2752512 | tf_op jit(solution)/shard_map/all_to_all | solution.py:300
  51.8 10.5 %collective-permute-start.1 = (bf16[128,1792]{1,0:T(8,128)(2,1)S(1)}, bf16[128,1792]{1,0:T(8,128)(2,1)S(1)}, u32[]{:S(2)}, u32[]{:S(2)}) collective-permute-start(bf16[128,1792]{1,0:T(8,128)(2,1)S(1)} %copy-done.3), channel_id=1, source_target_pairs={{0,256},{256,0},{1,257},{257,1},{2,258},{258,2},{3,259},{259,3},{4... | collective-permute-start | bytes 1376264 | tf_op jit(solution)/shard_map/ppermute | solution.py:316
  66.7 9.2 %collective-permute-start.2 = (bf16[4,448,384]{2,1,0:T(8,128)(2,1)S(1)}, bf16[4,448,384]{2,1,0:T(8,128)(2,1)S(1)}, u32[]{:S(2)}, u32[]{:S(2)}) collective-permute-start(bf16[4,448,384]{2,1,0:T(8,128)(2,1)S(1)} %all-to-all-done.1.disp_ref.own_ref), channel_id=1, source_target_pairs={{0,32},{32,0},{1,33},{33,1},{2,34},{34,2},{3,35},{35,3},{4,36},{36... | collective-permute-start | bytes 4128776 | tf_op jit(solution)/shard_map/ppermute | solution.py:316
  76.0 15.6 %collective-permute-start.3 = (bf16[128,1792]{1,0:T(8,128)(2,1)}, bf16[128,1792]{1,0:T(8,128)(2,1)}, u32[]{:S(2)}, u32[]{:S(2)}) collective-permute-start(bf16[128,1792]{1,0:T(8,128)(2,1)} %get-tuple-element.42), channel_id=1, source_target_pairs={{0,256},{256,0},{1,257},{257,1},{2,258},{258,2},{3,259},{259,3},{4... | collective-permute-start | bytes 1376264 | tf_op jit(solution)/shard_map/ppermute | solution.py:316
  81.8 9.8 %all-to-all-start.2 = ((f32[16,3,128]{2,1,0:T(4,128)}), f32[16,3,128]{2,1,0:T(4,128)S(1)}, u32[]{:S(2)}, u32[]{:S(2)}) async-start(f32[16,3,128]{2,1,0:T(4,128)} %get-tuple-element.40), calls=%async_computation.2 | async-start | bytes 65536 | tf_op jit(solution)/shard_map/all_to_all | solution.py:300
  85.8 23.9 %copy-start.2 = (s32[2]{0:T(128)S(1)}, s32[2]{0:T(128)}, u32[]{:S(2)}) copy-start(s32[2]{0:T(128)} %pad_add_fusion.place_ref) | copy-start | bytes 28
  89.4 30.2 %copy-start = (s32[32,8]{0,1:T(8,128)S(1)}, s32[32,8]{0,1:T(8,128)}, u32[]{:S(2)}) copy-start(s32[32,8]{0,1:T(8,128)} %param.6) | copy-start | bytes 3076
  89.4 30.2 %copy-start.1 = (f32[32,8]{0,1:T(8,128)S(1)}, f32[32,8]{0,1:T(8,128)}, u32[]{:S(2)}) copy-start(f32[32,8]{0,1:T(8,128)} %param.7) | copy-start | bytes 3076
  91.6 18.0 %collective-permute-start.4 = (bf16[128,2560]{1,0:T(8,128)(2,1)}, bf16[128,2560]{1,0:T(8,128)(2,1)S(1)}, u32[]{:S(2)}, u32[]{:S(2)}) collective-permute-start(bf16[128,2560]{1,0:T(8,128)(2,1)} %get-tuple-element.44), channel_id=1, source_target_pairs={{0,256},{256,0},{1,257},{257,1},{2,258},{258,2},{3,259},{259,3},{4... | collective-permute-start | bytes 1966088 | tf_op jit(solution)/shard_map/ppermute | solution.py:316
  94.6 25.0 %all-to-all-start.3 = ((f32[32,1,12]{2,1,0:T(1,128)}), f32[32,1,12]{2,1,0:T(1,128)S(1)}, u32[]{:S(2)}, u32[]{:S(2)}) async-start(f32[32,1,12]{2,1,0:T(1,128)} %bitcast.9), calls=%async_computation.3 | async-start | bytes 32768 | tf_op jit(solution)/shard_map/all_to_all | solution.py:300

commit v7 on v6

--- a/solution.py
+++ b/solution.py
@@ -117,9 +117,9 @@
         keep_ref[:, :mine] = part(far, core)
         keep_ref[:, mine:all_mine] = part(far, 1 - core)
         keep_ref[:, all_mine:] = flipped
-        far_ref[:, :mine] = part(1 - far, core)
-        far_ref[:, mine:] = flipped
-        later_ref[...] = part(1 - far, 1 - core)
+        far_ref[...] = part(1 - far, core)
+        later_ref[:, :mine] = part(1 - far, 1 - core)
+        later_ref[:, mine:] = flipped
 
     cases(place_ref, store)
 
@@ -154,7 +154,10 @@
                 for k, ref in enumerate((keep_ref.at[:, here], from_far))
             ]
         )
-    last = activations(keep_ref, far_ref, 2 * mine, mine, hidden, ready)
+    last = [
+        pltpu.make_async_copy(ref.at[:, pl.ds(start, slots)], hidden.at[k], ready.at[k])
+        for k, (ref, start) in enumerate(((keep_ref, 2 * mine), (later_ref, mine)))
+    ]
     for now in copies + [last]:
         for copy in now:
             copy.start()
@@ -171,76 +174,75 @@
     left = hidden[...].reshape(2 * units, slots).astype(F32)
     terms = jnp.sum(left * values, axis=0, keepdims=True)
     mine_ref[...] = values[:units]
-    theirs_ref[...] = values[units:]
+    theirs = values[units:]
+    high = theirs.astype(BF16)
+    theirs_ref[:, :slots] = high
+    theirs_ref[:, slots:] = (theirs - high.astype(F32)).astype(BF16)
     lines = [terms[:, i : i + LANES] for i in range(0, slots, LANES)]
     gate_ref[...] = jnp.broadcast_to(jnp.concatenate(lines, axis=0), gate_ref.shape)
 
 
-def activations(keep_ref, far_ref, keep_start, far_start, hidden, ready):
-    slots = hidden.shape[2]
-    return [
-        pltpu.make_async_copy(ref.at[:, pl.ds(start, slots)], hidden.at[k], ready.at[k])
-        for k, (ref, start) in enumerate(((keep_ref, keep_start), (far_ref, far_start)))
-    ]
-
-
-def down_kernel(disp_ref, keep_ref, far_ref, mine_ref, send_ref, hidden, ready):
+def down(left, disp_ref, out_ref, first):
     blocks, share, slots = disp_ref.shape
-    units, wide, mine = hidden.shape[1], 2 * share, blocks * share
-    copies = activations(keep_ref, far_ref, 2 * mine, mine, hidden, ready)
-    for copy in copies:
-        copy.start()
-    for copy in copies:
-        copy.wait()
-    left = hidden[...].reshape(2 * units, slots)
+    wide = 2 * share
     for step in range(blocks // 2):
         block = disp_ref[2 * step : 2 * step + 2].reshape(wide, slots)
-        down = lax.dot_general(
+        part = lax.dot_general(
             left, block, (((1,), (1,)), ((), ())), preferred_element_type=F32
-        ).astype(BF16)
-        mine_ref[:, wide * step : wide * (step + 1)] = down[:units]
-        send_ref[:, wide * step : wide * (step + 1)] = down[units:]
-
-
-def rest_kernel(
-    disp_ref, keep_ref, far_ref, values_ref, mine_ref, send_ref, hidden, ready
-):
-    down_kernel(disp_ref, keep_ref, far_ref, mine_ref, send_ref, hidden, ready)
-    mine, slots = mine_ref.shape[1], values_ref.shape[1]
-    values = values_ref[...]
-    high = values.astype(BF16)
-    send_ref[:, mine : mine + slots] = high
-    send_ref[:, mine + slots :] = (values - high.astype(F32)).astype(BF16)
+        )
+        start = first + wide * step
+        out_ref[:, start : start + wide] = part.astype(BF16)
+
+
+def far_kernel(own_ref, later_ref, out_ref):
+    down(later_ref[:, out_ref.shape[1] :], own_ref, out_ref, 0)
+
+
+def far_rest_kernel(other_ref, later_ref, first_ref, out_ref):
+    mine = first_ref.shape[1]
+    out_ref[:, :mine] = first_ref[...]
+    down(later_ref[:, mine:], other_ref, out_ref, mine)
+
+
+def own_kernel(own_ref, other_ref, keep_ref, out_ref, hidden, done):
+    mine = out_ref.shape[1] // 2
+    after = pl.ds(2 * mine, hidden.shape[1])
+    copy = pltpu.make_async_copy(keep_ref.at[:, after], hidden, done)
+    copy.start()
+    copy.wait()
+    for half, ref in enumerate((own_ref, other_ref)):
+        down(hidden[...], ref, out_ref, half * mine)
 
 
 def finish_kernel(
     place_ref,
     own_ref,
-    other_ref,
-    got_own_ref,
-    got_other_ref,
+    far_ref,
+    got_values_ref,
     values_ref,
     order_ref,
     down_ref,
     dhid_ref,
 ):
     slots = values_ref.shape[1]
-    mine = own_ref.shape[1]
+    mine = own_ref.shape[1] // 2
     blocks = 4
     share = mine // blocks
 
     def store(far, core):
         for f in range(2):
-            refs = (own_ref, other_ref) if f == far else (got_own_ref, got_other_ref)
-            refs = refs if core == 0 else refs[::-1]
+            ref = own_ref if f == far else far_ref
             for y in range(blocks):
-                pair = [ref[:, share * y : share * (y + 1)] for ref in refs]
+                pair = []
+                for c in range(2):
+                    start = (0 if c == core else mine) + share * y
+                    pair.append(ref[:, start : start + share])
                 start = 2 * share * (f * blocks + y)
                 down_ref[:, start : start + 2 * share] = jnp.concatenate(pair, axis=1)
 
     cases(place_ref, store)
-    high = got_other_ref[:, mine : mine + slots].astype(F32)
-    low = got_other_ref[:, mine + slots :].astype(F32)
+    high = got_values_ref[:, :slots].astype(F32)
+    low = got_values_ref[:, slots:].astype(F32)
     flipped = (values_ref[...] + (high + low)).T.astype(BF16)
     dhid_ref[...] = jnp.dot(
         order_ref[...], flipped, preferred_element_type=F32
@@ -328,8 +330,8 @@
         functools.partial(split_kernel, experts),
         out_shape=(
             bf16((units, 2 * mine + slots)),
+            bf16((units, mine)),
             bf16((units, mine + slots)),
-            bf16((units, mine)),
             bf16((slots, slots)),
         ),
         in_specs=[scalar(), whole(), whole()],
@@ -362,28 +364,36 @@
     keep, from_far, later = in_hbm(keep), in_hbm(from_far), in_vmem(later)
     flops = 2 * slots * units * width
     moved = slots * width + 2 * units * width
-    scratch = [
-        pltpu.VMEM((2, units, slots), BF16),
-        pltpu.SemaphoreType.DMA((2,)),
-    ]
-    down_own, back_own = pl.pallas_call(
-        down_kernel,
-        out_shape=(bf16((units, mine)), bf16((units, mine))),
-        in_specs=[whole(), stays(), stays()],
-        out_specs=(whole(),) * 2,
-        scratch_shapes=scratch,
-        compiler_params=limit(16),
-        cost_estimate=cost(flops // 2, moved // 2),
-        name="down",
-    )(dispatched, keep, from_far)
-    from_core, back_own = lax.optimization_barrier((from_core, back_own))
-    got_own = other(back_own, "x")
+    def kernel(body, name, out, *operands):
+        return pl.pallas_call(
+            body,
+            out_shape=out,
+            in_specs=[whole()] * len(operands),
+            out_specs=whole(),
+            compiler_params=limit(16),
+            cost_estimate=cost(flops // 4, moved // 4),
+            name=name,
+        )(*operands)
+
+    far_own = kernel(far_kernel, "far", bf16((units, mine)), dispatched, later)
+    from_core, far_own = lax.optimization_barrier((from_core, far_own))
+    far_both = kernel(
+        far_rest_kernel,
+        "far_rest",
+        bf16((units, 2 * mine)),
+        in_vmem(from_core),
+        later,
+        in_hbm(far_own),
+    )
+    from_core, far_both = lax.optimization_barrier((from_core, far_both))
+    from_core = in_vmem(from_core)
+    got = other(far_both, "x")
 
     mine_values, theirs, terms = pl.pallas_call(
         values_kernel,
         out_shape=(
             f32((units, slots)),
-            f32((units, slots)),
+            bf16((units, 2 * slots)),
             jax.ShapeDtypeStruct((4 * rows_y, slots // LANES, LANES), F32),
         ),
         in_specs=[whole()] * 2 + [stays()] * 2 + [whole()],
@@ -391,26 +401,27 @@
         scratch_shapes=[
             pltpu.VMEM((rows_y, 2, units, 2 * share), BF16),
             pltpu.SemaphoreType.DMA((rows_y, 2)),
-        ]
-        + scratch,
+            pltpu.VMEM((2, units, slots), BF16),
+            pltpu.SemaphoreType.DMA((2,)),
+        ],
         compiler_params=limit(16),
         cost_estimate=cost(flops, moved),
         name="values",
-    )(dispatched, in_vmem(from_core), keep, from_far, later)
+    )(dispatched, from_core, keep, from_far, later)
     parts = swap_all(terms, ("x", "y", "core"))
 
-    down_other, back_other = pl.pallas_call(
-        rest_kernel,
-        out_shape=(bf16((units, mine)), bf16((units, mine + 2 * slots))),
-        in_specs=[whole()] + [stays()] * 2 + [whole()],
-        out_specs=(whole(),) * 2,
-        scratch_shapes=scratch,
+    down_own = pl.pallas_call(
+        own_kernel,
+        out_shape=bf16((units, 2 * mine)),
+        in_specs=[whole()] * 2 + [stays()],
+        out_specs=whole(),
+        scratch_shapes=[pltpu.VMEM((units, slots), BF16), pltpu.SemaphoreType.DMA],
         compiler_params=limit(16),
         cost_estimate=cost(flops // 2, moved // 2),
-        name="rest",
-    )(in_vmem(from_core), keep, from_far, in_hbm(theirs))
-    parts, back_other, got_own = lax.optimization_barrier((parts, back_other, got_own))
-    got_other = other(back_other, "x")
+        name="own",
+    )(dispatched, from_core, keep)
+    parts, down_own, theirs = lax.optimization_barrier((parts, down_own, theirs))
+    got_values = other(theirs, "x")
 
     d_down, d_hidden = pl.pallas_call(
         finish_kernel,
@@ -418,7 +429,7 @@
             jax.ShapeDtypeStruct((units, width), BF16),
             jax.ShapeDtypeStruct((slots, units), BF16),
         ),
-        in_specs=[scalar()] + [whole()] * 6,
+        in_specs=[scalar()] + [whole()] * 5,
         out_specs=(whole(),) * 2,
         compiler_params=limit(16),
         cost_estimate=cost(2 * units * slots * slots, 4 * units * width),
@@ -426,9 +437,8 @@
     )(
         place,
         in_hbm(down_own),
-        in_hbm(down_other),
-        in_vmem(got_own),
-        in_vmem(got_other),
+        in_vmem(got),
+        in_vmem(got_values),
         in_hbm(mine_values),
         in_hbm(order),
     )

time: 121 us -> 131 us (1.083)
  waiting for transfers between devices: 43.8 us -> 55.1 us
  starting transfers between devices: 53.5 us -> 51.3 us
    all_to_all x4, waiting for transfers between devices: 15.8 us -> 29.6 us  [swap_all(): return lax.all_to_all(x, axis, split_axis=0, concat_axis=0, tiled=True)]
    ppermute x5, waiting for transfers between devices: 27.9 us -> 25.5 us  [other(): return lax.ppermute(x, axis, [(0, 1), (1, 0)])]
    all_to_all x4, starting transfers between devices: 38.2 us -> 36 us  [swap_all(): return lax.all_to_all(x, axis, split_axis=0, concat_axis=0, tiled=True)]
    pallas_call x3 -> x4, Pallas kernels: 9.82 us -> 10.3 us  [the longest x2 3.85 us: kernel(): pl.pallas_call(body, out_shape=out, in_specs=[whole()] * len(operands), o...]
  transfers between devices with their start and end apart: 9 -> 9, of which waited for: 8 -> 7; matrix products, arithmetic and copies ran while one was open for 0% -> 0% of each run, Pallas kernels for 14% -> 12%
where the time goes in v7:
time: 131 us; the launch traced here: 130 us
  waiting for transfers between devices  55.1 us (42%)
  starting transfers between devices  51.3 us (39%)
  Pallas kernels  22.3 us (17%)
    all_to_all x4, starting transfers between devices, swap_all(): return lax.all_to_all(x, axis, split_axis=0, concat_axis=0, tiled=True)  36 us
    all_to_all x4, waiting for transfers between devices, swap_all(): return lax.all_to_all(x, axis, split_axis=0, concat_axis=0, tiled=True)  29.6 us
    ppermute x5, waiting for transfers between devices, other(): return lax.ppermute(x, axis, [(0, 1), (1, 0)])  25.5 us
    ppermute x5, starting transfers between devices, other(): return lax.ppermute(x, axis, [(0, 1), (1, 0)])  15.3 us
    pallas_call x2, Pallas kernels, kernel(): pl.pallas_call(body, out_shape=out, in_specs=[whole()] * len(operands), o...  3.85 us
    pallas_call x1, Pallas kernels, on_device(): pl.pallas_call(values_kernel, out_shape=(f32((units, slots)), bf16((units...  3.62 us
    pallas_call x1, Pallas kernels, on_device(): pl.pallas_call(functools.partial(split_kernel, experts), out_shape=(bf16(...  3.62 us
    pallas_call x1, Pallas kernels, on_device(): pl.pallas_call(finish_kernel, out_shape=(jax.ShapeDtypeStruct((units, wid...  3.26 us
  transfers between devices with their start and end apart: 9, of which 7 were waited for; matrix products, arithmetic and copies ran while one was open for 0% of the time, Pallas kernels for 12%

profile of v7, /device:TPU:1, one launch (start us, length us, event | category | flops | bytes accessed | tf_op | source)
XLA Modules:
  0.0 130.1 jit_solution(13087004158003075921)
XLA Ops:
  0.6 2.0 %pack.1 = bf16[32,2,2688]{2,1,0:T(2,128)(2,1)} custom-call(bf16[32,448]{1,0:T(8,128)(2,1)} %grad_ref.1, s32[8,32]{1,0:T(8,128)} %bitcast.14, f32[8,32]{1,0:T(8,128)} %bitcast.16), custom_call_target="tpu_custom_call" | custom-call | tf_op jit(solution)/shard_map/pack/pallas_call | solution.py:320
  2.6 18.5 %all-to-all-start = ((bf16[32,2,2688]{2,1,0:T(2,128)(2,1)}), bf16[32,2,2688]{2,1,0:T(2,128)(2,1)S(1)}, u32[]{:S(2)}, u32[]{:S(2)}) async-start(bf16[32,2,2688]{2,1,0:T(2,128)(2,1)} %pack.1), calls=%async_computation | async-start | bytes 688128 | tf_op jit(solution)/shard_map/all_to_all | solution.py:302
  21.7 3.6 %split.1 = (bf16[128,3968]{1,0:T(8,128)(2,1)}, bf16[128,1792]{1,0:T(8,128)(2,1)}, bf16[128,2176]{1,0:T(8,128)(2,1)}, bf16[384,384]{1,0:T(8,128)(2,1)}) custom-call(s32[2]{0:T(128)} %pad_add_fusion.place_ref, bf16[128,7168]{1,0:T(8,128)(2,1)} %bitcast.18, bf16[384,128]{1,0:T(8,128)(2,1)} %bitcast.19), custom_call_target="tpu_custom_call" | custom-call | flops 37748736 | bytes 3670016 | tf_op jit(solution)/shard_map/split/pallas_call | solution.py:329
  25.3 2.2 %collective-permute-start = (bf16[128,1792]{1,0:T(8,128)(2,1)}, bf16[128,1792]{1,0:T(8,128)(2,1)}, u32[]{:S(2)}, u32[]{:S(2)}) collective-permute-start(bf16[128,1792]{1,0:T(8,128)(2,1)} %get-tuple-element.25), channel_id=1, source_target_pairs={{0,256},{256,0},{1,257},{257,1},{2,258},{258,2},{3,259},{259,3},{4... | collective-permute-start | bytes 1376264 | tf_op jit(solution)/shard_map/ppermute | solution.py:318
  27.5 13.7 %collective-permute-done.far_ref = bf16[128,1792]{1,0:T(8,128)(2,1)} collective-permute-done((bf16[128,1792]{1,0:T(8,128)(2,1)}, bf16[128,1792]{1,0:T(8,128)(2,1)}, u32[]{:S(2)}, u32[]{:S(2)}) %collective-permute-start) | collective-permute-done | bytes 458784 | tf_op jit(solution)/shard_map/ppermute | solution.py:318
  41.3 4.6 %all-to-all-done.in_ref = bf16[32,2,2688]{2,1,0:T(2,128)(2,1)S(1)} async-done(((bf16[32,2,2688]{2,1,0:T(2,128)(2,1)}), bf16[32,2,2688]{2,1,0:T(2,128)(2,1)S(1)}, u32[]{:S(2)}, u32[]{:S(2)}) %all-to-all-start) | async-done | bytes 344096 | tf_op jit(solution)/shard_map/all_to_all | solution.py:302
  45.8 1.6 %unpack.1 = bf16[4,448,384]{2,1,0:T(8,128)(2,1)} custom-call(bf16[32,2,2688]{2,1,0:T(2,128)(2,1)S(1)} %all-to-all-done.in_ref), custom_call_target="tpu_custom_call" | custom-call | tf_op jit(solution)/shard_map/unpack/pallas_call | solution.py:348
  47.4 4.3 %all-to-all-start.1 = ((bf16[4,448,384]{2,1,0:T(8,128)(2,1)}), bf16[4,448,384]{2,1,0:T(8,128)(2,1)S(1)}, u32[]{:S(2)}, u32[]{:S(2)}) async-start(bf16[4,448,384]{2,1,0:T(8,128)(2,1)} %unpack.1), calls=%async_computation.1 | async-start | bytes 2752512 | tf_op jit(solution)/shard_map/all_to_all | solution.py:302
  51.7 2.2 %collective-permute-start.1 = (bf16[128,2176]{1,0:T(8,128)(2,1)S(1)}, bf16[128,2176]{1,0:T(8,128)(2,1)S(1)}, u32[]{:S(2)}, u32[]{:S(2)}) collective-permute-start(bf16[128,2176]{1,0:T(8,128)(2,1)S(1)} %copy-done.3), channel_id=1, source_target_pairs={{0,256},{256,0},{1,257},{257,1},{2,258},{258,2},{3,259},{259,3},{4... | collective-permute-start | bytes 1671176 | tf_op jit(solution)/shard_map/ppermute | solution.py:318
  54.0 10.4 %collective-permute-done.1.later_ref = bf16[128,2176]{1,0:T(8,128)(2,1)S(1)} collective-permute-done((bf16[128,2176]{1,0:T(8,128)(2,1)S(1)}, bf16[128,2176]{1,0:T(8,128)(2,1)S(1)}, u32[]{:S(2)}, u32[]{:S(2)}) %collective-permute-start.1) | collective-permute-done | bytes 557088 | tf_op jit(solution)/shard_map/ppermute | solution.py:318
  64.4 2.3 %all-to-all-done.1.own_ref = bf16[4,448,384]{2,1,0:T(8,128)(2,1)S(1)} async-done(((bf16[4,448,384]{2,1,0:T(8,128)(2,1)}), bf16[4,448,384]{2,1,0:T(8,128)(2,1)S(1)}, u32[]{:S(2)}, u32[]{:S(2)}) %all-to-all-start.1) | async-done | bytes 1376288 | tf_op jit(solution)/shard_map/all_to_all | solution.py:302
  66.7 6.5 %collective-permute-start.2 = (bf16[4,448,384]{2,1,0:T(8,128)(2,1)S(1)}, bf16[4,448,384]{2,1,0:T(8,128)(2,1)S(1)}, u32[]{:S(2)}, u32[]{:S(2)}) collective-permute-start(bf16[4,448,384]{2,1,0:T(8,128)(2,1)S(1)} %all-to-all-done.1.own_ref), channel_id=1, source_target_pairs={{0,32},{32,0},{1,33},{33,1},{2,34},{34,2},{3,35},{35,3},{4,36},{36... | collective-permute-start | bytes 4128776 | tf_op jit(solution)/shard_map/ppermute | solution.py:318
  73.2 1.4 %far.1.first_ref = bf16[128,1792]{1,0:T(8,128)(2,1)} custom-call(bf16[4,448,384]{2,1,0:T(8,128)(2,1)S(1)} %all-to-all-done.1.own_ref, bf16[128,2176]{1,0:T(8,128)(2,1)S(1)} %collective-permute-done.1.later_ref), custom_call_target="tpu_custom_call" | custom-call | flops 176160768 | bytes 1146880 | tf_op jit(solution)/shard_map/far/pallas_call | solution.py:368
  74.6 1.4 %collective-permute-done.2.other_ref = bf16[4,448,384]{2,1,0:T(8,128)(2,1)S(1)} collective-permute-done((bf16[4,448,384]{2,1,0:T(8,128)(2,1)S(1)}, bf16[4,448,384]{2,1,0:T(8,128)(2,1)S(1)}, u32[]{:S(2)}, u32[]{:S(2)}) %collective-permute-start.2) | collective-permute-done | bytes 1376288 | tf_op jit(solution)/shard_map/ppermute | solution.py:318
  75.9 2.5 %far_rest.1 = bf16[128,3584]{1,0:T(8,128)(2,1)} custom-call(bf16[4,448,384]{2,1,0:T(8,128)(2,1)S(1)} %collective-permute-done.2.other_ref, bf16[128,2176]{1,0:T(8,128)(2,1)S(1)} %collective-permute-done.1.later_ref, bf16[128,1792]{1,0:T(8,128)(2,1)} %far.1.first_ref), custom_call_target="tpu_custom_call" | custom-call | flops 176160768 | bytes 1146880 | tf_op jit(solution)/shard_map/far_rest/pallas_call | solution.py:368
  78.4 2.2 %collective-permute-start.3 = (bf16[128,3584]{1,0:T(8,128)(2,1)}, bf16[128,3584]{1,0:T(8,128)(2,1)}, u32[]{:S(2)}, u32[]{:S(2)}) collective-permute-start(bf16[128,3584]{1,0:T(8,128)(2,1)} %far_rest.1), channel_id=1, source_target_pairs={{0,256},{256,0},{1,257},{257,1},{2,258},{258,2},{3,259},{259,3},{4... | collective-permute-start | bytes 2752520 | tf_op jit(solution)/shard_map/ppermute | solution.py:318
  80.6 3.6 %values.1 = (f32[128,384]{1,0:T(8,128)}, bf16[128,768]{1,0:T(8,128)(2,1)}, f32[16,3,128]{2,1,0:T(4,128)}) custom-call(bf16[4,448,384]{2,1,0:T(8,128)(2,1)S(1)} %all-to-all-done.1.own_ref, bf16[4,448,384]{2,1,0:T(8,128)(2,1)S(1)} %collective-permute-done.2.other_ref, bf16[128,3968]{1,0:T(8,128)(2,1)} %get-tuple-element.34.keep_ref, ...), custom_call_target="tpu_custom_call" | custom-call | flops 704643072 | bytes 4587520 | tf_op jit(solution)/shard_map/values/pallas_call | solution.py:392
  84.3 4.0 %all-to-all-start.2 = ((f32[16,3,128]{2,1,0:T(4,128)}), f32[16,3,128]{2,1,0:T(4,128)S(1)}, u32[]{:S(2)}, u32[]{:S(2)}) async-start(f32[16,3,128]{2,1,0:T(4,128)} %get-tuple-element.36), calls=%async_computation.2 | async-start | bytes 65536 | tf_op jit(solution)/shard_map/all_to_all | solution.py:302
  88.3 2.8 %own.1.own_ref = bf16[128,3584]{1,0:T(8,128)(2,1)} custom-call(bf16[4,448,384]{2,1,0:T(8,128)(2,1)S(1)} %all-to-all-done.1.own_ref, bf16[4,448,384]{2,1,0:T(8,128)(2,1)S(1)} %collective-permute-done.2.other_ref, bf16[128,3968]{1,0:T(8,128)(2,1)} %get-tuple-element.34.keep_ref), custom_call_target="tpu_custom_call" | custom-call | flops 352321536 | bytes 2293760 | tf_op jit(solution)/shard_map/own/pallas_call | solution.py:413
  91.2 12.3 %all-to-all-done.2.parts_ref = f32[16,3,128]{2,1,0:T(4,128)S(1)} async-done(((f32[16,3,128]{2,1,0:T(4,128)}), f32[16,3,128]{2,1,0:T(4,128)S(1)}, u32[]{:S(2)}, u32[]{:S(2)}) %all-to-all-start.2) | async-done | bytes 24608 | tf_op jit(solution)/shard_map/all_to_all | solution.py:302
  103.5 2.2 %collective-permute-start.4 = (bf16[128,768]{1,0:T(8,128)(2,1)S(1)}, bf16[128,768]{1,0:T(8,128)(2,1)S(1)}, u32[]{:S(2)}, u32[]{:S(2)}) collective-permute-start(bf16[128,768]{1,0:T(8,128)(2,1)S(1)} %copy-done.4), channel_id=1, source_target_pairs={{0,256},{256,0},{1,257},{257,1},{2,258},{258,2},{3,259},{259,3},{4... | collective-permute-start | bytes 589832 | tf_op jit(solution)/shard_map/ppermute | solution.py:318
  106.5 9.2 %all-to-all-start.3 = ((f32[32,1,12]{2,1,0:T(1,128)}), f32[32,1,12]{2,1,0:T(1,128)S(1)}, u32[]{:S(2)}, u32[]{:S(2)}) async-start(f32[32,1,12]{2,1,0:T(1,128)} %bitcast.9), calls=%async_computation.3 | async-start | bytes 32768 | tf_op jit(solution)/shard_map/all_to_all | solution.py:302
  115.7 3.3 %finish.1 = (bf16[128,7168]{1,0:T(8,128)(2,1)}, bf16[384,128]{1,0:T(8,128)(2,1)}) custom-call(s32[2]{0:T(128)S(1)} %copy-done.2, bf16[128,3584]{1,0:T(8,128)(2,1)} %own.1.own_ref, bf16[128,3584]{1,0:T(8,128)(2,1)} %collective-permute-done.3.far_ref, bf16[128,768]{1,0:T(8,128)(2,1)S(1)} %collective-permute-done.4.got_values_ref, ...), custom_call_target="tpu_custom_call" | custom-call | flops 37748736 | bytes 3670016 | tf_op jit(solution)/shard_map/finish/pallas_call | solution.py:426
  119.0 10.4 %all-to-all-done.3 = f32[32,1,12]{2,1,0:T(1,128)S(1)} async-done(((f32[32,1,12]{2,1,0:T(1,128)}), f32[32,1,12]{2,1,0:T(1,128)S(1)}, u32[]{:S(2)}, u32[]{:S(2)}) %all-to-all-start.3) | async-done | bytes 1568 | tf_op jit(solution)/shard_map/all_to_all | solution.py:302
  (15 shorter events, 2.1 us)
Async XLA Ops:
  2.6 43.2 %all-to-all-start = ((bf16[32,2,2688]{2,1,0:T(2,128)(2,1)}), bf16[32,2,2688]{2,1,0:T(2,128)(2,1)S(1)}, u32[]{:S(2)}, u32[]{:S(2)}) async-start(bf16[32,2,2688]{2,1,0:T(2,128)(2,1)} %pack.1), calls=%async_computation | async-start | bytes 688128 | tf_op jit(solution)/shard_map/all_to_all | solution.py:302
  25.3 16.0 %collective-permute-start = (bf16[128,1792]{1,0:T(8,128)(2,1)}, bf16[128,1792]{1,0:T(8,128)(2,1)}, u32[]{:S(2)}, u32[]{:S(2)}) collective-permute-start(bf16[128,1792]{1,0:T(8,128)(2,1)} %get-tuple-element.25), channel_id=1, source_target_pairs={{0,256},{256,0},{1,257},{257,1},{2,258},{258,2},{3,259},{259,3},{4... | collective-permute-start | bytes 1376264 | tf_op jit(solution)/shard_map/ppermute | solution.py:318
  47.4 4.3 %copy-start.3 = (bf16[128,2176]{1,0:T(8,128)(2,1)S(1)}, bf16[128,2176]{1,0:T(8,128)(2,1)}, u32[]{:S(2)}) copy-start(bf16[128,2176]{1,0:T(8,128)(2,1)} %get-tuple-element.28) | copy-start | bytes 1671172
  47.4 19.3 %all-to-all-start.1 = ((bf16[4,448,384]{2,1,0:T(8,128)(2,1)}), bf16[4,448,384]{2,1,0:T(8,128)(2,1)S(1)}, u32[]{:S(2)}, u32[]{:S(2)}) async-start(bf16[4,448,384]{2,1,0:T(8,128)(2,1)} %unpack.1), calls=%async_computation.1 | async-start | bytes 2752512 | tf_op jit(solution)/shard_map/all_to_all | solution.py:302
  51.7 12.6 %collective-permute-start.1 = (bf16[128,2176]{1,0:T(8,128)(2,1)S(1)}, bf16[128,2176]{1,0:T(8,128)(2,1)S(1)}, u32[]{:S(2)}, u32[]{:S(2)}) collective-permute-start(bf16[128,2176]{1,0:T(8,128)(2,1)S(1)} %copy-done.3), channel_id=1, source_target_pairs={{0,256},{256,0},{1,257},{257,1},{2,258},{258,2},{3,259},{259,3},{4... | collective-permute-start | bytes 1671176 | tf_op jit(solution)/shard_map/ppermute | solution.py:318
  66.7 9.2 %collective-permute-start.2 = (bf16[4,448,384]{2,1,0:T(8,128)(2,1)S(1)}, bf16[4,448,384]{2,1,0:T(8,128)(2,1)S(1)}, u32[]{:S(2)}, u32[]{:S(2)}) collective-permute-start(bf16[4,448,384]{2,1,0:T(8,128)(2,1)S(1)} %all-to-all-done.1.own_ref), channel_id=1, source_target_pairs={{0,32},{32,0},{1,33},{33,1},{2,34},{34,2},{3,35},{35,3},{4,36},{36... | collective-permute-start | bytes 4128776 | tf_op jit(solution)/shard_map/ppermute | solution.py:318
  78.4 37.2 %collective-permute-start.3 = (bf16[128,3584]{1,0:T(8,128)(2,1)}, bf16[128,3584]{1,0:T(8,128)(2,1)}, u32[]{:S(2)}, u32[]{:S(2)}) collective-permute-start(bf16[128,3584]{1,0:T(8,128)(2,1)} %far_rest.1), channel_id=1, source_target_pairs={{0,256},{256,0},{1,257},{257,1},{2,258},{258,2},{3,259},{259,3},{4... | collective-permute-start | bytes 2752520 | tf_op jit(solution)/shard_map/ppermute | solution.py:318
  84.3 19.2 %all-to-all-start.2 = ((f32[16,3,128]{2,1,0:T(4,128)}), f32[16,3,128]{2,1,0:T(4,128)S(1)}, u32[]{:S(2)}, u32[]{:S(2)}) async-start(f32[16,3,128]{2,1,0:T(4,128)} %get-tuple-element.36), calls=%async_computation.2 | async-start | bytes 65536 | tf_op jit(solution)/shard_map/all_to_all | solution.py:302
  88.3 15.2 %copy-start.4 = (bf16[128,768]{1,0:T(8,128)(2,1)S(1)}, bf16[128,768]{1,0:T(8,128)(2,1)}, u32[]{:S(2)}) copy-start(bf16[128,768]{1,0:T(8,128)(2,1)} %get-tuple-element.40) | copy-start | bytes 589828
  88.3 27.4 %copy-start.2 = (s32[2]{0:T(128)S(1)}, s32[2]{0:T(128)}, u32[]{:S(2)}) copy-start(s32[2]{0:T(128)} %pad_add_fusion.place_ref) | copy-start | bytes 28
  91.1 38.2 %copy-start = (s32[32,8]{0,1:T(8,128)S(1)}, s32[32,8]{0,1:T(8,128)}, u32[]{:S(2)}) copy-start(s32[32,8]{0,1:T(8,128)} %param.6) | copy-start | bytes 3076
  91.2 38.2 %copy-start.1 = (f32[32,8]{0,1:T(8,128)S(1)}, f32[32,8]{0,1:T(8,128)}, u32[]{:S(2)}) copy-start(f32[32,8]{0,1:T(8,128)} %param.7) | copy-start | bytes 3076
  103.5 12.2 %collective-permute-start.4 = (bf16[128,768]{1,0:T(8,128)(2,1)S(1)}, bf16[128,768]{1,0:T(8,128)(2,1)S(1)}, u32[]{:S(2)}, u32[]{:S(2)}) collective-permute-start(bf16[128,768]{1,0:T(8,128)(2,1)S(1)} %copy-done.4), channel_id=1, source_target_pairs={{0,256},{256,0},{1,257},{257,1},{2,258},{258,2},{3,259},{259,3},{4... | collective-permute-start | bytes 589832 | tf_op jit(solution)/shard_map/ppermute | solution.py:318
  106.5 22.9 %all-to-all-start.3 = ((f32[32,1,12]{2,1,0:T(1,128)}), f32[32,1,12]{2,1,0:T(1,128)S(1)}, u32[]{:S(2)}, u32[]{:S(2)}) async-start(f32[32,1,12]{2,1,0:T(1,128)} %bitcast.9), calls=%async_computation.3 | async-start | bytes 32768 | tf_op jit(solution)/shard_map/all_to_all | solution.py:302

commit v8 on v6

--- a/solution.py
+++ b/solution.py
@@ -117,9 +117,9 @@
         keep_ref[:, :mine] = part(far, core)
         keep_ref[:, mine:all_mine] = part(far, 1 - core)
         keep_ref[:, all_mine:] = flipped
-        far_ref[:, :mine] = part(1 - far, core)
-        far_ref[:, mine:] = flipped
-        later_ref[...] = part(1 - far, 1 - core)
+        far_ref[...] = part(1 - far, core)
+        later_ref[:, :mine] = part(1 - far, 1 - core)
+        later_ref[:, mine:] = flipped
 
     cases(place_ref, store)
 
@@ -154,7 +154,7 @@
                 for k, ref in enumerate((keep_ref.at[:, here], from_far))
             ]
         )
-    last = activations(keep_ref, far_ref, 2 * mine, mine, hidden, ready)
+    last = activations(keep_ref, later_ref, 2 * mine, mine, hidden, ready)
     for now in copies + [last]:
         for copy in now:
             copy.start()
@@ -247,23 +247,28 @@
     ).astype(BF16)
 
 
-def sum_kernel(parts_ref, out_ref):
-    sources, capacity = out_ref.shape
+def sum_kernel(far, parts_ref, out_ref):
+    near, width = out_ref.shape
     terms = jnp.sum(parts_ref[...], axis=0)
+    capacity = width // far
     rows = []
-    for c in range(capacity):
-        line, lane = divmod(c * sources, LANES)
-        rows.append(terms[line : line + 1, lane : lane + sources])
+    for f in range(far):
+        for c in range(capacity):
+            line, lane = divmod((c * far + f) * near, LANES)
+            rows.append(terms[line : line + 1, lane : lane + near])
     out_ref[...] = jnp.concatenate(rows, axis=0).T
 
 
-def gate_kernel(terms_ref, routes_ref, gates_ref, out_ref):
-    experts, capacity = terms_ref.shape
-    named, present, before = ranks(routes_ref[...], experts)
+def gate_kernel(near, terms_ref, routes_ref, gates_ref, out_ref):
+    far, _, length = terms_ref.shape
+    named, present, before = ranks(routes_ref[...], far * near)
     matched = jnp.zeros(present.shape, F32)
-    for c in range(capacity):
+    for c in range(length // near):
+        pieces = [terms_ref[f, :, near * c : near * (c + 1)] for f in range(far)]
+        row = jnp.concatenate(pieces, axis=1)
+        spread = jnp.broadcast_to(row, (8, far * near)).T[:, :1]
         here = jnp.logical_and(present, before == c)
-        matched = jnp.where(here, terms_ref[:, c : c + 1], matched)
+        matched = jnp.where(here, spread, matched)
     total = [jnp.sum(jnp.where(n, matched, 0.0), axis=0, keepdims=True) for n in named]
     out_ref[...] = jnp.concatenate(total, axis=0) / gates_ref[...]
 
@@ -301,7 +306,8 @@
 
 
 def on_device(grad_out, routes, gates, hidden, w_down):
-    experts, rows_y = lax.axis_size("expert"), lax.axis_size("y")
+    near, far = lax.axis_size("near"), lax.axis_size("far")
+    experts, rows_y = near * far, lax.axis_size("y")
     _, slots, units = hidden.shape
     width = w_down.shape[2]
     capacity = slots // experts
@@ -322,14 +328,14 @@
         out_specs=whole(),
         name="pack",
     )(grad_out, routes, gates)
-    arrived = swap_all(packed, "expert")
+    arrived = swap_all(packed, ("far", "near"))
 
     keep, to_far, to_far_later, order = pl.pallas_call(
         functools.partial(split_kernel, experts),
         out_shape=(
             bf16((units, 2 * mine + slots)),
+            bf16((units, mine)),
             bf16((units, mine + slots)),
-            bf16((units, mine)),
             bf16((slots, slots)),
         ),
         in_specs=[scalar(), whole(), whole()],
@@ -369,13 +375,13 @@
     down_own, back_own = pl.pallas_call(
         down_kernel,
         out_shape=(bf16((units, mine)), bf16((units, mine))),
-        in_specs=[whole(), stays(), stays()],
+        in_specs=[whole(), stays(), whole()],
         out_specs=(whole(),) * 2,
         scratch_shapes=scratch,
         compiler_params=limit(16),
         cost_estimate=cost(flops // 2, moved // 2),
         name="down",
-    )(dispatched, keep, from_far)
+    )(dispatched, keep, later)
     from_core, back_own = lax.optimization_barrier((from_core, back_own))
     got_own = other(back_own, "x")
 
@@ -402,13 +408,13 @@
     down_other, back_other = pl.pallas_call(
         rest_kernel,
         out_shape=(bf16((units, mine)), bf16((units, mine + 2 * slots))),
-        in_specs=[whole()] + [stays()] * 2 + [whole()],
+        in_specs=[whole(), stays(), whole(), whole()],
         out_specs=(whole(),) * 2,
         scratch_shapes=scratch,
         compiler_params=limit(16),
         cost_estimate=cost(flops // 2, moved // 2),
         name="rest",
-    )(in_vmem(from_core), keep, from_far, in_hbm(theirs))
+    )(in_vmem(from_core), keep, later, in_hbm(theirs))
     parts, back_other, got_own = lax.optimization_barrier((parts, back_other, got_own))
     got_other = other(back_other, "x")
 
@@ -434,17 +440,19 @@
     )
 
     sums = pl.pallas_call(
-        sum_kernel,
-        out_shape=jax.ShapeDtypeStruct((experts, capacity), F32),
+        functools.partial(sum_kernel, far),
+        out_shape=jax.ShapeDtypeStruct((near, far * capacity), F32),
         in_specs=[whole()],
         out_specs=whole(),
         compiler_params=limit(4),
         name="sum",
     )(parts)
-    returned = swap_all(sums, "expert")
+    returned = swap_all(sums, "near")
+    returned = returned.reshape(near, far, capacity).transpose(1, 2, 0)
+    returned = swap_all(returned.reshape(far, 1, capacity * near), "far")
     returned, _ = lax.optimization_barrier((returned, d_hidden))
     d_gate = pl.pallas_call(
-        gate_kernel,
+        functools.partial(gate_kernel, near),
         out_shape=jax.ShapeDtypeStruct(gates.shape, F32),
         in_specs=[whole()] * 3,
         out_specs=whole(),
@@ -456,17 +464,17 @@
 
 def solution(mesh):
     parts, experts = mesh.devices.shape
-    devices = mesh.devices.reshape(2, parts // 4, 2, experts)
-    finer = Mesh(devices, ("x", "y", "core", "expert"))
-    dp = ("x", "y", "core")
+    devices = mesh.devices.reshape(2, parts // 4, 2, 2, experts // 2)
+    finer = Mesh(devices, ("x", "y", "core", "far", "near"))
+    dp, expert = ("x", "y", "core"), ("far", "near")
     in_specs = (
-        P("expert", dp),
-        P("expert", None),
-        P("expert", None),
-        P("expert", None, dp),
-        P("expert", dp, None),
+        P(expert, dp),
+        P(expert, None),
+        P(expert, None),
+        P(expert, None, dp),
+        P(expert, dp, None),
     )
-    out_specs = (P("expert", None, dp), P("expert", dp, None), P("expert", None))
+    out_specs = (P(expert, None, dp), P(expert, dp, None), P(expert, None))
     return jax.shard_map(
         on_device, mesh=finer, in_specs=in_specs, out_specs=out_specs, check_vma=False
     )

time: 121 us -> 125 us (1.033); the launches traced: 120 us -> 123 us
  blocking collectives: 0 us -> 17.2 us
  waiting for transfers between devices: 43.8 us -> 34.3 us
  starting transfers between devices: 53.5 us -> 46.6 us
  local copies, waits for them, and re-layouts: 0.02 us -> 1.37 us
    all_to_all x0 -> x1, blocking collectives: none -> 17.2 us  [swap_all(): return lax.all_to_all(x, axis, split_axis=0, concat_axis=0, tiled=True)]
    all_to_all x4, starting transfers between devices: 38.2 us -> 31.3 us  [swap_all(): return lax.all_to_all(x, axis, split_axis=0, concat_axis=0, tiled=True)]
    all_to_all x4, waiting for transfers between devices: 15.8 us -> 10 us  [swap_all(): return lax.all_to_all(x, axis, split_axis=0, concat_axis=0, tiled=True)]
    ppermute x5, waiting for transfers between devices: 27.9 us -> 24.3 us  [other(): return lax.ppermute(x, axis, [(0, 1), (1, 0)])]
  transfers between devices with their start and end apart: 9 -> 9, of which waited for: 8 -> 7; matrix products, arithmetic and copies ran while one was open for 0% -> 2% of each run, Pallas kernels for 14% -> 14%
where the time goes in v8:
time: 125 us; the launch traced here: 123 us
  starting transfers between devices  46.6 us (37%)
  waiting for transfers between devices  34.3 us (27%)
  Pallas kernels  21.2 us (17%)
  blocking collectives  17.2 us (14%)
  local copies, waits for them, and re-layouts  1.37 us (1%)
  other arithmetic  1.28 us (1%)
    all_to_all x4, starting transfers between devices, swap_all(): return lax.all_to_all(x, axis, split_axis=0, concat_axis=0, tiled=True)  31.3 us
    ppermute x5, waiting for transfers between devices, other(): return lax.ppermute(x, axis, [(0, 1), (1, 0)])  24.3 us
    all_to_all x1, blocking collectives, swap_all(): return lax.all_to_all(x, axis, split_axis=0, concat_axis=0, tiled=True)  17.2 us
    ppermute x5, starting transfers between devices, other(): return lax.ppermute(x, axis, [(0, 1), (1, 0)])  15.3 us
    all_to_all x4, waiting for transfers between devices, swap_all(): return lax.all_to_all(x, axis, split_axis=0, concat_axis=0, tiled=True)  10 us
    pallas_call x1, Pallas kernels, on_device(): pl.pallas_call(values_kernel, out_shape=(f32((units, slots)), f32((units,...  3.63 us
    pallas_call x1, Pallas kernels, on_device(): pl.pallas_call(functools.partial(split_kernel, experts), out_shape=(bf16(...  3.62 us
    pallas_call x1, Pallas kernels, on_device(): pl.pallas_call(rest_kernel, out_shape=(bf16((units, mine)), bf16((units,...  3.55 us
  transfers between devices with their start and end apart: 9, of which 7 were waited for; matrix products, arithmetic and copies ran while one was open for 2% of the time, Pallas kernels for 14%

profile of v8, /device:TPU:1, one launch (start us, length us, event | category | flops | bytes accessed | tf_op | source)
XLA Modules:
  0.0 122.7 jit_solution(2143562661200570864)
XLA Ops:
  0.6 2.0 %pack.1 = bf16[32,2,2688]{2,1,0:T(2,128)(2,1)} custom-call(bf16[32,448]{1,0:T(8,128)(2,1)} %grad_ref.1, s32[8,32]{1,0:T(8,128)} %bitcast.14, f32[8,32]{1,0:T(8,128)} %bitcast.16), custom_call_target="tpu_custom_call" | custom-call | tf_op jit(solution)/shard_map/pack/pallas_call | solution.py:324
  2.6 18.5 %all-to-all-start = ((bf16[32,2,2688]{2,1,0:T(2,128)(2,1)}), bf16[32,2,2688]{2,1,0:T(2,128)(2,1)S(1)}, u32[]{:S(2)}, u32[]{:S(2)}) async-start(bf16[32,2,2688]{2,1,0:T(2,128)(2,1)} %pack.1), calls=%async_computation | async-start | bytes 688128 | tf_op jit(solution)/shard_map/all_to_all | solution.py:305
  21.8 3.6 %split.1 = (bf16[128,3968]{1,0:T(8,128)(2,1)}, bf16[128,1792]{1,0:T(8,128)(2,1)}, bf16[128,2176]{1,0:T(8,128)(2,1)}, bf16[384,384]{1,0:T(8,128)(2,1)}) custom-call(s32[2]{0:T(128)} %pad_add_fusion.place_ref, bf16[128,7168]{1,0:T(8,128)(2,1)} %bitcast.18, bf16[384,128]{1,0:T(8,128)(2,1)} %bitcast.19), custom_call_target="tpu_custom_call" | custom-call | flops 37748736 | bytes 3670016 | tf_op jit(solution)/shard_map/split/pallas_call | solution.py:333
  25.4 2.2 %collective-permute-start = (bf16[128,1792]{1,0:T(8,128)(2,1)}, bf16[128,1792]{1,0:T(8,128)(2,1)}, u32[]{:S(2)}, u32[]{:S(2)}) collective-permute-start(bf16[128,1792]{1,0:T(8,128)(2,1)} %get-tuple-element.27), channel_id=1, source_target_pairs={{0,256},{256,0},{1,257},{257,1},{2,258},{258,2},{3,259},{259,3},{4... | collective-permute-start | bytes 1376264 | tf_op jit(solution)/shard_map/ppermute | solution.py:322
  27.6 13.7 %collective-permute-done.far_ref = bf16[128,1792]{1,0:T(8,128)(2,1)} collective-permute-done((bf16[128,1792]{1,0:T(8,128)(2,1)}, bf16[128,1792]{1,0:T(8,128)(2,1)}, u32[]{:S(2)}, u32[]{:S(2)}) %collective-permute-start) | collective-permute-done | bytes 458784 | tf_op jit(solution)/shard_map/ppermute | solution.py:322
  41.3 4.5 %all-to-all-done.in_ref = bf16[32,2,2688]{2,1,0:T(2,128)(2,1)S(1)} async-done(((bf16[32,2,2688]{2,1,0:T(2,128)(2,1)}), bf16[32,2,2688]{2,1,0:T(2,128)(2,1)S(1)}, u32[]{:S(2)}, u32[]{:S(2)}) %all-to-all-start) | async-done | bytes 344096 | tf_op jit(solution)/shard_map/all_to_all | solution.py:305
  45.8 1.6 %unpack.1 = bf16[4,448,384]{2,1,0:T(8,128)(2,1)} custom-call(bf16[32,2,2688]{2,1,0:T(2,128)(2,1)S(1)} %all-to-all-done.in_ref), custom_call_target="tpu_custom_call" | custom-call | tf_op jit(solution)/shard_map/unpack/pallas_call | solution.py:352
  47.4 4.3 %all-to-all-start.1 = ((bf16[4,448,384]{2,1,0:T(8,128)(2,1)}), bf16[4,448,384]{2,1,0:T(8,128)(2,1)S(1)}, u32[]{:S(2)}, u32[]{:S(2)}) async-start(bf16[4,448,384]{2,1,0:T(8,128)(2,1)} %unpack.1), calls=%async_computation.1 | async-start | bytes 2752512 | tf_op jit(solution)/shard_map/all_to_all | solution.py:305
  51.8 2.2 %collective-permute-start.1 = (bf16[128,2176]{1,0:T(8,128)(2,1)S(1)}, bf16[128,2176]{1,0:T(8,128)(2,1)S(1)}, u32[]{:S(2)}, u32[]{:S(2)}) collective-permute-start(bf16[128,2176]{1,0:T(8,128)(2,1)S(1)} %copy-done.3), channel_id=1, source_target_pairs={{0,256},{256,0},{1,257},{257,1},{2,258},{258,2},{3,259},{259,3},{4... | collective-permute-start | bytes 1671176 | tf_op jit(solution)/shard_map/ppermute | solution.py:322
  54.0 10.4 %collective-permute-done.1.far_ref.later_ref = bf16[128,2176]{1,0:T(8,128)(2,1)S(1)} collective-permute-done((bf16[128,2176]{1,0:T(8,128)(2,1)S(1)}, bf16[128,2176]{1,0:T(8,128)(2,1)S(1)}, u32[]{:S(2)}, u32[]{:S(2)}) %collective-permute-start.1) | collective-permute-done | bytes 557088 | tf_op jit(solution)/shard_map/ppermute | solution.py:322
  64.4 2.3 %all-to-all-done.1.disp_ref.own_ref = bf16[4,448,384]{2,1,0:T(8,128)(2,1)S(1)} async-done(((bf16[4,448,384]{2,1,0:T(8,128)(2,1)}), bf16[4,448,384]{2,1,0:T(8,128)(2,1)S(1)}, u32[]{:S(2)}, u32[]{:S(2)}) %all-to-all-start.1) | async-done | bytes 1376288 | tf_op jit(solution)/shard_map/all_to_all | solution.py:305
  66.7 6.5 %collective-permute-start.2 = (bf16[4,448,384]{2,1,0:T(8,128)(2,1)S(1)}, bf16[4,448,384]{2,1,0:T(8,128)(2,1)S(1)}, u32[]{:S(2)}, u32[]{:S(2)}) collective-permute-start(bf16[4,448,384]{2,1,0:T(8,128)(2,1)S(1)} %all-to-all-done.1.disp_ref.own_ref), channel_id=1, source_target_pairs={{0,32},{32,0},{1,33},{33,1},{2,34},{34,2},{3,35},{35,3},{4,36},{36... | collective-permute-start | bytes 4128776 | tf_op jit(solution)/shard_map/ppermute | solution.py:322
  73.2 2.6 %down.1 = (bf16[128,1792]{1,0:T(8,128)(2,1)}, bf16[128,1792]{1,0:T(8,128)(2,1)}) custom-call(bf16[4,448,384]{2,1,0:T(8,128)(2,1)S(1)} %all-to-all-done.1.disp_ref.own_ref, bf16[128,3968]{1,0:T(8,128)(2,1)} %get-tuple-element.32.keep_ref, bf16[128,2176]{1,0:T(8,128)(2,1)S(1)} %collective-permute-done.1.far_ref.later_ref), custom_call_target="tpu_custom_call" | custom-call | flops 352321536 | bytes 2293760 | tf_op jit(solution)/shard_map/down/pallas_call | solution.py:375
  76.0 2.2 %collective-permute-start.3 = (bf16[128,1792]{1,0:T(8,128)(2,1)}, bf16[128,1792]{1,0:T(8,128)(2,1)}, u32[]{:S(2)}, u32[]{:S(2)}) collective-permute-start(bf16[128,1792]{1,0:T(8,128)(2,1)} %get-tuple-element.42), channel_id=1, source_target_pairs={{0,256},{256,0},{1,257},{257,1},{2,258},{258,2},{3,259},{259,3},{4... | collective-permute-start | bytes 1376264 | tf_op jit(solution)/shard_map/ppermute | solution.py:322
  78.2 3.6 %values.1 = (f32[128,384]{1,0:T(8,128)}, f32[128,384]{1,0:T(8,128)}, f32[16,3,128]{2,1,0:T(4,128)}) custom-call(bf16[4,448,384]{2,1,0:T(8,128)(2,1)S(1)} %all-to-all-done.1.disp_ref.own_ref, bf16[4,448,384]{2,1,0:T(8,128)(2,1)S(1)} %collective-permute-done.2.other_ref.disp_ref, bf16[128,3968]{1,0:T(8,128)(2,1)} %get-tuple-element.32.keep_ref, ...), custom_call_target="tpu_custom_call" | custom-call | flops 704643072 | bytes 4587520 | tf_op jit(solution)/shard_map/values/pallas_call | solution.py:388
  81.8 4.0 %all-to-all-start.2 = ((f32[16,3,128]{2,1,0:T(4,128)}), f32[16,3,128]{2,1,0:T(4,128)S(1)}, u32[]{:S(2)}, u32[]{:S(2)}) async-start(f32[16,3,128]{2,1,0:T(4,128)} %get-tuple-element.40), calls=%async_computation.2 | async-start | bytes 65536 | tf_op jit(solution)/shard_map/all_to_all | solution.py:305
  85.8 3.5 %rest.1 = (bf16[128,1792]{1,0:T(8,128)(2,1)}, bf16[128,2560]{1,0:T(8,128)(2,1)}) custom-call(bf16[4,448,384]{2,1,0:T(8,128)(2,1)S(1)} %collective-permute-done.2.other_ref.disp_ref, bf16[128,3968]{1,0:T(8,128)(2,1)} %get-tuple-element.32.keep_ref, bf16[128,2176]{1,0:T(8,128)(2,1)S(1)} %collective-permute-done.1.far_ref.later_ref, ...), custom_call_target="tpu_custom_call" | custom-call | flops 352321536 | bytes 2293760 | tf_op jit(solution)/shard_map/rest/pallas_call | solution.py:408
  89.4 2.2 %all-to-all-done.2.parts_ref = f32[16,3,128]{2,1,0:T(4,128)S(1)} async-done(((f32[16,3,128]{2,1,0:T(4,128)}), f32[16,3,128]{2,1,0:T(4,128)S(1)}, u32[]{:S(2)}, u32[]{:S(2)}) %all-to-all-start.2) | async-done | bytes 24608 | tf_op jit(solution)/shard_map/all_to_all | solution.py:305
  91.6 2.2 %collective-permute-start.4 = (bf16[128,2560]{1,0:T(8,128)(2,1)}, bf16[128,2560]{1,0:T(8,128)(2,1)S(1)}, u32[]{:S(2)}, u32[]{:S(2)}) collective-permute-start(bf16[128,2560]{1,0:T(8,128)(2,1)} %get-tuple-element.44), channel_id=1, source_target_pairs={{0,256},{256,0},{1,257},{257,1},{2,258},{258,2},{3,259},{259,3},{4... | collective-permute-start | bytes 1966088 | tf_op jit(solution)/shard_map/ppermute | solution.py:322
  94.0 17.2 %all_to_all.29 = f32[16,1,24]{2,1,0:T(1,128)S(1)} all-to-all(f32[16,1,24]{2,1,0:T(1,128)S(1)} %bitcast.13), channel_id=1, replica_groups=mesh['x'=2,'y'=4,'core'=2,'far'=2,'near'=16] {'near'}, dimensions={0} | all-to-all | bytes 3072 | tf_op jit(solution)/shard_map/all_to_all | solution.py:305
  113.2 4.5 %all-to-all-start.4 = ((f32[2,1,192]{2,1,0:T(1,128)}), f32[2,1,192]{2,1,0:T(1,128)S(1)}, u32[]{:S(2)}, u32[]{:S(2)}) async-start(f32[2,1,192]{2,1,0:T(1,128)} %reshape.17), calls=%async_computation.4 | async-start | bytes 4096 | tf_op jit(solution)/shard_map/all_to_all | solution.py:305
  117.7 3.2 %finish.1 = (bf16[128,7168]{1,0:T(8,128)(2,1)}, bf16[384,128]{1,0:T(8,128)(2,1)}) custom-call(s32[2]{0:T(128)S(1)} %copy-done.2, bf16[128,1792]{1,0:T(8,128)(2,1)} %get-tuple-element.34.own_ref, bf16[128,1792]{1,0:T(8,128)(2,1)} %get-tuple-element.39.other_ref, bf16[128,1792]{1,0:T(8,128)(2,1)} %collective-permute-done.3.got_own_ref, ...), custom_call_target="tpu_custom_call" | custom-call | flops 37748736 | bytes 3670016 | tf_op jit(solution)/shard_map/finish/pallas_call | solution.py:421
  120.9 1.0 all-to-all-done.4.terms_ref
  121.8 0.9 match.1
  (18 shorter events, 3.0 us)
Async XLA Ops:
  2.6 43.2 %all-to-all-start = ((bf16[32,2,2688]{2,1,0:T(2,128)(2,1)}), bf16[32,2,2688]{2,1,0:T(2,128)(2,1)S(1)}, u32[]{:S(2)}, u32[]{:S(2)}) async-start(bf16[32,2,2688]{2,1,0:T(2,128)(2,1)} %pack.1), calls=%async_computation | async-start | bytes 688128 | tf_op jit(solution)/shard_map/all_to_all | solution.py:305
  25.4 16.0 %collective-permute-start = (bf16[128,1792]{1,0:T(8,128)(2,1)}, bf16[128,1792]{1,0:T(8,128)(2,1)}, u32[]{:S(2)}, u32[]{:S(2)}) collective-permute-start(bf16[128,1792]{1,0:T(8,128)(2,1)} %get-tuple-element.27), channel_id=1, source_target_pairs={{0,256},{256,0},{1,257},{257,1},{2,258},{258,2},{3,259},{259,3},{4... | collective-permute-start | bytes 1376264 | tf_op jit(solution)/shard_map/ppermute | solution.py:322
  47.4 4.3 %copy-start.3 = (bf16[128,2176]{1,0:T(8,128)(2,1)S(1)}, bf16[128,2176]{1,0:T(8,128)(2,1)}, u32[]{:S(2)}) copy-start(bf16[128,2176]{1,0:T(8,128)(2,1)} %get-tuple-element.30) | copy-start | bytes 1671172
  47.4 19.3 %all-to-all-start.1 = ((bf16[4,448,384]{2,1,0:T(8,128)(2,1)}), bf16[4,448,384]{2,1,0:T(8,128)(2,1)S(1)}, u32[]{:S(2)}, u32[]{:S(2)}) async-start(bf16[4,448,384]{2,1,0:T(8,128)(2,1)} %unpack.1), calls=%async_computation.1 | async-start | bytes 2752512 | tf_op jit(solution)/shard_map/all_to_all | solution.py:305
  51.8 12.6 %collective-permute-start.1 = (bf16[128,2176]{1,0:T(8,128)(2,1)S(1)}, bf16[128,2176]{1,0:T(8,128)(2,1)S(1)}, u32[]{:S(2)}, u32[]{:S(2)}) collective-permute-start(bf16[128,2176]{1,0:T(8,128)(2,1)S(1)} %copy-done.3), channel_id=1, source_target_pairs={{0,256},{256,0},{1,257},{257,1},{2,258},{258,2},{3,259},{259,3},{4... | collective-permute-start | bytes 1671176 | tf_op jit(solution)/shard_map/ppermute | solution.py:322
  66.7 9.2 %collective-permute-start.2 = (bf16[4,448,384]{2,1,0:T(8,128)(2,1)S(1)}, bf16[4,448,384]{2,1,0:T(8,128)(2,1)S(1)}, u32[]{:S(2)}, u32[]{:S(2)}) collective-permute-start(bf16[4,448,384]{2,1,0:T(8,128)(2,1)S(1)} %all-to-all-done.1.disp_ref.own_ref), channel_id=1, source_target_pairs={{0,32},{32,0},{1,33},{33,1},{2,34},{34,2},{3,35},{35,3},{4,36},{36... | collective-permute-start | bytes 4128776 | tf_op jit(solution)/shard_map/ppermute | solution.py:322
  76.0 15.7 %collective-permute-start.3 = (bf16[128,1792]{1,0:T(8,128)(2,1)}, bf16[128,1792]{1,0:T(8,128)(2,1)}, u32[]{:S(2)}, u32[]{:S(2)}) collective-permute-start(bf16[128,1792]{1,0:T(8,128)(2,1)} %get-tuple-element.42), channel_id=1, source_target_pairs={{0,256},{256,0},{1,257},{257,1},{2,258},{258,2},{3,259},{259,3},{4... | collective-permute-start | bytes 1376264 | tf_op jit(solution)/shard_map/ppermute | solution.py:322
  81.8 9.8 %all-to-all-start.2 = ((f32[16,3,128]{2,1,0:T(4,128)}), f32[16,3,128]{2,1,0:T(4,128)S(1)}, u32[]{:S(2)}, u32[]{:S(2)}) async-start(f32[16,3,128]{2,1,0:T(4,128)} %get-tuple-element.40), calls=%async_computation.2 | async-start | bytes 65536 | tf_op jit(solution)/shard_map/all_to_all | solution.py:305
  85.8 31.9 %copy-start.2 = (s32[2]{0:T(128)S(1)}, s32[2]{0:T(128)}, u32[]{:S(2)}) copy-start(s32[2]{0:T(128)} %pad_add_fusion.place_ref) | copy-start | bytes 28
  89.4 32.5 %copy-start = (s32[32,8]{0,1:T(8,128)S(1)}, s32[32,8]{0,1:T(8,128)}, u32[]{:S(2)}) copy-start(s32[32,8]{0,1:T(8,128)} %param.6) | copy-start | bytes 3076
  89.4 32.4 %copy-start.1 = (f32[32,8]{0,1:T(8,128)S(1)}, f32[32,8]{0,1:T(8,128)}, u32[]{:S(2)}) copy-start(f32[32,8]{0,1:T(8,128)} %param.7) | copy-start | bytes 3076
  91.6 26.1 %collective-permute-start.4 = (bf16[128,2560]{1,0:T(8,128)(2,1)}, bf16[128,2560]{1,0:T(8,128)(2,1)S(1)}, u32[]{:S(2)}, u32[]{:S(2)}) collective-permute-start(bf16[128,2560]{1,0:T(8,128)(2,1)} %get-tuple-element.44), channel_id=1, source_target_pairs={{0,256},{256,0},{1,257},{257,1},{2,258},{258,2},{3,259},{259,3},{4... | collective-permute-start | bytes 1966088 | tf_op jit(solution)/shard_map/ppermute | solution.py:322
  113.2 8.6 %all-to-all-start.4 = ((f32[2,1,192]{2,1,0:T(1,128)}), f32[2,1,192]{2,1,0:T(1,128)S(1)}, u32[]{:S(2)}, u32[]{:S(2)}) async-start(f32[2,1,192]{2,1,0:T(1,128)} %reshape.17), calls=%async_computation.4 | async-start | bytes 4096 | tf_op jit(solution)/shard_map/all_to_all | solution.py:305

commit v9 on v8

--- a/solution.py
+++ b/solution.py
@@ -125,6 +125,8 @@
 
 
 def values_kernel(
+    far,
+    capacity,
     own_ref,
     other_ref,
     keep_ref,
@@ -172,8 +174,13 @@
     terms = jnp.sum(left * values, axis=0, keepdims=True)
     mine_ref[...] = values[:units]
     theirs_ref[...] = values[units:]
-    lines = [terms[:, i : i + LANES] for i in range(0, slots, LANES)]
-    gate_ref[...] = jnp.broadcast_to(jnp.concatenate(lines, axis=0), gate_ref.shape)
+    copies, near = gate_ref.shape[0] // far, gate_ref.shape[2] // capacity
+    for f in range(far):
+        starts = [(c * far + f) * near for c in range(capacity)]
+        row = jnp.concatenate([terms[:, i : i + near] for i in starts], axis=1)
+        gate_ref[f * copies : (f + 1) * copies] = jnp.broadcast_to(
+            row[None], (copies, *row.shape)
+        )
 
 
 def activations(keep_ref, far_ref, keep_start, far_start, hidden, ready):
@@ -249,26 +256,26 @@
 
 def sum_kernel(far, parts_ref, out_ref):
     near, width = out_ref.shape
-    terms = jnp.sum(parts_ref[...], axis=0)
-    capacity = width // far
+    copies = parts_ref.shape[0] // far
     rows = []
     for f in range(far):
-        for c in range(capacity):
-            line, lane = divmod((c * far + f) * near, LANES)
-            rows.append(terms[line : line + 1, lane : lane + near])
+        terms = jnp.sum(parts_ref[f * copies : (f + 1) * copies], axis=0)
+        for c in range(width // far):
+            rows.append(terms[:, near * c : near * (c + 1)])
     out_ref[...] = jnp.concatenate(rows, axis=0).T
 
 
-def gate_kernel(near, terms_ref, routes_ref, gates_ref, out_ref):
-    far, _, length = terms_ref.shape
+def gate_kernel(far, terms_ref, routes_ref, gates_ref, out_ref):
+    near, width = terms_ref.shape
+    capacity = width // far
     named, present, before = ranks(routes_ref[...], far * near)
     matched = jnp.zeros(present.shape, F32)
-    for c in range(length // near):
-        pieces = [terms_ref[f, :, near * c : near * (c + 1)] for f in range(far)]
-        row = jnp.concatenate(pieces, axis=1)
-        spread = jnp.broadcast_to(row, (8, far * near)).T[:, :1]
+    for c in range(capacity):
+        columns = [
+            terms_ref[:, f * capacity + c : f * capacity + c + 1] for f in range(far)
+        ]
         here = jnp.logical_and(present, before == c)
-        matched = jnp.where(here, spread, matched)
+        matched = jnp.where(here, jnp.concatenate(columns, axis=0), matched)
     total = [jnp.sum(jnp.where(n, matched, 0.0), axis=0, keepdims=True) for n in named]
     out_ref[...] = jnp.concatenate(total, axis=0) / gates_ref[...]
 
@@ -386,11 +393,11 @@
     got_own = other(back_own, "x")
 
     mine_values, theirs, terms = pl.pallas_call(
-        values_kernel,
+        functools.partial(values_kernel, far, capacity),
         out_shape=(
             f32((units, slots)),
             f32((units, slots)),
-            jax.ShapeDtypeStruct((4 * rows_y, slots // LANES, LANES), F32),
+            jax.ShapeDtypeStruct((far * 4 * rows_y, 1, capacity * near), F32),
         ),
         in_specs=[whole()] * 2 + [stays()] * 2 + [whole()],
         out_specs=(whole(),) * 3,
@@ -403,7 +410,7 @@
         cost_estimate=cost(flops, moved),
         name="values",
     )(dispatched, in_vmem(from_core), keep, from_far, later)
-    parts = swap_all(terms, ("x", "y", "core"))
+    parts = swap_all(terms, ("far", "x", "y", "core"))
 
     down_other, back_other = pl.pallas_call(
         rest_kernel,
@@ -448,11 +455,9 @@
         name="sum",
     )(parts)
     returned = swap_all(sums, "near")
-    returned = returned.reshape(near, far, capacity).transpose(1, 2, 0)
-    returned = swap_all(returned.reshape(far, 1, capacity * near), "far")
     returned, _ = lax.optimization_barrier((returned, d_hidden))
     d_gate = pl.pallas_call(
-        functools.partial(gate_kernel, near),
+        functools.partial(gate_kernel, far),
         out_shape=jax.ShapeDtypeStruct(gates.shape, F32),
         in_specs=[whole()] * 3,
         out_specs=whole(),

time: 125 us -> 117 us (0.936); the launches traced: 123 us -> 116 us
  blocking collectives: 17.2 us -> 0 us
  waiting for transfers between devices: 34.3 us -> 43 us
  starting transfers between devices: 46.6 us -> 50.3 us
  local copies, waits for them, and re-layouts: 1.37 us -> 0.02 us
    all_to_all x1 -> x0, blocking collectives: 17.2 us -> none  [swap_all(): return lax.all_to_all(x, axis, split_axis=0, concat_axis=0, tiled=True)]
    ppermute x5, waiting for transfers between devices: 24.3 us -> 31.3 us  [other(): return lax.ppermute(x, axis, [(0, 1), (1, 0)])]
    all_to_all x4, starting transfers between devices: 31.3 us -> 35 us  [swap_all(): return lax.all_to_all(x, axis, split_axis=0, concat_axis=0, tiled=True)]
    all_to_all x4, waiting for transfers between devices: 10 us -> 11.7 us  [swap_all(): return lax.all_to_all(x, axis, split_axis=0, concat_axis=0, tiled=True)]
  transfers between devices with their start and end apart: 9 -> 9, of which waited for: 7 -> 8; matrix products, arithmetic and copies ran while one was open for 2% -> 1% of each run, Pallas kernels for 14% -> 15%
where the time goes in v9:
time: 117 us; the launch traced here: 116 us
  starting transfers between devices  50.3 us (43%)
  waiting for transfers between devices  43 us (37%)
  Pallas kernels  21.7 us (19%)
    all_to_all x4, starting transfers between devices, swap_all(): return lax.all_to_all(x, axis, split_axis=0, concat_axis=0, tiled=True)  35 us
    ppermute x5, waiting for transfers between devices, other(): return lax.ppermute(x, axis, [(0, 1), (1, 0)])  31.3 us
    ppermute x5, starting transfers between devices, other(): return lax.ppermute(x, axis, [(0, 1), (1, 0)])  15.3 us
    all_to_all x4, waiting for transfers between devices, swap_all(): return lax.all_to_all(x, axis, split_axis=0, concat_axis=0, tiled=True)  11.7 us
    pallas_call x1, Pallas kernels, on_device(): pl.pallas_call(functools.partial(values_kernel, far, capacity), out_shape...  3.61 us
    pallas_call x1, Pallas kernels, on_device(): pl.pallas_call(functools.partial(split_kernel, experts), out_shape=(bf16(...  3.61 us
    pallas_call x1, Pallas kernels, on_device(): pl.pallas_call(rest_kernel, out_shape=(bf16((units, mine)), bf16((units,...  3.55 us
    pallas_call x1, Pallas kernels, on_device(): pl.pallas_call(finish_kernel, out_shape=(jax.ShapeDtypeStruct((units, wid...  3.17 us
  transfers between devices with their start and end apart: 9, of which 8 were waited for; matrix products, arithmetic and copies ran while one was open for 1% of the time, Pallas kernels for 15%

profile of v9, /device:TPU:1, one launch (start us, length us, event | category | flops | bytes accessed | tf_op | source)
XLA Modules:
  0.0 116.5 jit_solution(12756979252443095295)
XLA Ops:
  0.6 2.0 %pack.1 = bf16[32,2,2688]{2,1,0:T(2,128)(2,1)} custom-call(bf16[32,448]{1,0:T(8,128)(2,1)} %grad_ref.1, s32[8,32]{1,0:T(8,128)} %bitcast.14, f32[8,32]{1,0:T(8,128)} %bitcast.16), custom_call_target="tpu_custom_call" | custom-call | tf_op jit(solution)/shard_map/pack/pallas_call | solution.py:331
  2.7 18.5 %all-to-all-start = ((bf16[32,2,2688]{2,1,0:T(2,128)(2,1)}), bf16[32,2,2688]{2,1,0:T(2,128)(2,1)S(1)}, u32[]{:S(2)}, u32[]{:S(2)}) async-start(bf16[32,2,2688]{2,1,0:T(2,128)(2,1)} %pack.1), calls=%async_computation | async-start | bytes 688128 | tf_op jit(solution)/shard_map/all_to_all | solution.py:312
  21.8 3.6 %split.1 = (bf16[128,3968]{1,0:T(8,128)(2,1)}, bf16[128,1792]{1,0:T(8,128)(2,1)}, bf16[128,2176]{1,0:T(8,128)(2,1)}, bf16[384,384]{1,0:T(8,128)(2,1)}) custom-call(s32[2]{0:T(128)} %pad_add_fusion.place_ref, bf16[128,7168]{1,0:T(8,128)(2,1)} %bitcast.18, bf16[384,128]{1,0:T(8,128)(2,1)} %bitcast.19), custom_call_target="tpu_custom_call" | custom-call | flops 37748736 | bytes 3670016 | tf_op jit(solution)/shard_map/split/pallas_call | solution.py:340
  25.4 2.2 %collective-permute-start = (bf16[128,1792]{1,0:T(8,128)(2,1)}, bf16[128,1792]{1,0:T(8,128)(2,1)}, u32[]{:S(2)}, u32[]{:S(2)}) collective-permute-start(bf16[128,1792]{1,0:T(8,128)(2,1)} %get-tuple-element.27), channel_id=1, source_target_pairs={{0,256},{256,0},{1,257},{257,1},{2,258},{258,2},{3,259},{259,3},{4... | collective-permute-start | bytes 1376264 | tf_op jit(solution)/shard_map/ppermute | solution.py:329
  27.6 13.7 %collective-permute-done.far_ref = bf16[128,1792]{1,0:T(8,128)(2,1)} collective-permute-done((bf16[128,1792]{1,0:T(8,128)(2,1)}, bf16[128,1792]{1,0:T(8,128)(2,1)}, u32[]{:S(2)}, u32[]{:S(2)}) %collective-permute-start) | collective-permute-done | bytes 458784 | tf_op jit(solution)/shard_map/ppermute | solution.py:329
  41.4 4.5 %all-to-all-done.in_ref = bf16[32,2,2688]{2,1,0:T(2,128)(2,1)S(1)} async-done(((bf16[32,2,2688]{2,1,0:T(2,128)(2,1)}), bf16[32,2,2688]{2,1,0:T(2,128)(2,1)S(1)}, u32[]{:S(2)}, u32[]{:S(2)}) %all-to-all-start) | async-done | bytes 344096 | tf_op jit(solution)/shard_map/all_to_all | solution.py:312
  45.9 1.6 %unpack.1 = bf16[4,448,384]{2,1,0:T(8,128)(2,1)} custom-call(bf16[32,2,2688]{2,1,0:T(2,128)(2,1)S(1)} %all-to-all-done.in_ref), custom_call_target="tpu_custom_call" | custom-call | tf_op jit(solution)/shard_map/unpack/pallas_call | solution.py:359
  47.4 4.3 %all-to-all-start.1 = ((bf16[4,448,384]{2,1,0:T(8,128)(2,1)}), bf16[4,448,384]{2,1,0:T(8,128)(2,1)S(1)}, u32[]{:S(2)}, u32[]{:S(2)}) async-start(bf16[4,448,384]{2,1,0:T(8,128)(2,1)} %unpack.1), calls=%async_computation.1 | async-start | bytes 2752512 | tf_op jit(solution)/shard_map/all_to_all | solution.py:312
  51.8 2.2 %collective-permute-start.1 = (bf16[128,2176]{1,0:T(8,128)(2,1)S(1)}, bf16[128,2176]{1,0:T(8,128)(2,1)S(1)}, u32[]{:S(2)}, u32[]{:S(2)}) collective-permute-start(bf16[128,2176]{1,0:T(8,128)(2,1)S(1)} %copy-done.3), channel_id=1, source_target_pairs={{0,256},{256,0},{1,257},{257,1},{2,258},{258,2},{3,259},{259,3},{4... | collective-permute-start | bytes 1671176 | tf_op jit(solution)/shard_map/ppermute | solution.py:329
  54.0 10.4 %collective-permute-done.1.far_ref.later_ref = bf16[128,2176]{1,0:T(8,128)(2,1)S(1)} collective-permute-done((bf16[128,2176]{1,0:T(8,128)(2,1)S(1)}, bf16[128,2176]{1,0:T(8,128)(2,1)S(1)}, u32[]{:S(2)}, u32[]{:S(2)}) %collective-permute-start.1) | collective-permute-done | bytes 557088 | tf_op jit(solution)/shard_map/ppermute | solution.py:329
  64.4 2.3 %all-to-all-done.1.disp_ref.own_ref = bf16[4,448,384]{2,1,0:T(8,128)(2,1)S(1)} async-done(((bf16[4,448,384]{2,1,0:T(8,128)(2,1)}), bf16[4,448,384]{2,1,0:T(8,128)(2,1)S(1)}, u32[]{:S(2)}, u32[]{:S(2)}) %all-to-all-start.1) | async-done | bytes 1376288 | tf_op jit(solution)/shard_map/all_to_all | solution.py:312
  66.7 6.5 %collective-permute-start.2 = (bf16[4,448,384]{2,1,0:T(8,128)(2,1)S(1)}, bf16[4,448,384]{2,1,0:T(8,128)(2,1)S(1)}, u32[]{:S(2)}, u32[]{:S(2)}) collective-permute-start(bf16[4,448,384]{2,1,0:T(8,128)(2,1)S(1)} %all-to-all-done.1.disp_ref.own_ref), channel_id=1, source_target_pairs={{0,32},{32,0},{1,33},{33,1},{2,34},{34,2},{3,35},{35,3},{4,36},{36... | collective-permute-start | bytes 4128776 | tf_op jit(solution)/shard_map/ppermute | solution.py:329
  73.2 2.6 %down.1 = (bf16[128,1792]{1,0:T(8,128)(2,1)}, bf16[128,1792]{1,0:T(8,128)(2,1)}) custom-call(bf16[4,448,384]{2,1,0:T(8,128)(2,1)S(1)} %all-to-all-done.1.disp_ref.own_ref, bf16[128,3968]{1,0:T(8,128)(2,1)} %get-tuple-element.32.keep_ref, bf16[128,2176]{1,0:T(8,128)(2,1)S(1)} %collective-permute-done.1.far_ref.later_ref), custom_call_target="tpu_custom_call" | custom-call | flops 352321536 | bytes 2293760 | tf_op jit(solution)/shard_map/down/pallas_call | solution.py:382
  76.0 2.2 %collective-permute-start.3 = (bf16[128,1792]{1,0:T(8,128)(2,1)}, bf16[128,1792]{1,0:T(8,128)(2,1)}, u32[]{:S(2)}, u32[]{:S(2)}) collective-permute-start(bf16[128,1792]{1,0:T(8,128)(2,1)} %get-tuple-element.42), channel_id=1, source_target_pairs={{0,256},{256,0},{1,257},{257,1},{2,258},{258,2},{3,259},{259,3},{4... | collective-permute-start | bytes 1376264 | tf_op jit(solution)/shard_map/ppermute | solution.py:329
  78.2 3.6 %values.1 = (f32[128,384]{1,0:T(8,128)}, f32[128,384]{1,0:T(8,128)}, f32[32,1,192]{2,1,0:T(1,128)}) custom-call(bf16[4,448,384]{2,1,0:T(8,128)(2,1)S(1)} %all-to-all-done.1.disp_ref.own_ref, bf16[4,448,384]{2,1,0:T(8,128)(2,1)S(1)} %collective-permute-done.2.other_ref.disp_ref, bf16[128,3968]{1,0:T(8,128)(2,1)} %get-tuple-element.32.keep_ref, ...), custom_call_target="tpu_custom_call" | custom-call | flops 704643072 | bytes 4587520 | tf_op jit(solution)/shard_map/values/pallas_call | solution.py:395
  81.8 4.2 %all-to-all-start.2 = ((f32[32,1,192]{2,1,0:T(1,128)}), f32[32,1,192]{2,1,0:T(1,128)S(1)}, u32[]{:S(2)}, u32[]{:S(2)}) async-start(f32[32,1,192]{2,1,0:T(1,128)} %get-tuple-element.40), calls=%async_computation.2 | async-start | bytes 65536 | tf_op jit(solution)/shard_map/all_to_all | solution.py:312
  86.0 3.6 %rest.1 = (bf16[128,1792]{1,0:T(8,128)(2,1)}, bf16[128,2560]{1,0:T(8,128)(2,1)}) custom-call(bf16[4,448,384]{2,1,0:T(8,128)(2,1)S(1)} %collective-permute-done.2.other_ref.disp_ref, bf16[128,3968]{1,0:T(8,128)(2,1)} %get-tuple-element.32.keep_ref, bf16[128,2176]{1,0:T(8,128)(2,1)S(1)} %collective-permute-done.1.far_ref.later_ref, ...), custom_call_target="tpu_custom_call" | custom-call | flops 352321536 | bytes 2293760 | tf_op jit(solution)/shard_map/rest/pallas_call | solution.py:415
  89.6 3.8 %all-to-all-done.2.parts_ref = f32[32,1,192]{2,1,0:T(1,128)S(1)} async-done(((f32[32,1,192]{2,1,0:T(1,128)}), f32[32,1,192]{2,1,0:T(1,128)S(1)}, u32[]{:S(2)}, u32[]{:S(2)}) %all-to-all-start.2) | async-done | bytes 24608 | tf_op jit(solution)/shard_map/all_to_all | solution.py:312
  93.4 2.2 %collective-permute-start.4 = (bf16[128,2560]{1,0:T(8,128)(2,1)}, bf16[128,2560]{1,0:T(8,128)(2,1)S(1)}, u32[]{:S(2)}, u32[]{:S(2)}) collective-permute-start(bf16[128,2560]{1,0:T(8,128)(2,1)} %get-tuple-element.44), channel_id=1, source_target_pairs={{0,256},{256,0},{1,257},{257,1},{2,258},{258,2},{3,259},{259,3},{4... | collective-permute-start | bytes 1966088 | tf_op jit(solution)/shard_map/ppermute | solution.py:329
  96.4 8.0 %all-to-all-start.3 = ((f32[16,1,24]{2,1,0:T(1,128)}), f32[16,1,24]{2,1,0:T(1,128)S(1)}, u32[]{:S(2)}, u32[]{:S(2)}) async-start(f32[16,1,24]{2,1,0:T(1,128)} %bitcast.9), calls=%async_computation.3 | async-start | bytes 16384 | tf_op jit(solution)/shard_map/all_to_all | solution.py:312
  104.4 7.0 %collective-permute-done.4.got_other_ref = bf16[128,2560]{1,0:T(8,128)(2,1)S(1)} collective-permute-done((bf16[128,2560]{1,0:T(8,128)(2,1)}, bf16[128,2560]{1,0:T(8,128)(2,1)S(1)}, u32[]{:S(2)}, u32[]{:S(2)}) %collective-permute-start.4) | collective-permute-done | bytes 655392 | tf_op jit(solution)/shard_map/ppermute | solution.py:329
  111.4 3.2 %finish.1 = (bf16[128,7168]{1,0:T(8,128)(2,1)}, bf16[384,128]{1,0:T(8,128)(2,1)}) custom-call(s32[2]{0:T(128)S(1)} %copy-done.2, bf16[128,1792]{1,0:T(8,128)(2,1)} %get-tuple-element.34.own_ref, bf16[128,1792]{1,0:T(8,128)(2,1)} %get-tuple-element.39.other_ref, bf16[128,1792]{1,0:T(8,128)(2,1)} %collective-permute-done.3.got_own_ref, ...), custom_call_target="tpu_custom_call" | custom-call | flops 37748736 | bytes 3670016 | tf_op jit(solution)/shard_map/finish/pallas_call | solution.py:428
  114.6 1.1 all-to-all-done.3
  115.7 0.8 match.1
  (12 shorter events, 1.6 us)
Async XLA Ops:
  2.7 43.2 %all-to-all-start = ((bf16[32,2,2688]{2,1,0:T(2,128)(2,1)}), bf16[32,2,2688]{2,1,0:T(2,128)(2,1)S(1)}, u32[]{:S(2)}, u32[]{:S(2)}) async-start(bf16[32,2,2688]{2,1,0:T(2,128)(2,1)} %pack.1), calls=%async_computation | async-start | bytes 688128 | tf_op jit(solution)/shard_map/all_to_all | solution.py:312
  25.4 16.0 %collective-permute-start = (bf16[128,1792]{1,0:T(8,128)(2,1)}, bf16[128,1792]{1,0:T(8,128)(2,1)}, u32[]{:S(2)}, u32[]{:S(2)}) collective-permute-start(bf16[128,1792]{1,0:T(8,128)(2,1)} %get-tuple-element.27), channel_id=1, source_target_pairs={{0,256},{256,0},{1,257},{257,1},{2,258},{258,2},{3,259},{259,3},{4... | collective-permute-start | bytes 1376264 | tf_op jit(solution)/shard_map/ppermute | solution.py:329
  47.4 4.3 %copy-start.3 = (bf16[128,2176]{1,0:T(8,128)(2,1)S(1)}, bf16[128,2176]{1,0:T(8,128)(2,1)}, u32[]{:S(2)}) copy-start(bf16[128,2176]{1,0:T(8,128)(2,1)} %get-tuple-element.30) | copy-start | bytes 1671172
  47.4 19.3 %all-to-all-start.1 = ((bf16[4,448,384]{2,1,0:T(8,128)(2,1)}), bf16[4,448,384]{2,1,0:T(8,128)(2,1)S(1)}, u32[]{:S(2)}, u32[]{:S(2)}) async-start(bf16[4,448,384]{2,1,0:T(8,128)(2,1)} %unpack.1), calls=%async_computation.1 | async-start | bytes 2752512 | tf_op jit(solution)/shard_map/all_to_all | solution.py:312
  51.8 12.6 %collective-permute-start.1 = (bf16[128,2176]{1,0:T(8,128)(2,1)S(1)}, bf16[128,2176]{1,0:T(8,128)(2,1)S(1)}, u32[]{:S(2)}, u32[]{:S(2)}) collective-permute-start(bf16[128,2176]{1,0:T(8,128)(2,1)S(1)} %copy-done.3), channel_id=1, source_target_pairs={{0,256},{256,0},{1,257},{257,1},{2,258},{258,2},{3,259},{259,3},{4... | collective-permute-start | bytes 1671176 | tf_op jit(solution)/shard_map/ppermute | solution.py:329
  66.7 9.2 %collective-permute-start.2 = (bf16[4,448,384]{2,1,0:T(8,128)(2,1)S(1)}, bf16[4,448,384]{2,1,0:T(8,128)(2,1)S(1)}, u32[]{:S(2)}, u32[]{:S(2)}) collective-permute-start(bf16[4,448,384]{2,1,0:T(8,128)(2,1)S(1)} %all-to-all-done.1.disp_ref.own_ref), channel_id=1, source_target_pairs={{0,32},{32,0},{1,33},{33,1},{2,34},{34,2},{3,35},{35,3},{4,36},{36... | collective-permute-start | bytes 4128776 | tf_op jit(solution)/shard_map/ppermute | solution.py:329
  76.0 17.4 %collective-permute-start.3 = (bf16[128,1792]{1,0:T(8,128)(2,1)}, bf16[128,1792]{1,0:T(8,128)(2,1)}, u32[]{:S(2)}, u32[]{:S(2)}) collective-permute-start(bf16[128,1792]{1,0:T(8,128)(2,1)} %get-tuple-element.42), channel_id=1, source_target_pairs={{0,256},{256,0},{1,257},{257,1},{2,258},{258,2},{3,259},{259,3},{4... | collective-permute-start | bytes 1376264 | tf_op jit(solution)/shard_map/ppermute | solution.py:329
  81.8 11.6 %all-to-all-start.2 = ((f32[32,1,192]{2,1,0:T(1,128)}), f32[32,1,192]{2,1,0:T(1,128)S(1)}, u32[]{:S(2)}, u32[]{:S(2)}) async-start(f32[32,1,192]{2,1,0:T(1,128)} %get-tuple-element.40), calls=%async_computation.2 | async-start | bytes 65536 | tf_op jit(solution)/shard_map/all_to_all | solution.py:312
  86.0 25.4 %copy-start.2 = (s32[2]{0:T(128)S(1)}, s32[2]{0:T(128)}, u32[]{:S(2)}) copy-start(s32[2]{0:T(128)} %pad_add_fusion.place_ref) | copy-start | bytes 28
  89.5 26.1 %copy-start = (s32[32,8]{0,1:T(8,128)S(1)}, s32[32,8]{0,1:T(8,128)}, u32[]{:S(2)}) copy-start(s32[32,8]{0,1:T(8,128)} %param.6) | copy-start | bytes 3076
  89.6 26.1 %copy-start.1 = (f32[32,8]{0,1:T(8,128)S(1)}, f32[32,8]{0,1:T(8,128)}, u32[]{:S(2)}) copy-start(f32[32,8]{0,1:T(8,128)} %param.7) | copy-start | bytes 3076
  93.4 18.0 %collective-permute-start.4 = (bf16[128,2560]{1,0:T(8,128)(2,1)}, bf16[128,2560]{1,0:T(8,128)(2,1)S(1)}, u32[]{:S(2)}, u32[]{:S(2)}) collective-permute-start(bf16[128,2560]{1,0:T(8,128)(2,1)} %get-tuple-element.44), channel_id=1, source_target_pairs={{0,256},{256,0},{1,257},{257,1},{2,258},{258,2},{3,259},{259,3},{4... | collective-permute-start | bytes 1966088 | tf_op jit(solution)/shard_map/ppermute | solution.py:329
  96.4 19.3 %all-to-all-start.3 = ((f32[16,1,24]{2,1,0:T(1,128)}), f32[16,1,24]{2,1,0:T(1,128)S(1)}, u32[]{:S(2)}, u32[]{:S(2)}) async-start(f32[16,1,24]{2,1,0:T(1,128)} %bitcast.9), calls=%async_computation.3 | async-start | bytes 16384 | tf_op jit(solution)/shard_map/all_to_all | solution.py:312

commit v10 on v9

--- a/solution.py
+++ b/solution.py
@@ -191,39 +191,42 @@
     ]
 
 
-def down_kernel(disp_ref, keep_ref, far_ref, mine_ref, send_ref, hidden, ready):
+def down(left, disp_ref, out_ref, first):
     blocks, share, slots = disp_ref.shape
-    units, wide, mine = hidden.shape[1], 2 * share, blocks * share
-    copies = activations(keep_ref, far_ref, 2 * mine, mine, hidden, ready)
-    for copy in copies:
-        copy.start()
-    for copy in copies:
-        copy.wait()
-    left = hidden[...].reshape(2 * units, slots)
+    wide = 2 * share
     for step in range(blocks // 2):
         block = disp_ref[2 * step : 2 * step + 2].reshape(wide, slots)
-        down = lax.dot_general(
+        part = lax.dot_general(
             left, block, (((1,), (1,)), ((), ())), preferred_element_type=F32
-        ).astype(BF16)
-        mine_ref[:, wide * step : wide * (step + 1)] = down[:units]
-        send_ref[:, wide * step : wide * (step + 1)] = down[units:]
+        )
+        start = first + wide * step
+        out_ref[:, start : start + wide] = part.astype(BF16)
+
+
+def far_kernel(own_ref, later_ref, out_ref):
+    down(later_ref[:, out_ref.shape[1] :], own_ref, out_ref, 0)
 
 
 def rest_kernel(
-    disp_ref, keep_ref, far_ref, values_ref, mine_ref, send_ref, hidden, ready
+    own_ref, other_ref, keep_ref, later_ref, values_ref, mine_ref, send_ref, hidden, done
 ):
-    down_kernel(disp_ref, keep_ref, far_ref, mine_ref, send_ref, hidden, ready)
-    mine, slots = mine_ref.shape[1], values_ref.shape[1]
+    mine, slots = mine_ref.shape[1] // 2, values_ref.shape[1]
+    after = pl.ds(2 * mine, slots)
+    copy = pltpu.make_async_copy(keep_ref.at[:, after], hidden, done)
+    copy.start()
+    down(later_ref[:, mine:], other_ref, send_ref, 0)
     values = values_ref[...]
     high = values.astype(BF16)
     send_ref[:, mine : mine + slots] = high
     send_ref[:, mine + slots :] = (values - high.astype(F32)).astype(BF16)
+    copy.wait()
+    for half, ref in enumerate((own_ref, other_ref)):
+        down(hidden[...], ref, mine_ref, half * mine)
 
 
 def finish_kernel(
     place_ref,
     own_ref,
-    other_ref,
     got_own_ref,
     got_other_ref,
     values_ref,
@@ -232,16 +235,19 @@
     dhid_ref,
 ):
     slots = values_ref.shape[1]
-    mine = own_ref.shape[1]
+    mine = got_own_ref.shape[1]
     blocks = 4
     share = mine // blocks
 
     def store(far, core):
         for f in range(2):
-            refs = (own_ref, other_ref) if f == far else (got_own_ref, got_other_ref)
+            refs = ((own_ref, 0), (own_ref, mine))
+            if f != far:
+                refs = ((got_own_ref, 0), (got_other_ref, 0))
             refs = refs if core == 0 else refs[::-1]
             for y in range(blocks):
-                pair = [ref[:, share * y : share * (y + 1)] for ref in refs]
+                starts = [(ref, first + share * y) for ref, first in refs]
+                pair = [ref[:, start : start + share] for ref, start in starts]
                 start = 2 * share * (f * blocks + y)
                 down_ref[:, start : start + 2 * share] = jnp.concatenate(pair, axis=1)
 
@@ -379,17 +385,16 @@
         pltpu.VMEM((2, units, slots), BF16),
         pltpu.SemaphoreType.DMA((2,)),
     ]
-    down_own, back_own = pl.pallas_call(
-        down_kernel,
-        out_shape=(bf16((units, mine)), bf16((units, mine))),
-        in_specs=[whole(), stays(), whole()],
-        out_specs=(whole(),) * 2,
-        scratch_shapes=scratch,
+    back_own = pl.pallas_call(
+        far_kernel,
+        out_shape=bf16((units, mine)),
+        in_specs=[whole()] * 2,
+        out_specs=whole(),
         compiler_params=limit(16),
-        cost_estimate=cost(flops // 2, moved // 2),
-        name="down",
-    )(dispatched, keep, later)
-    from_core, back_own = lax.optimization_barrier((from_core, back_own))
+        cost_estimate=cost(flops // 4, moved // 4),
+        name="far",
+    )(dispatched, later)
+    from_core, _ = lax.optimization_barrier((from_core, back_own))
     got_own = other(back_own, "x")
 
     mine_values, theirs, terms = pl.pallas_call(
@@ -412,16 +417,16 @@
     )(dispatched, in_vmem(from_core), keep, from_far, later)
     parts = swap_all(terms, ("far", "x", "y", "core"))
 
-    down_other, back_other = pl.pallas_call(
+    down_mine, back_other = pl.pallas_call(
         rest_kernel,
-        out_shape=(bf16((units, mine)), bf16((units, mine + 2 * slots))),
-        in_specs=[whole(), stays(), whole(), whole()],
+        out_shape=(bf16((units, 2 * mine)), bf16((units, mine + 2 * slots))),
+        in_specs=[whole()] * 2 + [stays()] + [whole()] * 2,
         out_specs=(whole(),) * 2,
-        scratch_shapes=scratch,
+        scratch_shapes=[pltpu.VMEM((units, slots), BF16), pltpu.SemaphoreType.DMA],
         compiler_params=limit(16),
-        cost_estimate=cost(flops // 2, moved // 2),
+        cost_estimate=cost(3 * flops // 4, moved // 2),
         name="rest",
-    )(in_vmem(from_core), keep, later, in_hbm(theirs))
+    )(dispatched, in_vmem(from_core), keep, later, in_hbm(theirs))
     parts, back_other, got_own = lax.optimization_barrier((parts, back_other, got_own))
     got_other = other(back_other, "x")
 
@@ -431,15 +436,14 @@
             jax.ShapeDtypeStruct((units, width), BF16),
             jax.ShapeDtypeStruct((slots, units), BF16),
         ),
-        in_specs=[scalar()] + [whole()] * 6,
+        in_specs=[scalar()] + [whole()] * 5,
         out_specs=(whole(),) * 2,
         compiler_params=limit(16),
         cost_estimate=cost(2 * units * slots * slots, 4 * units * width),
         name="finish",
     )(
         place,
-        in_hbm(down_own),
-        in_hbm(down_other),
+        in_hbm(down_mine),
         in_vmem(got_own),
         in_vmem(got_other),
         in_hbm(mine_values),

time: 117 us -> 116 us (level)
  transfers between devices with their start and end apart: 9 -> 9, of which waited for: 8 -> 8; matrix products, arithmetic and copies ran while one was open for 1% -> 1% of each run, Pallas kernels for 15% -> 14%
where the time goes in v10:
time: 116 us; the launch traced here: 115 us
  starting transfers between devices  49.9 us (43%)
  waiting for transfers between devices  42.7 us (37%)
  Pallas kernels  20.6 us (18%)
    all_to_all x4, starting transfers between devices, swap_all(): return lax.all_to_all(x, axis, split_axis=0, concat_axis=0, tiled=True)  34.6 us
    ppermute x5, waiting for transfers between devices, other(): return lax.ppermute(x, axis, [(0, 1), (1, 0)])  32.1 us
    ppermute x5, starting transfers between devices, other(): return lax.ppermute(x, axis, [(0, 1), (1, 0)])  15.3 us
    all_to_all x4, waiting for transfers between devices, swap_all(): return lax.all_to_all(x, axis, split_axis=0, concat_axis=0, tiled=True)  10.6 us
    pallas_call x1, Pallas kernels, on_device(): pl.pallas_call(rest_kernel, out_shape=(bf16((units, 2 * mine)), bf16((uni...  3.78 us
    pallas_call x1, Pallas kernels, on_device(): pl.pallas_call(functools.partial(split_kernel, experts), out_shape=(bf16(...  3.62 us
    pallas_call x1, Pallas kernels, on_device(): pl.pallas_call(functools.partial(values_kernel, far, capacity), out_shape...  3.61 us
    pallas_call x1, Pallas kernels, on_device(): pl.pallas_call(finish_kernel, out_shape=(jax.ShapeDtypeStruct((units, wid...  3.13 us
  transfers between devices with their start and end apart: 9, of which 8 were waited for; matrix products, arithmetic and copies ran while one was open for 1% of the time, Pallas kernels for 14%

profile of v10, /device:TPU:1, one launch (start us, length us, event | category | flops | bytes accessed | tf_op | source)
XLA Modules:
  0.0 114.5 jit_solution(14215402663785324310)
XLA Ops:
  0.6 2.0 %pack.1 = bf16[32,2,2688]{2,1,0:T(2,128)(2,1)} custom-call(bf16[32,448]{1,0:T(8,128)(2,1)} %grad_ref.1, s32[8,32]{1,0:T(8,128)} %bitcast.14, f32[8,32]{1,0:T(8,128)} %bitcast.16), custom_call_target="tpu_custom_call" | custom-call | tf_op jit(solution)/shard_map/pack/pallas_call | solution.py:337
  2.6 18.5 %all-to-all-start = ((bf16[32,2,2688]{2,1,0:T(2,128)(2,1)}), bf16[32,2,2688]{2,1,0:T(2,128)(2,1)S(1)}, u32[]{:S(2)}, u32[]{:S(2)}) async-start(bf16[32,2,2688]{2,1,0:T(2,128)(2,1)} %pack.1), calls=%async_computation | async-start | bytes 688128 | tf_op jit(solution)/shard_map/all_to_all | solution.py:318
  21.7 3.6 %split.1 = (bf16[128,3968]{1,0:T(8,128)(2,1)}, bf16[128,1792]{1,0:T(8,128)(2,1)}, bf16[128,2176]{1,0:T(8,128)(2,1)}, bf16[384,384]{1,0:T(8,128)(2,1)}) custom-call(s32[2]{0:T(128)} %pad_add_fusion.place_ref, bf16[128,7168]{1,0:T(8,128)(2,1)} %bitcast.18, bf16[384,128]{1,0:T(8,128)(2,1)} %bitcast.19), custom_call_target="tpu_custom_call" | custom-call | flops 37748736 | bytes 3670016 | tf_op jit(solution)/shard_map/split/pallas_call | solution.py:346
  25.3 2.2 %collective-permute-start = (bf16[128,1792]{1,0:T(8,128)(2,1)}, bf16[128,1792]{1,0:T(8,128)(2,1)}, u32[]{:S(2)}, u32[]{:S(2)}) collective-permute-start(bf16[128,1792]{1,0:T(8,128)(2,1)} %get-tuple-element.24), channel_id=1, source_target_pairs={{0,256},{256,0},{1,257},{257,1},{2,258},{258,2},{3,259},{259,3},{4... | collective-permute-start | bytes 1376264 | tf_op jit(solution)/shard_map/ppermute | solution.py:335
  27.6 13.7 %collective-permute-done.far_ref = bf16[128,1792]{1,0:T(8,128)(2,1)} collective-permute-done((bf16[128,1792]{1,0:T(8,128)(2,1)}, bf16[128,1792]{1,0:T(8,128)(2,1)}, u32[]{:S(2)}, u32[]{:S(2)}) %collective-permute-start) | collective-permute-done | bytes 458784 | tf_op jit(solution)/shard_map/ppermute | solution.py:335
  41.3 4.5 %all-to-all-done.in_ref = bf16[32,2,2688]{2,1,0:T(2,128)(2,1)S(1)} async-done(((bf16[32,2,2688]{2,1,0:T(2,128)(2,1)}), bf16[32,2,2688]{2,1,0:T(2,128)(2,1)S(1)}, u32[]{:S(2)}, u32[]{:S(2)}) %all-to-all-start) | async-done | bytes 344096 | tf_op jit(solution)/shard_map/all_to_all | solution.py:318
  45.8 1.6 %unpack.1 = bf16[4,448,384]{2,1,0:T(8,128)(2,1)} custom-call(bf16[32,2,2688]{2,1,0:T(2,128)(2,1)S(1)} %all-to-all-done.in_ref), custom_call_target="tpu_custom_call" | custom-call | tf_op jit(solution)/shard_map/unpack/pallas_call | solution.py:365
  47.4 4.3 %all-to-all-start.1 = ((bf16[4,448,384]{2,1,0:T(8,128)(2,1)}), bf16[4,448,384]{2,1,0:T(8,128)(2,1)S(1)}, u32[]{:S(2)}, u32[]{:S(2)}) async-start(bf16[4,448,384]{2,1,0:T(8,128)(2,1)} %unpack.1), calls=%async_computation.1 | async-start | bytes 2752512 | tf_op jit(solution)/shard_map/all_to_all | solution.py:318
  51.7 2.2 %collective-permute-start.1 = (bf16[128,2176]{1,0:T(8,128)(2,1)S(1)}, bf16[128,2176]{1,0:T(8,128)(2,1)S(1)}, u32[]{:S(2)}, u32[]{:S(2)}) collective-permute-start(bf16[128,2176]{1,0:T(8,128)(2,1)S(1)} %copy-done.3), channel_id=1, source_target_pairs={{0,256},{256,0},{1,257},{257,1},{2,258},{258,2},{3,259},{259,3},{4... | collective-permute-start | bytes 1671176 | tf_op jit(solution)/shard_map/ppermute | solution.py:335
  54.0 10.4 %collective-permute-done.1.later_ref = bf16[128,2176]{1,0:T(8,128)(2,1)S(1)} collective-permute-done((bf16[128,2176]{1,0:T(8,128)(2,1)S(1)}, bf16[128,2176]{1,0:T(8,128)(2,1)S(1)}, u32[]{:S(2)}, u32[]{:S(2)}) %collective-permute-start.1) | collective-permute-done | bytes 557088 | tf_op jit(solution)/shard_map/ppermute | solution.py:335
  64.4 2.3 %all-to-all-done.1.own_ref = bf16[4,448,384]{2,1,0:T(8,128)(2,1)S(1)} async-done(((bf16[4,448,384]{2,1,0:T(8,128)(2,1)}), bf16[4,448,384]{2,1,0:T(8,128)(2,1)S(1)}, u32[]{:S(2)}, u32[]{:S(2)}) %all-to-all-start.1) | async-done | bytes 1376288 | tf_op jit(solution)/shard_map/all_to_all | solution.py:318
  66.7 6.5 %collective-permute-start.2 = (bf16[4,448,384]{2,1,0:T(8,128)(2,1)S(1)}, bf16[4,448,384]{2,1,0:T(8,128)(2,1)S(1)}, u32[]{:S(2)}, u32[]{:S(2)}) collective-permute-start(bf16[4,448,384]{2,1,0:T(8,128)(2,1)S(1)} %all-to-all-done.1.own_ref), channel_id=1, source_target_pairs={{0,32},{32,0},{1,33},{33,1},{2,34},{34,2},{3,35},{35,3},{4,36},{36... | collective-permute-start | bytes 4128776 | tf_op jit(solution)/shard_map/ppermute | solution.py:335
  73.2 1.3 %far.1 = bf16[128,1792]{1,0:T(8,128)(2,1)} custom-call(bf16[4,448,384]{2,1,0:T(8,128)(2,1)S(1)} %all-to-all-done.1.own_ref, bf16[128,2176]{1,0:T(8,128)(2,1)S(1)} %collective-permute-done.1.later_ref), custom_call_target="tpu_custom_call" | custom-call | flops 176160768 | bytes 1146880 | tf_op jit(solution)/shard_map/far/pallas_call | solution.py:388
  74.5 2.2 %collective-permute-start.3 = (bf16[128,1792]{1,0:T(8,128)(2,1)}, bf16[128,1792]{1,0:T(8,128)(2,1)}, u32[]{:S(2)}, u32[]{:S(2)}) collective-permute-start(bf16[128,1792]{1,0:T(8,128)(2,1)} %far.1), channel_id=1, source_target_pairs={{0,256},{256,0},{1,257},{257,1},{2,258},{258,2},{3,259},{259,3},{4... | collective-permute-start | bytes 1376264 | tf_op jit(solution)/shard_map/ppermute | solution.py:335
  76.7 3.6 %values.1 = (f32[128,384]{1,0:T(8,128)}, f32[128,384]{1,0:T(8,128)}, f32[32,1,192]{2,1,0:T(1,128)}) custom-call(bf16[4,448,384]{2,1,0:T(8,128)(2,1)S(1)} %all-to-all-done.1.own_ref, bf16[4,448,384]{2,1,0:T(8,128)(2,1)S(1)} %collective-permute-done.2.other_ref, bf16[128,3968]{1,0:T(8,128)(2,1)} %get-tuple-element.31.keep_ref, ...), custom_call_target="tpu_custom_call" | custom-call | flops 704643072 | bytes 4587520 | tf_op jit(solution)/shard_map/values/pallas_call | solution.py:400
  80.4 3.8 %all-to-all-start.2 = ((f32[32,1,192]{2,1,0:T(1,128)}), f32[32,1,192]{2,1,0:T(1,128)S(1)}, u32[]{:S(2)}, u32[]{:S(2)}) async-start(f32[32,1,192]{2,1,0:T(1,128)} %get-tuple-element.35), calls=%async_computation.2 | async-start | bytes 65536 | tf_op jit(solution)/shard_map/all_to_all | solution.py:318
  84.2 3.8 %rest.1 = (bf16[128,3584]{1,0:T(8,128)(2,1)}, bf16[128,2560]{1,0:T(8,128)(2,1)}) custom-call(bf16[4,448,384]{2,1,0:T(8,128)(2,1)S(1)} %all-to-all-done.1.own_ref, bf16[4,448,384]{2,1,0:T(8,128)(2,1)S(1)} %collective-permute-done.2.other_ref, bf16[128,3968]{1,0:T(8,128)(2,1)} %get-tuple-element.31.keep_ref, ...), custom_call_target="tpu_custom_call" | custom-call | flops 528482304 | bytes 2293760 | tf_op jit(solution)/shard_map/rest/pallas_call | solution.py:420
  88.0 0.9 collective-permute-done.3.got_own_ref
  88.9 2.7 %all-to-all-done.2.parts_ref = f32[32,1,192]{2,1,0:T(1,128)S(1)} async-done(((f32[32,1,192]{2,1,0:T(1,128)}), f32[32,1,192]{2,1,0:T(1,128)S(1)}, u32[]{:S(2)}, u32[]{:S(2)}) %all-to-all-start.2) | async-done | bytes 24608 | tf_op jit(solution)/shard_map/all_to_all | solution.py:318
  91.6 2.2 %collective-permute-start.4 = (bf16[128,2560]{1,0:T(8,128)(2,1)}, bf16[128,2560]{1,0:T(8,128)(2,1)S(1)}, u32[]{:S(2)}, u32[]{:S(2)}) collective-permute-start(bf16[128,2560]{1,0:T(8,128)(2,1)} %get-tuple-element.38), channel_id=1, source_target_pairs={{0,256},{256,0},{1,257},{257,1},{2,258},{258,2},{3,259},{259,3},{4... | collective-permute-start | bytes 1966088 | tf_op jit(solution)/shard_map/ppermute | solution.py:335
  94.6 7.9 %all-to-all-start.3 = ((f32[16,1,24]{2,1,0:T(1,128)}), f32[16,1,24]{2,1,0:T(1,128)S(1)}, u32[]{:S(2)}, u32[]{:S(2)}) async-start(f32[16,1,24]{2,1,0:T(1,128)} %bitcast.9), calls=%async_computation.3 | async-start | bytes 16384 | tf_op jit(solution)/shard_map/all_to_all | solution.py:318
  102.5 7.1 %collective-permute-done.4.got_other_ref = bf16[128,2560]{1,0:T(8,128)(2,1)S(1)} collective-permute-done((bf16[128,2560]{1,0:T(8,128)(2,1)}, bf16[128,2560]{1,0:T(8,128)(2,1)S(1)}, u32[]{:S(2)}, u32[]{:S(2)}) %collective-permute-start.4) | collective-permute-done | bytes 655392 | tf_op jit(solution)/shard_map/ppermute | solution.py:335
  109.6 3.1 %finish.1 = (bf16[128,7168]{1,0:T(8,128)(2,1)}, bf16[384,128]{1,0:T(8,128)(2,1)}) custom-call(s32[2]{0:T(128)S(1)} %copy-done.2, bf16[128,3584]{1,0:T(8,128)(2,1)} %get-tuple-element.34.own_ref, bf16[128,1792]{1,0:T(8,128)(2,1)} %collective-permute-done.3.got_own_ref, bf16[128,2560]{1,0:T(8,128)(2,1)S(1)} %collective-permute-done.4.got_other_ref, ...), custom_call_target="tpu_custom_call" | custom-call | flops 37748736 | bytes 3670016 | tf_op jit(solution)/shard_map/finish/pallas_call | solution.py:433
  112.7 1.0 all-to-all-done.3
  (12 shorter events, 2.2 us)
Async XLA Ops:
  2.6 43.2 %all-to-all-start = ((bf16[32,2,2688]{2,1,0:T(2,128)(2,1)}), bf16[32,2,2688]{2,1,0:T(2,128)(2,1)S(1)}, u32[]{:S(2)}, u32[]{:S(2)}) async-start(bf16[32,2,2688]{2,1,0:T(2,128)(2,1)} %pack.1), calls=%async_computation | async-start | bytes 688128 | tf_op jit(solution)/shard_map/all_to_all | solution.py:318
  25.3 16.0 %collective-permute-start = (bf16[128,1792]{1,0:T(8,128)(2,1)}, bf16[128,1792]{1,0:T(8,128)(2,1)}, u32[]{:S(2)}, u32[]{:S(2)}) collective-permute-start(bf16[128,1792]{1,0:T(8,128)(2,1)} %get-tuple-element.24), channel_id=1, source_target_pairs={{0,256},{256,0},{1,257},{257,1},{2,258},{258,2},{3,259},{259,3},{4... | collective-permute-start | bytes 1376264 | tf_op jit(solution)/shard_map/ppermute | solution.py:335
  47.4 4.3 %copy-start.3 = (bf16[128,2176]{1,0:T(8,128)(2,1)S(1)}, bf16[128,2176]{1,0:T(8,128)(2,1)}, u32[]{:S(2)}) copy-start(bf16[128,2176]{1,0:T(8,128)(2,1)} %get-tuple-element.27) | copy-start | bytes 1671172
  47.4 19.3 %all-to-all-start.1 = ((bf16[4,448,384]{2,1,0:T(8,128)(2,1)}), bf16[4,448,384]{2,1,0:T(8,128)(2,1)S(1)}, u32[]{:S(2)}, u32[]{:S(2)}) async-start(bf16[4,448,384]{2,1,0:T(8,128)(2,1)} %unpack.1), calls=%async_computation.1 | async-start | bytes 2752512 | tf_op jit(solution)/shard_map/all_to_all | solution.py:318
  51.7 12.6 %collective-permute-start.1 = (bf16[128,2176]{1,0:T(8,128)(2,1)S(1)}, bf16[128,2176]{1,0:T(8,128)(2,1)S(1)}, u32[]{:S(2)}, u32[]{:S(2)}) collective-permute-start(bf16[128,2176]{1,0:T(8,128)(2,1)S(1)} %copy-done.3), channel_id=1, source_target_pairs={{0,256},{256,0},{1,257},{257,1},{2,258},{258,2},{3,259},{259,3},{4... | collective-permute-start | bytes 1671176 | tf_op jit(solution)/shard_map/ppermute | solution.py:335
  66.7 10.0 %collective-permute-start.2 = (bf16[4,448,384]{2,1,0:T(8,128)(2,1)S(1)}, bf16[4,448,384]{2,1,0:T(8,128)(2,1)S(1)}, u32[]{:S(2)}, u32[]{:S(2)}) collective-permute-start(bf16[4,448,384]{2,1,0:T(8,128)(2,1)S(1)} %all-to-all-done.1.own_ref), channel_id=1, source_target_pairs={{0,32},{32,0},{1,33},{33,1},{2,34},{34,2},{3,35},{35,3},{4,36},{36... | collective-permute-start | bytes 4128776 | tf_op jit(solution)/shard_map/ppermute | solution.py:335
  74.5 14.3 %collective-permute-start.3 = (bf16[128,1792]{1,0:T(8,128)(2,1)}, bf16[128,1792]{1,0:T(8,128)(2,1)}, u32[]{:S(2)}, u32[]{:S(2)}) collective-permute-start(bf16[128,1792]{1,0:T(8,128)(2,1)} %far.1), channel_id=1, source_target_pairs={{0,256},{256,0},{1,257},{257,1},{2,258},{258,2},{3,259},{259,3},{4... | collective-permute-start | bytes 1376264 | tf_op jit(solution)/shard_map/ppermute | solution.py:335
  80.4 11.2 %all-to-all-start.2 = ((f32[32,1,192]{2,1,0:T(1,128)}), f32[32,1,192]{2,1,0:T(1,128)S(1)}, u32[]{:S(2)}, u32[]{:S(2)}) async-start(f32[32,1,192]{2,1,0:T(1,128)} %get-tuple-element.35), calls=%async_computation.2 | async-start | bytes 65536 | tf_op jit(solution)/shard_map/all_to_all | solution.py:318
  84.2 25.4 %copy-start.2 = (s32[2]{0:T(128)S(1)}, s32[2]{0:T(128)}, u32[]{:S(2)}) copy-start(s32[2]{0:T(128)} %pad_add_fusion.place_ref) | copy-start | bytes 28
  88.0 25.7 %copy-start = (s32[32,8]{0,1:T(8,128)S(1)}, s32[32,8]{0,1:T(8,128)}, u32[]{:S(2)}) copy-start(s32[32,8]{0,1:T(8,128)} %param.6) | copy-start | bytes 3076
  88.0 25.7 %copy-start.1 = (f32[32,8]{0,1:T(8,128)S(1)}, f32[32,8]{0,1:T(8,128)}, u32[]{:S(2)}) copy-start(f32[32,8]{0,1:T(8,128)} %param.7) | copy-start | bytes 3076
  91.6 18.0 %collective-permute-start.4 = (bf16[128,2560]{1,0:T(8,128)(2,1)}, bf16[128,2560]{1,0:T(8,128)(2,1)S(1)}, u32[]{:S(2)}, u32[]{:S(2)}) collective-permute-start(bf16[128,2560]{1,0:T(8,128)(2,1)} %get-tuple-element.38), channel_id=1, source_target_pairs={{0,256},{256,0},{1,257},{257,1},{2,258},{258,2},{3,259},{259,3},{4... | collective-permute-start | bytes 1966088 | tf_op jit(solution)/shard_map/ppermute | solution.py:335
  94.6 19.2 %all-to-all-start.3 = ((f32[16,1,24]{2,1,0:T(1,128)}), f32[16,1,24]{2,1,0:T(1,128)S(1)}, u32[]{:S(2)}, u32[]{:S(2)}) async-start(f32[16,1,24]{2,1,0:T(1,128)} %bitcast.9), calls=%async_computation.3 | async-start | bytes 16384 | tf_op jit(solution)/shard_map/all_to_all | solution.py:318

commit v11 on v10

--- a/solution.py
+++ b/solution.py
@@ -137,40 +137,30 @@
     gate_ref,
     weight,
     done,
-    hidden,
-    ready,
 ):
     blocks, share, slots = own_ref.shape
-    units, wide, mine = mine_ref.shape[0], 2 * share, blocks * share
-    steps = blocks // 2
-    copies = []
-    for step in range(2 * steps):
-        here = pl.ds(step * wide, wide)
-        if step < steps:
-            from_far = far_ref.at[:, here]
-        else:
-            from_far = later_ref.at[:, pl.ds(step * wide - mine, wide)]
-        copies.append(
-            [
-                pltpu.make_async_copy(ref, weight.at[step, k], done.at[step, k])
-                for k, ref in enumerate((keep_ref.at[:, here], from_far))
-            ]
+    units, mine = mine_ref.shape[0], blocks * share
+    copy = pltpu.make_async_copy(far_ref, weight, done)
+    copy.start()
+    values = []
+    for first, second, start in ((keep_ref, keep_ref, mine), (weight, later_ref, 0)):
+        if first is weight:
+            copy.wait()
+        values.append(
+            jnp.dot(
+                first[:, :mine],
+                own_ref[...].reshape(mine, slots),
+                preferred_element_type=F32,
+            )
+            + jnp.dot(
+                second[:, start : start + mine],
+                other_ref[...].reshape(mine, slots),
+                preferred_element_type=F32,
+            )
         )
-    last = activations(keep_ref, later_ref, 2 * mine, mine, hidden, ready)
-    for now in copies + [last]:
-        for copy in now:
-            copy.start()
-    values = jnp.zeros((2 * units, slots), F32)
-    for step, now in enumerate(copies):
-        for copy in now:
-            copy.wait()
-        rows = weight[step].reshape(2 * units, wide)
-        ref, first = (own_ref, step) if step < steps else (other_ref, step - steps)
-        block = ref[2 * first : 2 * first + 2].reshape(wide, slots)
-        values += jnp.dot(rows, block, preferred_element_type=F32)
-    for copy in last:
-        copy.wait()
-    left = hidden[...].reshape(2 * units, slots).astype(F32)
+    values = jnp.concatenate(values, axis=0)
+    left = [keep_ref[:, 2 * mine :], later_ref[:, mine:]]
+    left = jnp.concatenate(left, axis=0).astype(F32)
     terms = jnp.sum(left * values, axis=0, keepdims=True)
     mine_ref[...] = values[:units]
     theirs_ref[...] = values[units:]
@@ -183,14 +173,6 @@
         )
 
 
-def activations(keep_ref, far_ref, keep_start, far_start, hidden, ready):
-    slots = hidden.shape[2]
-    return [
-        pltpu.make_async_copy(ref.at[:, pl.ds(start, slots)], hidden.at[k], ready.at[k])
-        for k, (ref, start) in enumerate(((keep_ref, keep_start), (far_ref, far_start)))
-    ]
-
-
 def down(left, disp_ref, out_ref, first):
     blocks, share, slots = disp_ref.shape
     wide = 2 * share
@@ -208,20 +190,16 @@
 
 
 def rest_kernel(
-    own_ref, other_ref, keep_ref, later_ref, values_ref, mine_ref, send_ref, hidden, done
+    own_ref, other_ref, keep_ref, later_ref, values_ref, mine_ref, send_ref
 ):
     mine, slots = mine_ref.shape[1] // 2, values_ref.shape[1]
-    after = pl.ds(2 * mine, slots)
-    copy = pltpu.make_async_copy(keep_ref.at[:, after], hidden, done)
-    copy.start()
     down(later_ref[:, mine:], other_ref, send_ref, 0)
     values = values_ref[...]
     high = values.astype(BF16)
     send_ref[:, mine : mine + slots] = high
     send_ref[:, mine + slots :] = (values - high.astype(F32)).astype(BF16)
-    copy.wait()
     for half, ref in enumerate((own_ref, other_ref)):
-        down(hidden[...], ref, mine_ref, half * mine)
+        down(keep_ref[:, 2 * mine :], ref, mine_ref, half * mine)
 
 
 def finish_kernel(
@@ -346,7 +324,7 @@
     keep, to_far, to_far_later, order = pl.pallas_call(
         functools.partial(split_kernel, experts),
         out_shape=(
-            bf16((units, 2 * mine + slots)),
+            pltpu.VMEM((units, 2 * mine + slots), BF16),
             bf16((units, mine)),
             bf16((units, mine + slots)),
             bf16((slots, slots)),
@@ -378,13 +356,9 @@
     from_core = other(dispatched, "core")
     dispatched = in_vmem(dispatched)
 
-    keep, from_far, later = in_hbm(keep), in_hbm(from_far), in_vmem(later)
+    keep, from_far, later = in_vmem(keep), in_hbm(from_far), in_vmem(later)
     flops = 2 * slots * units * width
     moved = slots * width + 2 * units * width
-    scratch = [
-        pltpu.VMEM((2, units, slots), BF16),
-        pltpu.SemaphoreType.DMA((2,)),
-    ]
     back_own = pl.pallas_call(
         far_kernel,
         out_shape=bf16((units, mine)),
@@ -404,13 +378,9 @@
             f32((units, slots)),
             jax.ShapeDtypeStruct((far * 4 * rows_y, 1, capacity * near), F32),
         ),
-        in_specs=[whole()] * 2 + [stays()] * 2 + [whole()],
+        in_specs=[whole()] * 3 + [stays(), whole()],
         out_specs=(whole(),) * 3,
-        scratch_shapes=[
-            pltpu.VMEM((rows_y, 2, units, 2 * share), BF16),
-            pltpu.SemaphoreType.DMA((rows_y, 2)),
-        ]
-        + scratch,
+        scratch_shapes=[pltpu.VMEM((units, mine), BF16), pltpu.SemaphoreType.DMA],
         compiler_params=limit(16),
         cost_estimate=cost(flops, moved),
         name="values",
@@ -420,9 +390,8 @@
     down_mine, back_other = pl.pallas_call(
         rest_kernel,
         out_shape=(bf16((units, 2 * mine)), bf16((units, mine + 2 * slots))),
-        in_specs=[whole()] * 2 + [stays()] + [whole()] * 2,
+        in_specs=[whole()] * 5,
         out_specs=(whole(),) * 2,
-        scratch_shapes=[pltpu.VMEM((units, slots), BF16), pltpu.SemaphoreType.DMA],
         compiler_params=limit(16),
         cost_estimate=cost(3 * flops // 4, moved // 2),
         name="rest",

time: 116 us -> 115 us (level)
  Pallas kernels: 20.6 us -> 19.1 us
  local copies, waits for them, and re-layouts: 0.02 us -> 1.23 us
    unnamed x8 -> x14, local copies, waits for them, and re-layouts: 0.02 us -> 1.23 us
  transfers between devices with their start and end apart: 9 -> 9, of which waited for: 8 -> 8; matrix products, arithmetic and copies ran while one was open for 1% -> 1% of each run, Pallas kernels for 14% -> 13%
where the time goes in v11:
time: 115 us; the launch traced here: 114 us
  starting transfers between devices  49.7 us (43%)
  waiting for transfers between devices  42.3 us (37%)
  Pallas kernels  19.1 us (17%)
  local copies, waits for them, and re-layouts  1.23 us (1%)
    all_to_all x4, starting transfers between devices, swap_all(): return lax.all_to_all(x, axis, split_axis=0, concat_axis=0, tiled=True)  34.3 us
    ppermute x5, waiting for transfers between devices, other(): return lax.ppermute(x, axis, [(0, 1), (1, 0)])  32.4 us
    ppermute x5, starting transfers between devices, other(): return lax.ppermute(x, axis, [(0, 1), (1, 0)])  15.5 us
    all_to_all x4, waiting for transfers between devices, swap_all(): return lax.all_to_all(x, axis, split_axis=0, concat_axis=0, tiled=True)  9.84 us
    pallas_call x1, Pallas kernels, on_device(): pl.pallas_call(rest_kernel, out_shape=(bf16((units, 2 * mine)), bf16((uni...  3.41 us
    pallas_call x1, Pallas kernels, on_device(): pl.pallas_call(functools.partial(split_kernel, experts), out_shape=(pltpu...  3.29 us
    pallas_call x1, Pallas kernels, on_device(): pl.pallas_call(finish_kernel, out_shape=(jax.ShapeDtypeStruct((units, wid...  3.13 us
    pallas_call x1, Pallas kernels, on_device(): pl.pallas_call(functools.partial(values_kernel, far, capacity), out_shape...  2.76 us
  transfers between devices with their start and end apart: 9, of which 8 were waited for; matrix products, arithmetic and copies ran while one was open for 1% of the time, Pallas kernels for 13%

profile of v11, /device:TPU:1, one launch (start us, length us, event | category | flops | bytes accessed | tf_op | source)
XLA Modules:
  0.0 113.7 jit_solution(7778762515734070163)
XLA Ops:
  0.6 2.0 %pack.1 = bf16[32,2,2688]{2,1,0:T(2,128)(2,1)} custom-call(bf16[32,448]{1,0:T(8,128)(2,1)} %grad_ref.1, s32[8,32]{1,0:T(8,128)} %bitcast.14, f32[8,32]{1,0:T(8,128)} %bitcast.16), custom_call_target="tpu_custom_call" | custom-call | tf_op jit(solution)/shard_map/pack/pallas_call | solution.py:315
  2.7 18.5 %all-to-all-start = ((bf16[32,2,2688]{2,1,0:T(2,128)(2,1)}), bf16[32,2,2688]{2,1,0:T(2,128)(2,1)S(1)}, u32[]{:S(2)}, u32[]{:S(2)}) async-start(bf16[32,2,2688]{2,1,0:T(2,128)(2,1)} %pack.1), calls=%async_computation | async-start | bytes 688128 | tf_op jit(solution)/shard_map/all_to_all | solution.py:296
  21.8 3.3 %split.1 = (bf16[128,3968]{1,0:T(8,128)(2,1)S(1)}, bf16[128,1792]{1,0:T(8,128)(2,1)}, bf16[128,2176]{1,0:T(8,128)(2,1)}, bf16[384,384]{1,0:T(8,128)(2,1)}) custom-call(s32[2]{0:T(128)} %pad_add_fusion.place_ref, bf16[128,7168]{1,0:T(8,128)(2,1)} %bitcast.18, bf16[384,128]{1,0:T(8,128)(2,1)} %bitcast.19), custom_call_target="tpu_custom_call" | custom-call | flops 37748736 | bytes 3670016 | tf_op jit(solution)/shard_map/split/pallas_call | solution.py:324
  25.1 2.2 %collective-permute-start = (bf16[128,1792]{1,0:T(8,128)(2,1)}, bf16[128,1792]{1,0:T(8,128)(2,1)}, u32[]{:S(2)}, u32[]{:S(2)}) collective-permute-start(bf16[128,1792]{1,0:T(8,128)(2,1)} %get-tuple-element.24), channel_id=1, source_target_pairs={{0,256},{256,0},{1,257},{257,1},{2,258},{258,2},{3,259},{259,3},{4... | collective-permute-start | bytes 1376264 | tf_op jit(solution)/shard_map/ppermute | solution.py:313
  27.3 13.8 %collective-permute-done.far_ref = bf16[128,1792]{1,0:T(8,128)(2,1)} collective-permute-done((bf16[128,1792]{1,0:T(8,128)(2,1)}, bf16[128,1792]{1,0:T(8,128)(2,1)}, u32[]{:S(2)}, u32[]{:S(2)}) %collective-permute-start) | collective-permute-done | bytes 458784 | tf_op jit(solution)/shard_map/ppermute | solution.py:313
  41.1 4.8 %all-to-all-done.in_ref = bf16[32,2,2688]{2,1,0:T(2,128)(2,1)S(1)} async-done(((bf16[32,2,2688]{2,1,0:T(2,128)(2,1)}), bf16[32,2,2688]{2,1,0:T(2,128)(2,1)S(1)}, u32[]{:S(2)}, u32[]{:S(2)}) %all-to-all-start) | async-done | bytes 344096 | tf_op jit(solution)/shard_map/all_to_all | solution.py:296
  45.9 1.6 %unpack.1 = bf16[4,448,384]{2,1,0:T(8,128)(2,1)} custom-call(bf16[32,2,2688]{2,1,0:T(2,128)(2,1)S(1)} %all-to-all-done.in_ref), custom_call_target="tpu_custom_call" | custom-call | tf_op jit(solution)/shard_map/unpack/pallas_call | solution.py:343
  47.5 4.3 %all-to-all-start.1 = ((bf16[4,448,384]{2,1,0:T(8,128)(2,1)}), bf16[4,448,384]{2,1,0:T(8,128)(2,1)S(1)}, u32[]{:S(2)}, u32[]{:S(2)}) async-start(bf16[4,448,384]{2,1,0:T(8,128)(2,1)} %unpack.1), calls=%async_computation.1 | async-start | bytes 2752512 | tf_op jit(solution)/shard_map/all_to_all | solution.py:296
  51.8 2.2 %collective-permute-start.1 = (bf16[128,2176]{1,0:T(8,128)(2,1)S(1)}, bf16[128,2176]{1,0:T(8,128)(2,1)S(1)}, u32[]{:S(2)}, u32[]{:S(2)}) collective-permute-start(bf16[128,2176]{1,0:T(8,128)(2,1)S(1)} %copy-done.6), channel_id=1, source_target_pairs={{0,256},{256,0},{1,257},{257,1},{2,258},{258,2},{3,259},{259,3},{4... | collective-permute-start | bytes 1671176 | tf_op jit(solution)/shard_map/ppermute | solution.py:313
  54.0 10.4 %collective-permute-done.1.later_ref = bf16[128,2176]{1,0:T(8,128)(2,1)S(1)} collective-permute-done((bf16[128,2176]{1,0:T(8,128)(2,1)S(1)}, bf16[128,2176]{1,0:T(8,128)(2,1)S(1)}, u32[]{:S(2)}, u32[]{:S(2)}) %collective-permute-start.1) | collective-permute-done | bytes 557088 | tf_op jit(solution)/shard_map/ppermute | solution.py:313
  64.4 2.3 %all-to-all-done.1.own_ref = bf16[4,448,384]{2,1,0:T(8,128)(2,1)S(1)} async-done(((bf16[4,448,384]{2,1,0:T(8,128)(2,1)}), bf16[4,448,384]{2,1,0:T(8,128)(2,1)S(1)}, u32[]{:S(2)}, u32[]{:S(2)}) %all-to-all-start.1) | async-done | bytes 1376288 | tf_op jit(solution)/shard_map/all_to_all | solution.py:296
  66.7 6.6 %collective-permute-start.2 = (bf16[4,448,384]{2,1,0:T(8,128)(2,1)S(1)}, bf16[4,448,384]{2,1,0:T(8,128)(2,1)S(1)}, u32[]{:S(2)}, u32[]{:S(2)}) collective-permute-start(bf16[4,448,384]{2,1,0:T(8,128)(2,1)S(1)} %all-to-all-done.1.own_ref), channel_id=1, source_target_pairs={{0,32},{32,0},{1,33},{33,1},{2,34},{34,2},{3,35},{35,3},{4,36},{36... | collective-permute-start | bytes 4128776 | tf_op jit(solution)/shard_map/ppermute | solution.py:313
  73.4 1.3 %far.1 = bf16[128,1792]{1,0:T(8,128)(2,1)} custom-call(bf16[4,448,384]{2,1,0:T(8,128)(2,1)S(1)} %all-to-all-done.1.own_ref, bf16[128,2176]{1,0:T(8,128)(2,1)S(1)} %collective-permute-done.1.later_ref), custom_call_target="tpu_custom_call" | custom-call | flops 176160768 | bytes 1146880 | tf_op jit(solution)/shard_map/far/pallas_call | solution.py:362
  74.7 2.2 %collective-permute-start.3 = (bf16[128,1792]{1,0:T(8,128)(2,1)}, bf16[128,1792]{1,0:T(8,128)(2,1)}, u32[]{:S(2)}, u32[]{:S(2)}) collective-permute-start(bf16[128,1792]{1,0:T(8,128)(2,1)} %far.1), channel_id=1, source_target_pairs={{0,256},{256,0},{1,257},{257,1},{2,258},{258,2},{3,259},{259,3},{4... | collective-permute-start | bytes 1376264 | tf_op jit(solution)/shard_map/ppermute | solution.py:313
  76.9 2.8 %values.1 = (f32[128,384]{1,0:T(8,128)}, f32[128,384]{1,0:T(8,128)}, f32[32,1,192]{2,1,0:T(1,128)}) custom-call(bf16[4,448,384]{2,1,0:T(8,128)(2,1)S(1)} %all-to-all-done.1.own_ref, bf16[4,448,384]{2,1,0:T(8,128)(2,1)S(1)} %collective-permute-done.2.other_ref, bf16[128,3968]{1,0:T(8,128)(2,1)S(1)} %copy-done.1, ...), custom_call_target="tpu_custom_call" | custom-call | flops 704643072 | bytes 4587520 | tf_op jit(solution)/shard_map/values/pallas_call | solution.py:374
  79.7 3.8 %all-to-all-start.2 = ((f32[32,1,192]{2,1,0:T(1,128)}), f32[32,1,192]{2,1,0:T(1,128)S(1)}, u32[]{:S(2)}, u32[]{:S(2)}) async-start(f32[32,1,192]{2,1,0:T(1,128)} %get-tuple-element.35), calls=%async_computation.2 | async-start | bytes 65536 | tf_op jit(solution)/shard_map/all_to_all | solution.py:296
  83.5 1.2 %copy-done.2 = bf16[128,3968]{1,0:T(8,128)(2,1)S(1)} copy-done((bf16[128,3968]{1,0:T(8,128)(2,1)S(1)}, bf16[128,3968]{1,0:T(8,128)(2,1)}, u32[]{:S(2)}) %copy-start.2) | copy-done | bytes 1015832
  84.8 3.4 %rest.1 = (bf16[128,3584]{1,0:T(8,128)(2,1)}, bf16[128,2560]{1,0:T(8,128)(2,1)}) custom-call(bf16[4,448,384]{2,1,0:T(8,128)(2,1)S(1)} %all-to-all-done.1.own_ref, bf16[4,448,384]{2,1,0:T(8,128)(2,1)S(1)} %collective-permute-done.2.other_ref, bf16[128,3968]{1,0:T(8,128)(2,1)S(1)} %copy-done.2, bf16[128,2176]{1,0:T(8,128)(2,1)S(1)} %collective-permute-done.1.later_ref, ...), custom_call_target="tpu_custom_call" | custom-call | flops 528482304 | bytes 2293760 | tf_op jit(solution)/shard_map/rest/pallas_call | solution.py:390
  88.2 0.9 collective-permute-done.3.got_own_ref
  89.1 1.9 %all-to-all-done.2.parts_ref = f32[32,1,192]{2,1,0:T(1,128)S(1)} async-done(((f32[32,1,192]{2,1,0:T(1,128)}), f32[32,1,192]{2,1,0:T(1,128)S(1)}, u32[]{:S(2)}, u32[]{:S(2)}) %all-to-all-start.2) | async-done | bytes 24608 | tf_op jit(solution)/shard_map/all_to_all | solution.py:296
  90.9 2.2 %collective-permute-start.4 = (bf16[128,2560]{1,0:T(8,128)(2,1)}, bf16[128,2560]{1,0:T(8,128)(2,1)S(1)}, u32[]{:S(2)}, u32[]{:S(2)}) collective-permute-start(bf16[128,2560]{1,0:T(8,128)(2,1)} %get-tuple-element.38), channel_id=1, source_target_pairs={{0,256},{256,0},{1,257},{257,1},{2,258},{258,2},{3,259},{259,3},{4... | collective-permute-start | bytes 1966088 | tf_op jit(solution)/shard_map/ppermute | solution.py:313
  93.9 7.6 %all-to-all-start.3 = ((f32[16,1,24]{2,1,0:T(1,128)}), f32[16,1,24]{2,1,0:T(1,128)S(1)}, u32[]{:S(2)}, u32[]{:S(2)}) async-start(f32[16,1,24]{2,1,0:T(1,128)} %bitcast.9), calls=%async_computation.3 | async-start | bytes 16384 | tf_op jit(solution)/shard_map/all_to_all | solution.py:296
  101.6 7.3 %collective-permute-done.4.got_other_ref = bf16[128,2560]{1,0:T(8,128)(2,1)S(1)} collective-permute-done((bf16[128,2560]{1,0:T(8,128)(2,1)}, bf16[128,2560]{1,0:T(8,128)(2,1)S(1)}, u32[]{:S(2)}, u32[]{:S(2)}) %collective-permute-start.4) | collective-permute-done | bytes 655392 | tf_op jit(solution)/shard_map/ppermute | solution.py:313
  108.9 3.1 %finish.1 = (bf16[128,7168]{1,0:T(8,128)(2,1)}, bf16[384,128]{1,0:T(8,128)(2,1)}) custom-call(s32[2]{0:T(128)S(1)} %copy-done.5, bf16[128,3584]{1,0:T(8,128)(2,1)} %get-tuple-element.34.own_ref, bf16[128,1792]{1,0:T(8,128)(2,1)} %collective-permute-done.3.got_own_ref, bf16[128,2560]{1,0:T(8,128)(2,1)S(1)} %collective-permute-done.4.got_other_ref, ...), custom_call_target="tpu_custom_call" | custom-call | flops 37748736 | bytes 3670016 | tf_op jit(solution)/shard_map/finish/pallas_call | solution.py:402
  (18 shorter events, 3.0 us)
Async XLA Ops:
  2.7 43.2 %all-to-all-start = ((bf16[32,2,2688]{2,1,0:T(2,128)(2,1)}), bf16[32,2,2688]{2,1,0:T(2,128)(2,1)S(1)}, u32[]{:S(2)}, u32[]{:S(2)}) async-start(bf16[32,2,2688]{2,1,0:T(2,128)(2,1)} %pack.1), calls=%async_computation | async-start | bytes 688128 | tf_op jit(solution)/shard_map/all_to_all | solution.py:296
  25.0 22.4 %copy-start = (bf16[128,3968]{1,0:T(8,128)(2,1)}, bf16[128,3968]{1,0:T(8,128)(2,1)S(1)}, u32[]{:S(2)}) copy-start(bf16[128,3968]{1,0:T(8,128)(2,1)S(1)} %get-tuple-element.31.keep_ref) | copy-start | bytes 3047428
  25.1 16.0 %collective-permute-start = (bf16[128,1792]{1,0:T(8,128)(2,1)}, bf16[128,1792]{1,0:T(8,128)(2,1)}, u32[]{:S(2)}, u32[]{:S(2)}) collective-permute-start(bf16[128,1792]{1,0:T(8,128)(2,1)} %get-tuple-element.24), channel_id=1, source_target_pairs={{0,256},{256,0},{1,257},{257,1},{2,258},{258,2},{3,259},{259,3},{4... | collective-permute-start | bytes 1376264 | tf_op jit(solution)/shard_map/ppermute | solution.py:313
  47.4 4.3 %copy-start.6 = (bf16[128,2176]{1,0:T(8,128)(2,1)S(1)}, bf16[128,2176]{1,0:T(8,128)(2,1)}, u32[]{:S(2)}) copy-start(bf16[128,2176]{1,0:T(8,128)(2,1)} %get-tuple-element.27) | copy-start | bytes 1671172
  47.5 19.3 %all-to-all-start.1 = ((bf16[4,448,384]{2,1,0:T(8,128)(2,1)}), bf16[4,448,384]{2,1,0:T(8,128)(2,1)S(1)}, u32[]{:S(2)}, u32[]{:S(2)}) async-start(bf16[4,448,384]{2,1,0:T(8,128)(2,1)} %unpack.1), calls=%async_computation.1 | async-start | bytes 2752512 | tf_op jit(solution)/shard_map/all_to_all | solution.py:296
  51.8 12.6 %collective-permute-start.1 = (bf16[128,2176]{1,0:T(8,128)(2,1)S(1)}, bf16[128,2176]{1,0:T(8,128)(2,1)S(1)}, u32[]{:S(2)}, u32[]{:S(2)}) collective-permute-start(bf16[128,2176]{1,0:T(8,128)(2,1)S(1)} %copy-done.6), channel_id=1, source_target_pairs={{0,256},{256,0},{1,257},{257,1},{2,258},{258,2},{3,259},{259,3},{4... | collective-permute-start | bytes 1671176 | tf_op jit(solution)/shard_map/ppermute | solution.py:313
  66.7 10.2 %copy-start.1 = (bf16[128,3968]{1,0:T(8,128)(2,1)S(1)}, bf16[128,3968]{1,0:T(8,128)(2,1)}, u32[]{:S(2)}) copy-start(bf16[128,3968]{1,0:T(8,128)(2,1)} %copy-done) | copy-start | bytes 3047428
  66.7 10.2 %collective-permute-start.2 = (bf16[4,448,384]{2,1,0:T(8,128)(2,1)S(1)}, bf16[4,448,384]{2,1,0:T(8,128)(2,1)S(1)}, u32[]{:S(2)}, u32[]{:S(2)}) collective-permute-start(bf16[4,448,384]{2,1,0:T(8,128)(2,1)S(1)} %all-to-all-done.1.own_ref), channel_id=1, source_target_pairs={{0,32},{32,0},{1,33},{33,1},{2,34},{34,2},{3,35},{35,3},{4,36},{36... | collective-permute-start | bytes 4128776 | tf_op jit(solution)/shard_map/ppermute | solution.py:313
  74.7 14.3 %collective-permute-start.3 = (bf16[128,1792]{1,0:T(8,128)(2,1)}, bf16[128,1792]{1,0:T(8,128)(2,1)}, u32[]{:S(2)}, u32[]{:S(2)}) collective-permute-start(bf16[128,1792]{1,0:T(8,128)(2,1)} %far.1), channel_id=1, source_target_pairs={{0,256},{256,0},{1,257},{257,1},{2,258},{258,2},{3,259},{259,3},{4... | collective-permute-start | bytes 1376264 | tf_op jit(solution)/shard_map/ppermute | solution.py:313
  79.7 11.2 %all-to-all-start.2 = ((f32[32,1,192]{2,1,0:T(1,128)}), f32[32,1,192]{2,1,0:T(1,128)S(1)}, u32[]{:S(2)}, u32[]{:S(2)}) async-start(f32[32,1,192]{2,1,0:T(1,128)} %get-tuple-element.35), calls=%async_computation.2 | async-start | bytes 65536 | tf_op jit(solution)/shard_map/all_to_all | solution.py:296
  83.5 1.2 %copy-start.2 = (bf16[128,3968]{1,0:T(8,128)(2,1)S(1)}, bf16[128,3968]{1,0:T(8,128)(2,1)}, u32[]{:S(2)}) copy-start(bf16[128,3968]{1,0:T(8,128)(2,1)} %copy-done) | copy-start | bytes 3047428
  84.7 24.2 %copy-start.5 = (s32[2]{0:T(128)S(1)}, s32[2]{0:T(128)}, u32[]{:S(2)}) copy-start(s32[2]{0:T(128)} %pad_add_fusion.place_ref) | copy-start | bytes 28
  88.2 24.7 %copy-start.3 = (s32[32,8]{0,1:T(8,128)S(1)}, s32[32,8]{0,1:T(8,128)}, u32[]{:S(2)}) copy-start(s32[32,8]{0,1:T(8,128)} %param.6) | copy-start | bytes 3076
  88.2 24.7 %copy-start.4 = (f32[32,8]{0,1:T(8,128)S(1)}, f32[32,8]{0,1:T(8,128)}, u32[]{:S(2)}) copy-start(f32[32,8]{0,1:T(8,128)} %param.7) | copy-start | bytes 3076
  90.9 18.0 %collective-permute-start.4 = (bf16[128,2560]{1,0:T(8,128)(2,1)}, bf16[128,2560]{1,0:T(8,128)(2,1)S(1)}, u32[]{:S(2)}, u32[]{:S(2)}) collective-permute-start(bf16[128,2560]{1,0:T(8,128)(2,1)} %get-tuple-element.38), channel_id=1, source_target_pairs={{0,256},{256,0},{1,257},{257,1},{2,258},{258,2},{3,259},{259,3},{4... | collective-permute-start | bytes 1966088 | tf_op jit(solution)/shard_map/ppermute | solution.py:313
  93.9 19.0 %all-to-all-start.3 = ((f32[16,1,24]{2,1,0:T(1,128)}), f32[16,1,24]{2,1,0:T(1,128)S(1)}, u32[]{:S(2)}, u32[]{:S(2)}) async-start(f32[16,1,24]{2,1,0:T(1,128)} %bitcast.9), calls=%async_computation.3 | async-start | bytes 16384 | tf_op jit(solution)/shard_map/all_to_all | solution.py:296

commit v12 on v11

--- a/solution.py
+++ b/solution.py
@@ -117,9 +117,14 @@
         keep_ref[:, :mine] = part(far, core)
         keep_ref[:, mine:all_mine] = part(far, 1 - core)
         keep_ref[:, all_mine:] = flipped
-        far_ref[...] = part(1 - far, core)
+        far_ref[...] = part(1 - far, core)[:, : far_ref.shape[1]]
         later_ref[:, :mine] = part(1 - far, 1 - core)
-        later_ref[:, mine:] = flipped
+        later_ref[:, mine : mine + slots] = flipped
+        behind = mine + slots
+        later_ref[:, later_ref.shape[1] - LANES :] = jnp.zeros(
+            (later_ref.shape[0], LANES), BF16
+        )
+        later_ref[:, behind : behind + share] = part(1 - far, core)[:, mine - share :]
 
     cases(place_ref, store)
 
@@ -142,24 +147,25 @@
     units, mine = mine_ref.shape[0], blocks * share
     copy = pltpu.make_async_copy(far_ref, weight, done)
     copy.start()
-    values = []
-    for first, second, start in ((keep_ref, keep_ref, mine), (weight, later_ref, 0)):
-        if first is weight:
-            copy.wait()
-        values.append(
-            jnp.dot(
-                first[:, :mine],
-                own_ref[...].reshape(mine, slots),
-                preferred_element_type=F32,
-            )
-            + jnp.dot(
-                second[:, start : start + mine],
-                other_ref[...].reshape(mine, slots),
-                preferred_element_type=F32,
-            )
+
+    def times(rows, ref):
+        return jnp.dot(
+            rows,
+            ref.reshape(ref.shape[0] * share, slots),
+            preferred_element_type=F32,
         )
+
+    values = [
+        times(keep_ref[:, :mine], own_ref[...])
+        + times(keep_ref[:, mine : 2 * mine], other_ref[...])
+    ]
+    behind = times(later_ref[:, :mine], other_ref[...])
+    after = mine + slots
+    behind += times(later_ref[:, after : after + share], own_ref[blocks - 1 :])
+    copy.wait()
+    values.append(times(weight[:, : mine - share], own_ref[: blocks - 1]) + behind)
     values = jnp.concatenate(values, axis=0)
-    left = [keep_ref[:, 2 * mine :], later_ref[:, mine:]]
+    left = [keep_ref[:, 2 * mine :], later_ref[:, mine : mine + slots]]
     left = jnp.concatenate(left, axis=0).astype(F32)
     terms = jnp.sum(left * values, axis=0, keepdims=True)
     mine_ref[...] = values[:units]
@@ -186,14 +192,15 @@
 
 
 def far_kernel(own_ref, later_ref, out_ref):
-    down(later_ref[:, out_ref.shape[1] :], own_ref, out_ref, 0)
+    mine, slots = out_ref.shape[1], own_ref.shape[2]
+    down(later_ref[:, mine : mine + slots], own_ref, out_ref, 0)
 
 
 def rest_kernel(
     own_ref, other_ref, keep_ref, later_ref, values_ref, mine_ref, send_ref
 ):
     mine, slots = mine_ref.shape[1] // 2, values_ref.shape[1]
-    down(later_ref[:, mine:], other_ref, send_ref, 0)
+    down(later_ref[:, mine : mine + slots], other_ref, send_ref, 0)
     values = values_ref[...]
     high = values.astype(BF16)
     send_ref[:, mine : mine + slots] = high
@@ -276,6 +283,10 @@
     return pl.BlockSpec(memory_space=pltpu.HBM)
 
 
+def lanes(width):
+    return -(-width // LANES) * LANES
+
+
 def in_hbm(x):
     return pltpu.with_memory_space_constraint(x, pltpu.HBM)
 
@@ -325,8 +336,8 @@
         functools.partial(split_kernel, experts),
         out_shape=(
             pltpu.VMEM((units, 2 * mine + slots), BF16),
-            bf16((units, mine)),
-            bf16((units, mine + slots)),
+            bf16((units, lanes(mine - share))),
+            bf16((units, mine + slots + lanes(share))),
             bf16((slots, slots)),
         ),
         in_specs=[scalar(), whole(), whole()],
@@ -380,7 +391,10 @@
         ),
         in_specs=[whole()] * 3 + [stays(), whole()],
         out_specs=(whole(),) * 3,
-        scratch_shapes=[pltpu.VMEM((units, mine), BF16), pltpu.SemaphoreType.DMA],
+        scratch_shapes=[
+            pltpu.VMEM((units, lanes(mine - share)), BF16),
+            pltpu.SemaphoreType.DMA,
+        ],
         compiler_params=limit(16),
         cost_estimate=cost(flops, moved),
         name="values",

time: 115 us -> 116 us (level)
  waiting for transfers between devices: 42.3 us -> 43.6 us
    ppermute x5, waiting for transfers between devices: 32.4 us -> 33.6 us  [other(): return lax.ppermute(x, axis, [(0, 1), (1, 0)])]
  transfers between devices with their start and end apart: 9 -> 9, of which waited for: 8 -> 5; matrix products, arithmetic and copies ran while one was open for 1% -> 1% of each run, Pallas kernels for 13% -> 13%
where the time goes in v12:
time: 116 us; the launch traced here: 115 us
  starting transfers between devices  49.6 us (43%)
  waiting for transfers between devices  43.6 us (38%)
  Pallas kernels  19.4 us (17%)
  local copies, waits for them, and re-layouts  1.23 us (1%)
    all_to_all x4, starting transfers between devices, swap_all(): return lax.all_to_all(x, axis, split_axis=0, concat_axis=0, tiled=True)  34.5 us
    ppermute x5, waiting for transfers between devices, other(): return lax.ppermute(x, axis, [(0, 1), (1, 0)])  33.6 us
    ppermute x5, starting transfers between devices, other(): return lax.ppermute(x, axis, [(0, 1), (1, 0)])  15.2 us
    all_to_all x4, waiting for transfers between devices, swap_all(): return lax.all_to_all(x, axis, split_axis=0, concat_axis=0, tiled=True)  9.97 us
    pallas_call x1, Pallas kernels, on_device(): pl.pallas_call(rest_kernel, out_shape=(bf16((units, 2 * mine)), bf16((uni...  3.4 us
    pallas_call x1, Pallas kernels, on_device(): pl.pallas_call(functools.partial(split_kernel, experts), out_shape=(pltpu...  3.35 us
    pallas_call x1, Pallas kernels, on_device(): pl.pallas_call(finish_kernel, out_shape=(jax.ShapeDtypeStruct((units, wid...  3.13 us
    pallas_call x1, Pallas kernels, on_device(): pl.pallas_call(functools.partial(values_kernel, far, capacity), out_shape...  3.02 us
  transfers between devices with their start and end apart: 9, of which 5 were waited for; matrix products, arithmetic and copies ran while one was open for 1% of the time, Pallas kernels for 13%

profile of v12, /device:TPU:1, one launch (start us, length us, event | category | flops | bytes accessed | tf_op | source)
XLA Modules:
  0.0 115.2 jit_solution(375405370504995570)
XLA Ops:
  0.6 2.0 %pack.1 = bf16[32,2,2688]{2,1,0:T(2,128)(2,1)} custom-call(bf16[32,448]{1,0:T(8,128)(2,1)} %grad_ref.1, s32[8,32]{1,0:T(8,128)} %bitcast.14, f32[8,32]{1,0:T(8,128)} %bitcast.16), custom_call_target="tpu_custom_call" | custom-call | tf_op jit(solution)/shard_map/pack/pallas_call | solution.py:326
  2.6 18.5 %all-to-all-start = ((bf16[32,2,2688]{2,1,0:T(2,128)(2,1)}), bf16[32,2,2688]{2,1,0:T(2,128)(2,1)S(1)}, u32[]{:S(2)}, u32[]{:S(2)}) async-start(bf16[32,2,2688]{2,1,0:T(2,128)(2,1)} %pack.1), calls=%async_computation | async-start | bytes 688128 | tf_op jit(solution)/shard_map/all_to_all | solution.py:307
  21.7 3.4 %split.1 = (bf16[128,3968]{1,0:T(8,128)(2,1)S(1)}, bf16[128,1408]{1,0:T(8,128)(2,1)}, bf16[128,2688]{1,0:T(8,128)(2,1)}, bf16[384,384]{1,0:T(8,128)(2,1)}) custom-call(s32[2]{0:T(128)} %pad_add_fusion.place_ref, bf16[128,7168]{1,0:T(8,128)(2,1)} %bitcast.18, bf16[384,128]{1,0:T(8,128)(2,1)} %bitcast.19), custom_call_target="tpu_custom_call" | custom-call | flops 37748736 | bytes 3670016 | tf_op jit(solution)/shard_map/split/pallas_call | solution.py:335
  25.1 2.2 %collective-permute-start = (bf16[128,1408]{1,0:T(8,128)(2,1)}, bf16[128,1408]{1,0:T(8,128)(2,1)}, u32[]{:S(2)}, u32[]{:S(2)}) collective-permute-start(bf16[128,1408]{1,0:T(8,128)(2,1)} %get-tuple-element.24), channel_id=1, source_target_pairs={{0,256},{256,0},{1,257},{257,1},{2,258},{258,2},{3,259},{259,3},{4... | collective-permute-start | bytes 1081352 | tf_op jit(solution)/shard_map/ppermute | solution.py:324
  27.3 11.2 %collective-permute-done.far_ref = bf16[128,1408]{1,0:T(8,128)(2,1)} collective-permute-done((bf16[128,1408]{1,0:T(8,128)(2,1)}, bf16[128,1408]{1,0:T(8,128)(2,1)}, u32[]{:S(2)}, u32[]{:S(2)}) %collective-permute-start) | collective-permute-done | bytes 360480 | tf_op jit(solution)/shard_map/ppermute | solution.py:324
  38.5 7.3 %all-to-all-done.in_ref = bf16[32,2,2688]{2,1,0:T(2,128)(2,1)S(1)} async-done(((bf16[32,2,2688]{2,1,0:T(2,128)(2,1)}), bf16[32,2,2688]{2,1,0:T(2,128)(2,1)S(1)}, u32[]{:S(2)}, u32[]{:S(2)}) %all-to-all-start) | async-done | bytes 344096 | tf_op jit(solution)/shard_map/all_to_all | solution.py:307
  45.8 1.6 %unpack.1 = bf16[4,448,384]{2,1,0:T(8,128)(2,1)} custom-call(bf16[32,2,2688]{2,1,0:T(2,128)(2,1)S(1)} %all-to-all-done.in_ref), custom_call_target="tpu_custom_call" | custom-call | tf_op jit(solution)/shard_map/unpack/pallas_call | solution.py:354
  47.4 4.3 %all-to-all-start.1 = ((bf16[4,448,384]{2,1,0:T(8,128)(2,1)}), bf16[4,448,384]{2,1,0:T(8,128)(2,1)S(1)}, u32[]{:S(2)}, u32[]{:S(2)}) async-start(bf16[4,448,384]{2,1,0:T(8,128)(2,1)} %unpack.1), calls=%async_computation.1 | async-start | bytes 2752512 | tf_op jit(solution)/shard_map/all_to_all | solution.py:307
  51.8 2.2 %collective-permute-start.1 = (bf16[128,2688]{1,0:T(8,128)(2,1)S(1)}, bf16[128,2688]{1,0:T(8,128)(2,1)S(1)}, u32[]{:S(2)}, u32[]{:S(2)}) collective-permute-start(bf16[128,2688]{1,0:T(8,128)(2,1)S(1)} %copy-done.6), channel_id=1, source_target_pairs={{0,256},{256,0},{1,257},{257,1},{2,258},{258,2},{3,259},{259,3},{4... | collective-permute-start | bytes 2064392 | tf_op jit(solution)/shard_map/ppermute | solution.py:324
  54.0 13.2 %collective-permute-done.1.later_ref = bf16[128,2688]{1,0:T(8,128)(2,1)S(1)} collective-permute-done((bf16[128,2688]{1,0:T(8,128)(2,1)S(1)}, bf16[128,2688]{1,0:T(8,128)(2,1)S(1)}, u32[]{:S(2)}, u32[]{:S(2)}) %collective-permute-start.1) | collective-permute-done | bytes 688160 | tf_op jit(solution)/shard_map/ppermute | solution.py:324
  67.2 6.3 %collective-permute-start.2 = (bf16[4,448,384]{2,1,0:T(8,128)(2,1)S(1)}, bf16[4,448,384]{2,1,0:T(8,128)(2,1)S(1)}, u32[]{:S(2)}, u32[]{:S(2)}) collective-permute-start(bf16[4,448,384]{2,1,0:T(8,128)(2,1)S(1)} %all-to-all-done.1.own_ref), channel_id=1, source_target_pairs={{0,32},{32,0},{1,33},{33,1},{2,34},{34,2},{3,35},{35,3},{4,36},{36... | collective-permute-start | bytes 4128776 | tf_op jit(solution)/shard_map/ppermute | solution.py:324
  73.5 1.3 %far.1 = bf16[128,1792]{1,0:T(8,128)(2,1)} custom-call(bf16[4,448,384]{2,1,0:T(8,128)(2,1)S(1)} %all-to-all-done.1.own_ref, bf16[128,2688]{1,0:T(8,128)(2,1)S(1)} %collective-permute-done.1.later_ref), custom_call_target="tpu_custom_call" | custom-call | flops 176160768 | bytes 1146880 | tf_op jit(solution)/shard_map/far/pallas_call | solution.py:373
  74.9 2.2 %collective-permute-start.3 = (bf16[128,1792]{1,0:T(8,128)(2,1)}, bf16[128,1792]{1,0:T(8,128)(2,1)}, u32[]{:S(2)}, u32[]{:S(2)}) collective-permute-start(bf16[128,1792]{1,0:T(8,128)(2,1)} %far.1), channel_id=1, source_target_pairs={{0,256},{256,0},{1,257},{257,1},{2,258},{258,2},{3,259},{259,3},{4... | collective-permute-start | bytes 1376264 | tf_op jit(solution)/shard_map/ppermute | solution.py:324
  77.1 3.0 %values.1 = (f32[128,384]{1,0:T(8,128)}, f32[128,384]{1,0:T(8,128)}, f32[32,1,192]{2,1,0:T(1,128)}) custom-call(bf16[4,448,384]{2,1,0:T(8,128)(2,1)S(1)} %all-to-all-done.1.own_ref, bf16[4,448,384]{2,1,0:T(8,128)(2,1)S(1)} %collective-permute-done.2.other_ref, bf16[128,3968]{1,0:T(8,128)(2,1)S(1)} %copy-done.1, ...), custom_call_target="tpu_custom_call" | custom-call | flops 704643072 | bytes 4587520 | tf_op jit(solution)/shard_map/values/pallas_call | solution.py:385
  80.1 5.8 %all-to-all-start.2 = ((f32[32,1,192]{2,1,0:T(1,128)}), f32[32,1,192]{2,1,0:T(1,128)S(1)}, u32[]{:S(2)}, u32[]{:S(2)}) async-start(f32[32,1,192]{2,1,0:T(1,128)} %get-tuple-element.35), calls=%async_computation.2 | async-start | bytes 65536 | tf_op jit(solution)/shard_map/all_to_all | solution.py:307
  86.0 1.2 %copy-done.2 = bf16[128,3968]{1,0:T(8,128)(2,1)S(1)} copy-done((bf16[128,3968]{1,0:T(8,128)(2,1)S(1)}, bf16[128,3968]{1,0:T(8,128)(2,1)}, u32[]{:S(2)}) %copy-start.2) | copy-done | bytes 1015832
  87.2 3.4 %rest.1 = (bf16[128,3584]{1,0:T(8,128)(2,1)}, bf16[128,2560]{1,0:T(8,128)(2,1)}) custom-call(bf16[4,448,384]{2,1,0:T(8,128)(2,1)S(1)} %all-to-all-done.1.own_ref, bf16[4,448,384]{2,1,0:T(8,128)(2,1)S(1)} %collective-permute-done.2.other_ref, bf16[128,3968]{1,0:T(8,128)(2,1)S(1)} %copy-done.2, bf16[128,2688]{1,0:T(8,128)(2,1)S(1)} %collective-permute-done.1.later_ref, ...), custom_call_target="tpu_custom_call" | custom-call | flops 528482304 | bytes 2293760 | tf_op jit(solution)/shard_map/rest/pallas_call | solution.py:404
  90.6 2.6 %all-to-all-done.2.parts_ref = f32[32,1,192]{2,1,0:T(1,128)S(1)} async-done(((f32[32,1,192]{2,1,0:T(1,128)}), f32[32,1,192]{2,1,0:T(1,128)S(1)}, u32[]{:S(2)}, u32[]{:S(2)}) %all-to-all-start.2) | async-done | bytes 24608 | tf_op jit(solution)/shard_map/all_to_all | solution.py:307
  93.3 2.2 %collective-permute-start.4 = (bf16[128,2560]{1,0:T(8,128)(2,1)}, bf16[128,2560]{1,0:T(8,128)(2,1)S(1)}, u32[]{:S(2)}, u32[]{:S(2)}) collective-permute-start(bf16[128,2560]{1,0:T(8,128)(2,1)} %get-tuple-element.38), channel_id=1, source_target_pairs={{0,256},{256,0},{1,257},{257,1},{2,258},{258,2},{3,259},{259,3},{4... | collective-permute-start | bytes 1966088 | tf_op jit(solution)/shard_map/ppermute | solution.py:324
  95.5 0.8 sum.1
  96.3 5.8 %all-to-all-start.3 = ((f32[16,1,24]{2,1,0:T(1,128)}), f32[16,1,24]{2,1,0:T(1,128)S(1)}, u32[]{:S(2)}, u32[]{:S(2)}) async-start(f32[16,1,24]{2,1,0:T(1,128)} %bitcast.9), calls=%async_computation.3 | async-start | bytes 16384 | tf_op jit(solution)/shard_map/all_to_all | solution.py:307
  102.1 9.2 %collective-permute-done.4.got_other_ref = bf16[128,2560]{1,0:T(8,128)(2,1)S(1)} collective-permute-done((bf16[128,2560]{1,0:T(8,128)(2,1)}, bf16[128,2560]{1,0:T(8,128)(2,1)S(1)}, u32[]{:S(2)}, u32[]{:S(2)}) %collective-permute-start.4) | collective-permute-done | bytes 655392 | tf_op jit(solution)/shard_map/ppermute | solution.py:324
  111.3 3.1 %finish.1 = (bf16[128,7168]{1,0:T(8,128)(2,1)}, bf16[384,128]{1,0:T(8,128)(2,1)}) custom-call(s32[2]{0:T(128)S(1)} %copy-done.5, bf16[128,3584]{1,0:T(8,128)(2,1)} %get-tuple-element.34.own_ref, bf16[128,1792]{1,0:T(8,128)(2,1)} %collective-permute-done.3.got_own_ref, bf16[128,2560]{1,0:T(8,128)(2,1)S(1)} %collective-permute-done.4.got_other_ref, ...), custom_call_target="tpu_custom_call" | custom-call | flops 37748736 | bytes 3670016 | tf_op jit(solution)/shard_map/finish/pallas_call | solution.py:416
  114.4 0.8 match.1
  (18 shorter events, 0.6 us)
Async XLA Ops:
  2.6 43.2 %all-to-all-start = ((bf16[32,2,2688]{2,1,0:T(2,128)(2,1)}), bf16[32,2,2688]{2,1,0:T(2,128)(2,1)S(1)}, u32[]{:S(2)}, u32[]{:S(2)}) async-start(bf16[32,2,2688]{2,1,0:T(2,128)(2,1)} %pack.1), calls=%async_computation | async-start | bytes 688128 | tf_op jit(solution)/shard_map/all_to_all | solution.py:307
  25.1 22.3 %copy-start = (bf16[128,3968]{1,0:T(8,128)(2,1)}, bf16[128,3968]{1,0:T(8,128)(2,1)S(1)}, u32[]{:S(2)}) copy-start(bf16[128,3968]{1,0:T(8,128)(2,1)S(1)} %get-tuple-element.31.keep_ref) | copy-start | bytes 3047428
  25.1 13.4 %collective-permute-start = (bf16[128,1408]{1,0:T(8,128)(2,1)}, bf16[128,1408]{1,0:T(8,128)(2,1)}, u32[]{:S(2)}, u32[]{:S(2)}) collective-permute-start(bf16[128,1408]{1,0:T(8,128)(2,1)} %get-tuple-element.24), channel_id=1, source_target_pairs={{0,256},{256,0},{1,257},{257,1},{2,258},{258,2},{3,259},{259,3},{4... | collective-permute-start | bytes 1081352 | tf_op jit(solution)/shard_map/ppermute | solution.py:324
  47.4 4.3 %copy-start.6 = (bf16[128,2688]{1,0:T(8,128)(2,1)S(1)}, bf16[128,2688]{1,0:T(8,128)(2,1)}, u32[]{:S(2)}) copy-start(bf16[128,2688]{1,0:T(8,128)(2,1)} %get-tuple-element.27) | copy-start | bytes 2064388
  47.4 19.8 %all-to-all-start.1 = ((bf16[4,448,384]{2,1,0:T(8,128)(2,1)}), bf16[4,448,384]{2,1,0:T(8,128)(2,1)S(1)}, u32[]{:S(2)}, u32[]{:S(2)}) async-start(bf16[4,448,384]{2,1,0:T(8,128)(2,1)} %unpack.1), calls=%async_computation.1 | async-start | bytes 2752512 | tf_op jit(solution)/shard_map/all_to_all | solution.py:307
  51.8 15.4 %collective-permute-start.1 = (bf16[128,2688]{1,0:T(8,128)(2,1)S(1)}, bf16[128,2688]{1,0:T(8,128)(2,1)S(1)}, u32[]{:S(2)}, u32[]{:S(2)}) collective-permute-start(bf16[128,2688]{1,0:T(8,128)(2,1)S(1)} %copy-done.6), channel_id=1, source_target_pairs={{0,256},{256,0},{1,257},{257,1},{2,258},{258,2},{3,259},{259,3},{4... | collective-permute-start | bytes 2064392 | tf_op jit(solution)/shard_map/ppermute | solution.py:324
  67.2 9.9 %copy-start.1 = (bf16[128,3968]{1,0:T(8,128)(2,1)S(1)}, bf16[128,3968]{1,0:T(8,128)(2,1)}, u32[]{:S(2)}) copy-start(bf16[128,3968]{1,0:T(8,128)(2,1)} %copy-done) | copy-start | bytes 3047428
  67.2 9.9 %collective-permute-start.2 = (bf16[4,448,384]{2,1,0:T(8,128)(2,1)S(1)}, bf16[4,448,384]{2,1,0:T(8,128)(2,1)S(1)}, u32[]{:S(2)}, u32[]{:S(2)}) collective-permute-start(bf16[4,448,384]{2,1,0:T(8,128)(2,1)S(1)} %all-to-all-done.1.own_ref), channel_id=1, source_target_pairs={{0,32},{32,0},{1,33},{33,1},{2,34},{34,2},{3,35},{35,3},{4,36},{36... | collective-permute-start | bytes 4128776 | tf_op jit(solution)/shard_map/ppermute | solution.py:324
  74.9 15.7 %collective-permute-start.3 = (bf16[128,1792]{1,0:T(8,128)(2,1)}, bf16[128,1792]{1,0:T(8,128)(2,1)}, u32[]{:S(2)}, u32[]{:S(2)}) collective-permute-start(bf16[128,1792]{1,0:T(8,128)(2,1)} %far.1), channel_id=1, source_target_pairs={{0,256},{256,0},{1,257},{257,1},{2,258},{258,2},{3,259},{259,3},{4... | collective-permute-start | bytes 1376264 | tf_op jit(solution)/shard_map/ppermute | solution.py:324
  80.1 13.1 %all-to-all-start.2 = ((f32[32,1,192]{2,1,0:T(1,128)}), f32[32,1,192]{2,1,0:T(1,128)S(1)}, u32[]{:S(2)}, u32[]{:S(2)}) async-start(f32[32,1,192]{2,1,0:T(1,128)} %get-tuple-element.35), calls=%async_computation.2 | async-start | bytes 65536 | tf_op jit(solution)/shard_map/all_to_all | solution.py:307
  86.0 1.2 %copy-start.2 = (bf16[128,3968]{1,0:T(8,128)(2,1)S(1)}, bf16[128,3968]{1,0:T(8,128)(2,1)}, u32[]{:S(2)}) copy-start(bf16[128,3968]{1,0:T(8,128)(2,1)} %copy-done) | copy-start | bytes 3047428
  87.2 24.1 %copy-start.5 = (s32[2]{0:T(128)S(1)}, s32[2]{0:T(128)}, u32[]{:S(2)}) copy-start(s32[2]{0:T(128)} %pad_add_fusion.place_ref) | copy-start | bytes 28
  90.6 23.8 %copy-start.3 = (s32[32,8]{0,1:T(8,128)S(1)}, s32[32,8]{0,1:T(8,128)}, u32[]{:S(2)}) copy-start(s32[32,8]{0,1:T(8,128)} %param.6) | copy-start | bytes 3076
  90.6 23.8 %copy-start.4 = (f32[32,8]{0,1:T(8,128)S(1)}, f32[32,8]{0,1:T(8,128)}, u32[]{:S(2)}) copy-start(f32[32,8]{0,1:T(8,128)} %param.7) | copy-start | bytes 3076
  93.3 18.0 %collective-permute-start.4 = (bf16[128,2560]{1,0:T(8,128)(2,1)}, bf16[128,2560]{1,0:T(8,128)(2,1)S(1)}, u32[]{:S(2)}, u32[]{:S(2)}) collective-permute-start(bf16[128,2560]{1,0:T(8,128)(2,1)} %get-tuple-element.38), channel_id=1, source_target_pairs={{0,256},{256,0},{1,257},{257,1},{2,258},{258,2},{3,259},{259,3},{4... | collective-permute-start | bytes 1966088 | tf_op jit(solution)/shard_map/ppermute | solution.py:324
  96.3 18.1 %all-to-all-start.3 = ((f32[16,1,24]{2,1,0:T(1,128)}), f32[16,1,24]{2,1,0:T(1,128)S(1)}, u32[]{:S(2)}, u32[]{:S(2)}) async-start(f32[16,1,24]{2,1,0:T(1,128)} %bitcast.9), calls=%async_computation.3 | async-start | bytes 16384 | tf_op jit(solution)/shard_map/all_to_all | solution.py:307

commit v13 on v11

--- a/solution.py
+++ b/solution.py
@@ -34,15 +34,20 @@
     for k, here in enumerate(named):
         gate = jnp.where(here, gates[k : k + 1, :], gate)
 
-    def slot(c):
-        placed = jnp.logical_and(present, before == c).astype(F32)
-        row_gate = jnp.sum(placed * gate, axis=1, keepdims=True)
-        return row_gate * jnp.dot(
-            placed.astype(BF16), grad, preferred_element_type=F32
-        )
-
+    capacity = lines * fitting
+    placed = [jnp.logical_and(present, before == c).astype(F32) for c in range(capacity)]
+    placed = jnp.concatenate(placed, axis=0)
+    row_gate = jnp.sum(
+        placed * jnp.concatenate([gate] * capacity, axis=0), axis=1, keepdims=True
+    )
+    scaled = row_gate * jnp.dot(
+        placed.astype(BF16), grad, preferred_element_type=F32
+    )
     for line in range(lines):
-        rows = [slot(fitting * line + i) for i in range(fitting)]
+        rows = [
+            scaled[experts * c : experts * (c + 1)]
+            for c in range(fitting * line, fitting * (line + 1))
+        ]
         out_ref[:, line, :] = jnp.concatenate(rows, axis=1).astype(BF16)
 
 

time: 115 us -> 115 us (level)
  no operation moved by 1% of the time
where the time goes in v13:
time: 115 us; the launch traced here: 114 us
  starting transfers between devices  49.7 us (43%)
  waiting for transfers between devices  42.3 us (37%)
  Pallas kernels  19.1 us (17%)
  local copies, waits for them, and re-layouts  1.23 us (1%)
    all_to_all x4, starting transfers between devices, swap_all(): return lax.all_to_all(x, axis, split_axis=0, concat_axis=0, tiled=True)  34.3 us
    ppermute x5, waiting for transfers between devices, other(): return lax.ppermute(x, axis, [(0, 1), (1, 0)])  32.4 us
    ppermute x5, starting transfers between devices, other(): return lax.ppermute(x, axis, [(0, 1), (1, 0)])  15.5 us
    all_to_all x4, waiting for transfers between devices, swap_all(): return lax.all_to_all(x, axis, split_axis=0, concat_axis=0, tiled=True)  9.84 us
    pallas_call x1, Pallas kernels, on_device(): pl.pallas_call(rest_kernel, out_shape=(bf16((units, 2 * mine)), bf16((uni...  3.4 us
    pallas_call x1, Pallas kernels, on_device(): pl.pallas_call(functools.partial(split_kernel, experts), out_shape=(pltpu...  3.29 us
    pallas_call x1, Pallas kernels, on_device(): pl.pallas_call(finish_kernel, out_shape=(jax.ShapeDtypeStruct((units, wid...  3.13 us
    pallas_call x1, Pallas kernels, on_device(): pl.pallas_call(functools.partial(values_kernel, far, capacity), out_shape...  2.76 us
  transfers between devices with their start and end apart: 9, of which 8 were waited for; matrix products, arithmetic and copies ran while one was open for 1% of the time, Pallas kernels for 13%

profile of v13, /device:TPU:1, one launch (start us, length us, event | category | flops | bytes accessed | tf_op | source)
XLA Modules:
  0.0 113.7 jit_solution(9093823819861234636)
XLA Ops:
  0.6 2.0 %pack.1 = bf16[32,2,2688]{2,1,0:T(2,128)(2,1)} custom-call(bf16[32,448]{1,0:T(8,128)(2,1)} %grad_ref.1, s32[8,32]{1,0:T(8,128)} %bitcast.14, f32[8,32]{1,0:T(8,128)} %bitcast.16), custom_call_target="tpu_custom_call" | custom-call | tf_op jit(solution)/shard_map/pack/pallas_call | solution.py:320
  2.7 18.5 %all-to-all-start = ((bf16[32,2,2688]{2,1,0:T(2,128)(2,1)}), bf16[32,2,2688]{2,1,0:T(2,128)(2,1)S(1)}, u32[]{:S(2)}, u32[]{:S(2)}) async-start(bf16[32,2,2688]{2,1,0:T(2,128)(2,1)} %pack.1), calls=%async_computation | async-start | bytes 688128 | tf_op jit(solution)/shard_map/all_to_all | solution.py:301
  21.8 3.3 %split.1 = (bf16[128,3968]{1,0:T(8,128)(2,1)S(1)}, bf16[128,1792]{1,0:T(8,128)(2,1)}, bf16[128,2176]{1,0:T(8,128)(2,1)}, bf16[384,384]{1,0:T(8,128)(2,1)}) custom-call(s32[2]{0:T(128)} %pad_add_fusion.place_ref, bf16[128,7168]{1,0:T(8,128)(2,1)} %bitcast.18, bf16[384,128]{1,0:T(8,128)(2,1)} %bitcast.19), custom_call_target="tpu_custom_call" | custom-call | flops 37748736 | bytes 3670016 | tf_op jit(solution)/shard_map/split/pallas_call | solution.py:329
  25.1 2.2 %collective-permute-start = (bf16[128,1792]{1,0:T(8,128)(2,1)}, bf16[128,1792]{1,0:T(8,128)(2,1)}, u32[]{:S(2)}, u32[]{:S(2)}) collective-permute-start(bf16[128,1792]{1,0:T(8,128)(2,1)} %get-tuple-element.24), channel_id=1, source_target_pairs={{0,256},{256,0},{1,257},{257,1},{2,258},{258,2},{3,259},{259,3},{4... | collective-permute-start | bytes 1376264 | tf_op jit(solution)/shard_map/ppermute | solution.py:318
  27.3 13.8 %collective-permute-done.far_ref = bf16[128,1792]{1,0:T(8,128)(2,1)} collective-permute-done((bf16[128,1792]{1,0:T(8,128)(2,1)}, bf16[128,1792]{1,0:T(8,128)(2,1)}, u32[]{:S(2)}, u32[]{:S(2)}) %collective-permute-start) | collective-permute-done | bytes 458784 | tf_op jit(solution)/shard_map/ppermute | solution.py:318
  41.0 4.8 %all-to-all-done.in_ref = bf16[32,2,2688]{2,1,0:T(2,128)(2,1)S(1)} async-done(((bf16[32,2,2688]{2,1,0:T(2,128)(2,1)}), bf16[32,2,2688]{2,1,0:T(2,128)(2,1)S(1)}, u32[]{:S(2)}, u32[]{:S(2)}) %all-to-all-start) | async-done | bytes 344096 | tf_op jit(solution)/shard_map/all_to_all | solution.py:301
  45.9 1.6 %unpack.1 = bf16[4,448,384]{2,1,0:T(8,128)(2,1)} custom-call(bf16[32,2,2688]{2,1,0:T(2,128)(2,1)S(1)} %all-to-all-done.in_ref), custom_call_target="tpu_custom_call" | custom-call | tf_op jit(solution)/shard_map/unpack/pallas_call | solution.py:348
  47.5 4.3 %all-to-all-start.1 = ((bf16[4,448,384]{2,1,0:T(8,128)(2,1)}), bf16[4,448,384]{2,1,0:T(8,128)(2,1)S(1)}, u32[]{:S(2)}, u32[]{:S(2)}) async-start(bf16[4,448,384]{2,1,0:T(8,128)(2,1)} %unpack.1), calls=%async_computation.1 | async-start | bytes 2752512 | tf_op jit(solution)/shard_map/all_to_all | solution.py:301
  51.8 2.2 %collective-permute-start.1 = (bf16[128,2176]{1,0:T(8,128)(2,1)S(1)}, bf16[128,2176]{1,0:T(8,128)(2,1)S(1)}, u32[]{:S(2)}, u32[]{:S(2)}) collective-permute-start(bf16[128,2176]{1,0:T(8,128)(2,1)S(1)} %copy-done.6), channel_id=1, source_target_pairs={{0,256},{256,0},{1,257},{257,1},{2,258},{258,2},{3,259},{259,3},{4... | collective-permute-start | bytes 1671176 | tf_op jit(solution)/shard_map/ppermute | solution.py:318
  54.0 10.4 %collective-permute-done.1.later_ref = bf16[128,2176]{1,0:T(8,128)(2,1)S(1)} collective-permute-done((bf16[128,2176]{1,0:T(8,128)(2,1)S(1)}, bf16[128,2176]{1,0:T(8,128)(2,1)S(1)}, u32[]{:S(2)}, u32[]{:S(2)}) %collective-permute-start.1) | collective-permute-done | bytes 557088 | tf_op jit(solution)/shard_map/ppermute | solution.py:318
  64.4 2.3 %all-to-all-done.1.own_ref = bf16[4,448,384]{2,1,0:T(8,128)(2,1)S(1)} async-done(((bf16[4,448,384]{2,1,0:T(8,128)(2,1)}), bf16[4,448,384]{2,1,0:T(8,128)(2,1)S(1)}, u32[]{:S(2)}, u32[]{:S(2)}) %all-to-all-start.1) | async-done | bytes 1376288 | tf_op jit(solution)/shard_map/all_to_all | solution.py:301
  66.7 6.6 %collective-permute-start.2 = (bf16[4,448,384]{2,1,0:T(8,128)(2,1)S(1)}, bf16[4,448,384]{2,1,0:T(8,128)(2,1)S(1)}, u32[]{:S(2)}, u32[]{:S(2)}) collective-permute-start(bf16[4,448,384]{2,1,0:T(8,128)(2,1)S(1)} %all-to-all-done.1.own_ref), channel_id=1, source_target_pairs={{0,32},{32,0},{1,33},{33,1},{2,34},{34,2},{3,35},{35,3},{4,36},{36... | collective-permute-start | bytes 4128776 | tf_op jit(solution)/shard_map/ppermute | solution.py:318
  73.4 1.3 %far.1 = bf16[128,1792]{1,0:T(8,128)(2,1)} custom-call(bf16[4,448,384]{2,1,0:T(8,128)(2,1)S(1)} %all-to-all-done.1.own_ref, bf16[128,2176]{1,0:T(8,128)(2,1)S(1)} %collective-permute-done.1.later_ref), custom_call_target="tpu_custom_call" | custom-call | flops 176160768 | bytes 1146880 | tf_op jit(solution)/shard_map/far/pallas_call | solution.py:367
  74.7 2.2 %collective-permute-start.3 = (bf16[128,1792]{1,0:T(8,128)(2,1)}, bf16[128,1792]{1,0:T(8,128)(2,1)}, u32[]{:S(2)}, u32[]{:S(2)}) collective-permute-start(bf16[128,1792]{1,0:T(8,128)(2,1)} %far.1), channel_id=1, source_target_pairs={{0,256},{256,0},{1,257},{257,1},{2,258},{258,2},{3,259},{259,3},{4... | collective-permute-start | bytes 1376264 | tf_op jit(solution)/shard_map/ppermute | solution.py:318
  76.9 2.8 %values.1 = (f32[128,384]{1,0:T(8,128)}, f32[128,384]{1,0:T(8,128)}, f32[32,1,192]{2,1,0:T(1,128)}) custom-call(bf16[4,448,384]{2,1,0:T(8,128)(2,1)S(1)} %all-to-all-done.1.own_ref, bf16[4,448,384]{2,1,0:T(8,128)(2,1)S(1)} %collective-permute-done.2.other_ref, bf16[128,3968]{1,0:T(8,128)(2,1)S(1)} %copy-done.1, ...), custom_call_target="tpu_custom_call" | custom-call | flops 704643072 | bytes 4587520 | tf_op jit(solution)/shard_map/values/pallas_call | solution.py:379
  79.7 3.8 %all-to-all-start.2 = ((f32[32,1,192]{2,1,0:T(1,128)}), f32[32,1,192]{2,1,0:T(1,128)S(1)}, u32[]{:S(2)}, u32[]{:S(2)}) async-start(f32[32,1,192]{2,1,0:T(1,128)} %get-tuple-element.35), calls=%async_computation.2 | async-start | bytes 65536 | tf_op jit(solution)/shard_map/all_to_all | solution.py:301
  83.5 1.2 %copy-done.2 = bf16[128,3968]{1,0:T(8,128)(2,1)S(1)} copy-done((bf16[128,3968]{1,0:T(8,128)(2,1)S(1)}, bf16[128,3968]{1,0:T(8,128)(2,1)}, u32[]{:S(2)}) %copy-start.2) | copy-done | bytes 1015832
  84.8 3.4 %rest.1 = (bf16[128,3584]{1,0:T(8,128)(2,1)}, bf16[128,2560]{1,0:T(8,128)(2,1)}) custom-call(bf16[4,448,384]{2,1,0:T(8,128)(2,1)S(1)} %all-to-all-done.1.own_ref, bf16[4,448,384]{2,1,0:T(8,128)(2,1)S(1)} %collective-permute-done.2.other_ref, bf16[128,3968]{1,0:T(8,128)(2,1)S(1)} %copy-done.2, bf16[128,2176]{1,0:T(8,128)(2,1)S(1)} %collective-permute-done.1.later_ref, ...), custom_call_target="tpu_custom_call" | custom-call | flops 528482304 | bytes 2293760 | tf_op jit(solution)/shard_map/rest/pallas_call | solution.py:395
  88.2 0.9 collective-permute-done.3.got_own_ref
  89.1 1.9 %all-to-all-done.2.parts_ref = f32[32,1,192]{2,1,0:T(1,128)S(1)} async-done(((f32[32,1,192]{2,1,0:T(1,128)}), f32[32,1,192]{2,1,0:T(1,128)S(1)}, u32[]{:S(2)}, u32[]{:S(2)}) %all-to-all-start.2) | async-done | bytes 24608 | tf_op jit(solution)/shard_map/all_to_all | solution.py:301
  90.9 2.2 %collective-permute-start.4 = (bf16[128,2560]{1,0:T(8,128)(2,1)}, bf16[128,2560]{1,0:T(8,128)(2,1)S(1)}, u32[]{:S(2)}, u32[]{:S(2)}) collective-permute-start(bf16[128,2560]{1,0:T(8,128)(2,1)} %get-tuple-element.38), channel_id=1, source_target_pairs={{0,256},{256,0},{1,257},{257,1},{2,258},{258,2},{3,259},{259,3},{4... | collective-permute-start | bytes 1966088 | tf_op jit(solution)/shard_map/ppermute | solution.py:318
  93.9 7.6 %all-to-all-start.3 = ((f32[16,1,24]{2,1,0:T(1,128)}), f32[16,1,24]{2,1,0:T(1,128)S(1)}, u32[]{:S(2)}, u32[]{:S(2)}) async-start(f32[16,1,24]{2,1,0:T(1,128)} %bitcast.9), calls=%async_computation.3 | async-start | bytes 16384 | tf_op jit(solution)/shard_map/all_to_all | solution.py:301
  101.6 7.3 %collective-permute-done.4.got_other_ref = bf16[128,2560]{1,0:T(8,128)(2,1)S(1)} collective-permute-done((bf16[128,2560]{1,0:T(8,128)(2,1)}, bf16[128,2560]{1,0:T(8,128)(2,1)S(1)}, u32[]{:S(2)}, u32[]{:S(2)}) %collective-permute-start.4) | collective-permute-done | bytes 655392 | tf_op jit(solution)/shard_map/ppermute | solution.py:318
  108.9 3.1 %finish.1 = (bf16[128,7168]{1,0:T(8,128)(2,1)}, bf16[384,128]{1,0:T(8,128)(2,1)}) custom-call(s32[2]{0:T(128)S(1)} %copy-done.5, bf16[128,3584]{1,0:T(8,128)(2,1)} %get-tuple-element.34.own_ref, bf16[128,1792]{1,0:T(8,128)(2,1)} %collective-permute-done.3.got_own_ref, bf16[128,2560]{1,0:T(8,128)(2,1)S(1)} %collective-permute-done.4.got_other_ref, ...), custom_call_target="tpu_custom_call" | custom-call | flops 37748736 | bytes 3670016 | tf_op jit(solution)/shard_map/finish/pallas_call | solution.py:407
  (18 shorter events, 3.0 us)
Async XLA Ops:
  2.7 43.2 %all-to-all-start = ((bf16[32,2,2688]{2,1,0:T(2,128)(2,1)}), bf16[32,2,2688]{2,1,0:T(2,128)(2,1)S(1)}, u32[]{:S(2)}, u32[]{:S(2)}) async-start(bf16[32,2,2688]{2,1,0:T(2,128)(2,1)} %pack.1), calls=%async_computation | async-start | bytes 688128 | tf_op jit(solution)/shard_map/all_to_all | solution.py:301
  25.0 22.4 %copy-start = (bf16[128,3968]{1,0:T(8,128)(2,1)}, bf16[128,3968]{1,0:T(8,128)(2,1)S(1)}, u32[]{:S(2)}) copy-start(bf16[128,3968]{1,0:T(8,128)(2,1)S(1)} %get-tuple-element.31.keep_ref) | copy-start | bytes 3047428
  25.1 16.0 %collective-permute-start = (bf16[128,1792]{1,0:T(8,128)(2,1)}, bf16[128,1792]{1,0:T(8,128)(2,1)}, u32[]{:S(2)}, u32[]{:S(2)}) collective-permute-start(bf16[128,1792]{1,0:T(8,128)(2,1)} %get-tuple-element.24), channel_id=1, source_target_pairs={{0,256},{256,0},{1,257},{257,1},{2,258},{258,2},{3,259},{259,3},{4... | collective-permute-start | bytes 1376264 | tf_op jit(solution)/shard_map/ppermute | solution.py:318
  47.4 4.3 %copy-start.6 = (bf16[128,2176]{1,0:T(8,128)(2,1)S(1)}, bf16[128,2176]{1,0:T(8,128)(2,1)}, u32[]{:S(2)}) copy-start(bf16[128,2176]{1,0:T(8,128)(2,1)} %get-tuple-element.27) | copy-start | bytes 1671172
  47.5 19.3 %all-to-all-start.1 = ((bf16[4,448,384]{2,1,0:T(8,128)(2,1)}), bf16[4,448,384]{2,1,0:T(8,128)(2,1)S(1)}, u32[]{:S(2)}, u32[]{:S(2)}) async-start(bf16[4,448,384]{2,1,0:T(8,128)(2,1)} %unpack.1), calls=%async_computation.1 | async-start | bytes 2752512 | tf_op jit(solution)/shard_map/all_to_all | solution.py:301
  51.8 12.6 %collective-permute-start.1 = (bf16[128,2176]{1,0:T(8,128)(2,1)S(1)}, bf16[128,2176]{1,0:T(8,128)(2,1)S(1)}, u32[]{:S(2)}, u32[]{:S(2)}) collective-permute-start(bf16[128,2176]{1,0:T(8,128)(2,1)S(1)} %copy-done.6), channel_id=1, source_target_pairs={{0,256},{256,0},{1,257},{257,1},{2,258},{258,2},{3,259},{259,3},{4... | collective-permute-start | bytes 1671176 | tf_op jit(solution)/shard_map/ppermute | solution.py:318
  66.7 10.2 %copy-start.1 = (bf16[128,3968]{1,0:T(8,128)(2,1)S(1)}, bf16[128,3968]{1,0:T(8,128)(2,1)}, u32[]{:S(2)}) copy-start(bf16[128,3968]{1,0:T(8,128)(2,1)} %copy-done) | copy-start | bytes 3047428
  66.7 10.2 %collective-permute-start.2 = (bf16[4,448,384]{2,1,0:T(8,128)(2,1)S(1)}, bf16[4,448,384]{2,1,0:T(8,128)(2,1)S(1)}, u32[]{:S(2)}, u32[]{:S(2)}) collective-permute-start(bf16[4,448,384]{2,1,0:T(8,128)(2,1)S(1)} %all-to-all-done.1.own_ref), channel_id=1, source_target_pairs={{0,32},{32,0},{1,33},{33,1},{2,34},{34,2},{3,35},{35,3},{4,36},{36... | collective-permute-start | bytes 4128776 | tf_op jit(solution)/shard_map/ppermute | solution.py:318
  74.7 14.3 %collective-permute-start.3 = (bf16[128,1792]{1,0:T(8,128)(2,1)}, bf16[128,1792]{1,0:T(8,128)(2,1)}, u32[]{:S(2)}, u32[]{:S(2)}) collective-permute-start(bf16[128,1792]{1,0:T(8,128)(2,1)} %far.1), channel_id=1, source_target_pairs={{0,256},{256,0},{1,257},{257,1},{2,258},{258,2},{3,259},{259,3},{4... | collective-permute-start | bytes 1376264 | tf_op jit(solution)/shard_map/ppermute | solution.py:318
  79.7 11.2 %all-to-all-start.2 = ((f32[32,1,192]{2,1,0:T(1,128)}), f32[32,1,192]{2,1,0:T(1,128)S(1)}, u32[]{:S(2)}, u32[]{:S(2)}) async-start(f32[32,1,192]{2,1,0:T(1,128)} %get-tuple-element.35), calls=%async_computation.2 | async-start | bytes 65536 | tf_op jit(solution)/shard_map/all_to_all | solution.py:301
  83.5 1.2 %copy-start.2 = (bf16[128,3968]{1,0:T(8,128)(2,1)S(1)}, bf16[128,3968]{1,0:T(8,128)(2,1)}, u32[]{:S(2)}) copy-start(bf16[128,3968]{1,0:T(8,128)(2,1)} %copy-done) | copy-start | bytes 3047428
  84.7 24.2 %copy-start.5 = (s32[2]{0:T(128)S(1)}, s32[2]{0:T(128)}, u32[]{:S(2)}) copy-start(s32[2]{0:T(128)} %pad_add_fusion.place_ref) | copy-start | bytes 28
  88.2 24.7 %copy-start.3 = (s32[32,8]{0,1:T(8,128)S(1)}, s32[32,8]{0,1:T(8,128)}, u32[]{:S(2)}) copy-start(s32[32,8]{0,1:T(8,128)} %param.6) | copy-start | bytes 3076
  88.2 24.7 %copy-start.4 = (f32[32,8]{0,1:T(8,128)S(1)}, f32[32,8]{0,1:T(8,128)}, u32[]{:S(2)}) copy-start(f32[32,8]{0,1:T(8,128)} %param.7) | copy-start | bytes 3076
  90.9 18.0 %collective-permute-start.4 = (bf16[128,2560]{1,0:T(8,128)(2,1)}, bf16[128,2560]{1,0:T(8,128)(2,1)S(1)}, u32[]{:S(2)}, u32[]{:S(2)}) collective-permute-start(bf16[128,2560]{1,0:T(8,128)(2,1)} %get-tuple-element.38), channel_id=1, source_target_pairs={{0,256},{256,0},{1,257},{257,1},{2,258},{258,2},{3,259},{259,3},{4... | collective-permute-start | bytes 1966088 | tf_op jit(solution)/shard_map/ppermute | solution.py:318
  93.9 19.0 %all-to-all-start.3 = ((f32[16,1,24]{2,1,0:T(1,128)}), f32[16,1,24]{2,1,0:T(1,128)S(1)}, u32[]{:S(2)}, u32[]{:S(2)}) async-start(f32[16,1,24]{2,1,0:T(1,128)} %bitcast.9), calls=%async_computation.3 | async-start | bytes 16384 | tf_op jit(solution)/shard_map/all_to_all | solution.py:301
